TPU v7x, 128 devices: a whole 4x4x4 slice. The times are simulated.
128 devices in a mesh: brow: 8 (over z, core), bcol: 16 (over x, y).
Axes of the slice: x: 4, y: 4, z: 4, core: 2. Of those that a mesh axis runs over, the one named last changes fastest.
Arguments:
- blocks: bfloat16 [8, 16, 40, 256, 256], P('brow', 'bcol'), may hold values from -6 to 6
- pattern_rows: int32 [8, 16, 40], P('brow', 'bcol'), may hold values from 0 to 47
- pattern_cols: int32 [8, 16, 40], P('brow', 'bcol'), may hold values from 0 to 23
- live_count: int32 [8, 16], P('brow', 'bcol'), may hold values from 10 to 40, as said below
- degree_scale: float32 [98304], P(('brow', 'bcol')), may hold values from 0.03125 to 0.125
- eigen_block: float32 [32, 98304], P(None, ('brow', 'bcol')), may hold values from -6 to 6
- direction: float32 [32, 98304], P(None, ('brow', 'bcol')), may hold values from -6 to 6
- cutoff: float32 [1], replicated, may hold values from 0.9 to 1
Outputs:
- eigen_next: float32 [32, 98304], P(None, ('brow', 'bcol'))
- direction_next: float32 [32, 98304], P(None, ('brow', 'bcol'))
- residual: float32 [32, 98304], P(None, ('brow', 'bcol'))
- direction_image: float32 [32, 98304], P(None, ('brow', 'bcol'))
Inputs may be any that keep to these rules, and one draw needn't show every extreme that they name: `live_count`: some owner uses all 40 slots in every draw.
All inputs are finite; a program needn't handle non-finite values.
Results may differ from a plain program's by a relative error of at most 0.033.
Values may be sent and summed in bfloat16 or wider, within the bound.
No kernel may reach another device: no remote copies, remote signals or barrier semaphores. Data moves between devices by JAX's collectives and lax.ppermute only.
A program may use at most 64 MiB of HBM per device.

v0:
```python
import jax
import jax.numpy as jnp
from jax import lax
from jax.sharding import PartitionSpec as P

ITERS = 2
NS_STEPS = 8


def highest_dot(left, right):
    return jnp.dot(left, right, precision=lax.Precision.HIGHEST)


def solve_quotient(gram_x, rayleigh_x):
    lower = jnp.linalg.cholesky(gram_x)
    middle = lax.linalg.triangular_solve(lower, rayleigh_x, left_side=True, lower=True)
    return lax.linalg.triangular_solve(lower, middle, left_side=True, lower=True, transpose_a=True)


def ritz_coefficients(gram_b, gram_a, cutoff, wanted):
    lower = jnp.linalg.cholesky(gram_b)
    first = lax.linalg.triangular_solve(lower, gram_a, left_side=True, lower=True)
    small = lax.linalg.triangular_solve(lower, first.T, left_side=True, lower=True)
    identity = jnp.eye(small.shape[0], dtype=jnp.float32)
    shifted = cutoff[0] * identity - small
    sign_now = shifted / jnp.sqrt(jnp.sum(shifted * shifted) + 1e-06)
    for sweep_index in range(NS_STEPS):
        sign_now = 1.5 * sign_now - 0.5 * highest_dot(sign_now, highest_dot(sign_now, sign_now))
    projector = 0.5 * (identity + sign_now)
    inner = highest_dot(projector, lower.T[:, :wanted])
    return lax.linalg.triangular_solve(lower, inner, left_side=True, lower=True, transpose_a=True)


def local_partial(block_set, row_index, col_index, live_slots, gathered, out_rows):
    columns = gathered.shape[0]
    block_side = block_set.shape[-1]
    panel = gathered.reshape(columns, -1, block_side)
    empty = jnp.zeros((columns, out_rows, block_side), jnp.float32)
    picked = jnp.take(panel, col_index, axis=1)
    products = jnp.einsum("sab,csb->csa", block_set, picked, preferred_element_type=jnp.float32)
    kept_mask = (jnp.arange(block_set.shape[0]) < live_slots).astype(jnp.float32)
    total = empty.at[:, row_index].add(products * kept_mask[None, :, None])
    return total.reshape(columns, out_rows * block_side)


def local(
    blocks, pattern_rows, pattern_cols, live_count, degree_scale, eigen_block, direction, cutoff
):
    block_set = blocks[0, 0]
    row_index = pattern_rows[0, 0]
    col_index = pattern_cols[0, 0]
    live_slots = live_count[0, 0]
    block_side = block_set.shape[-1]
    out_rows = lax.axis_size("bcol") * (degree_scale.shape[0] // block_side)
    wanted = eigen_block.shape[0]

    def fetch(scaled):
        return lax.all_gather(scaled, "brow", axis=1, tiled=True)

    def apply_graph(gathered):
        partial_value = local_partial(
            block_set, row_index, col_index, live_slots, gathered, out_rows
        )
        return lax.psum_scatter(
            partial_value.astype(jnp.bfloat16), "bcol", scatter_dimension=1, tiled=True
        ).astype(jnp.float32)

    vectors, searches = (eigen_block, direction)
    stacked = None
    for section_index in range(ITERS + 1):
        stacked = fetch(
            (degree_scale * jnp.concatenate([vectors, searches], 0)).astype(jnp.bfloat16)
        )
        image = apply_graph(stacked)
        image_x = vectors - degree_scale * image[:wanted]
        image_p = searches - degree_scale * image[wanted:]
        gram_x, rayleigh_x = lax.psum(
            (highest_dot(vectors, vectors.T), highest_dot(vectors, image_x.T)), ("brow", "bcol")
        )
        quotient = solve_quotient(gram_x, rayleigh_x)
        remainder = image_x - highest_dot(quotient.T, vectors)
        if section_index < ITERS:
            residual_gathered = fetch((degree_scale * remainder).astype(jnp.bfloat16))
            image_r = remainder - degree_scale * apply_graph(residual_gathered)
            basis = jnp.concatenate([vectors, remainder, searches], 0)
            basis_image = jnp.concatenate([image_x, image_r, image_p], 0)
            gram_b, cross = lax.psum(
                (highest_dot(basis, basis.T), highest_dot(basis, basis_image.T)), ("brow", "bcol")
            )
            gram_a = 0.5 * (cross + cross.T)
            coeffs = ritz_coefficients(gram_b, gram_a, cutoff, wanted)
            row_mask = (jnp.arange(coeffs.shape[0]) >= wanted).astype(jnp.float32)
            dir_coeffs = coeffs * row_mask[:, None]
            vectors = highest_dot(coeffs.T, basis)
            searches = highest_dot(dir_coeffs.T, basis)
            stacked = None
    return (vectors, searches, remainder, image_p)


def solution(mesh):
    placed = (
        P("brow", "bcol", None, None, None),
        P("brow", "bcol", None),
        P("brow", "bcol", None),
        P("brow", "bcol"),
        P(("brow", "bcol")),
        P(None, ("brow", "bcol")),
        P(None, ("brow", "bcol")),
        P(),
    )
    return jax.shard_map(
        local,
        mesh=mesh,
        in_specs=placed,
        out_specs=(
            P(None, ("brow", "bcol")),
            P(None, ("brow", "bcol")),
            P(None, ("brow", "bcol")),
            P(None, ("brow", "bcol")),
        ),
        check_vma=False,
    )
```

profile of v0, /device:TPU:1, one launch (start us, length us, event | category | flops | bytes accessed | tf_op | source)
XLA Modules:
  0.0 1067.6 jit_solution(16130553832608869253)
XLA Ops:
  10.2 15.9 %all_gather.15 = bf16[64,6144]{1,0:T(8,128)(2,1)S(1)} all-gather(bf16[64,768]{1,0:T(8,128)(2,1)S(1)} %fusion.77), channel_id=1, replica_groups=mesh['brow'=8,'bcol'=16] {'brow'}, dimensions={1}, use_global_device_ids=true | all-gather | bytes 884736 | tf_op jit(solution)/shard_map/all_gather | solution.py:58
  32.9 6.6 scatter_fusion
  42.1 71.7 %reduce-scatter.6.cloned.1.call-done = bf16[64,768]{1,0:T(8,128)(2,1)} async-done(((bf16[64,12288]{1,0:T(8,128)(2,1)}), bf16[64,768]{1,0:T(8,128)(2,1)}) %reduce-scatter.6.cloned.1.call-update) | async-done | bytes 98320 | tf_op jit(solution)/shard_map/reduce_scatter | solution.py:64
  115.0 66.2 %all-reduce.4 = (f32[32,32]{0,1:T(8,128)S(1)}, f32[32,32]{0,1:T(8,128)S(1)}) all-reduce(f32[32,32]{0,1:T(8,128)S(1)} %convolution_bitcast_fusion.2, f32[32,32]{0,1:T(8,128)S(1)} %fusion.163), channel_id=1, replica_groups=mesh['brow'=8,'bcol'=16] {'brow','bcol'}, use_global_device_ids=true, to_apply=%region_5.8 | all-reduce | flops 2048 | bytes 16384 | tf_op jit(solution)/shard_map/psum | solution.py:77
  188.7 13.7 %all_gather.16 = bf16[32,6144]{1,0:T(8,128)(2,1)S(1)} all-gather(bf16[32,768]{1,0:T(8,128)(2,1)S(1)} %get-tuple-element.30), channel_id=1, replica_groups=mesh['brow'=8,'bcol'=16] {'brow'}, dimensions={1}, use_global_device_ids=true | all-gather | bytes 442368 | tf_op jit(solution)/shard_map/all_gather | solution.py:58
  212.4 66.0 %reduce-scatter.8.cloned.1.call-done = bf16[32,768]{1,0:T(8,128)(2,1)} async-done(((bf16[32,12288]{1,0:T(8,128)(2,1)}), bf16[32,768]{1,0:T(8,128)(2,1)}) %reduce-scatter.8.cloned.1.call-update) | async-done | bytes 49168 | tf_op jit(solution)/shard_map/reduce_scatter | solution.py:64
  281.5 142.3 %all-reduce.10.cloned.1.call-done = (f32[96,96]{1,0:T(8,128)}, f32[96,96]{0,1:T(8,128)}) async-done(((f32[96,96]{1,0:T(8,128)}, f32[96,96]{0,1:T(8,128)}), (f32[96,96]{1,0:T(8,128)}, f32[96,96]{0,1:T(8,128)})) %all-reduce.10.cloned.1.call-update) | async-done | bytes 73744 | tf_op jit(solution)/shard_map/psum | solution.py:87
  425.5 8.8 cholesky.112
  435.6 7.4 custom-call.28
  450.6 14.1 %all_gather.17 = bf16[64,6144]{1,0:T(8,128)(2,1)S(1)} all-gather(bf16[64,768]{1,0:T(8,128)(2,1)S(1)} %fusion.78), channel_id=1, replica_groups=mesh['brow'=8,'bcol'=16] {'brow'}, dimensions={1}, use_global_device_ids=true | all-gather | bytes 884736 | tf_op jit(solution)/shard_map/all_gather | solution.py:58
  465.5 5.7 fusion.13
  471.6 6.6 scatter_fusion.2
  479.9 68.6 %reduce-scatter.10.cloned.1.call-done = bf16[64,768]{1,0:T(8,128)(2,1)} async-done(((bf16[64,12288]{1,0:T(8,128)(2,1)}), bf16[64,768]{1,0:T(8,128)(2,1)}) %reduce-scatter.10.cloned.1.call-update) | async-done | bytes 98320 | tf_op jit(solution)/shard_map/reduce_scatter | solution.py:64
  549.7 66.2 %all-reduce.2 = (f32[32,32]{1,0:T(8,128)S(1)}, f32[32,32]{0,1:T(8,128)S(1)}) all-reduce(f32[32,32]{1,0:T(8,128)S(1)} %fusion.172, f32[32,32]{0,1:T(8,128)S(1)} %fusion.171), channel_id=1, replica_groups=mesh['brow'=8,'bcol'=16] {'brow','bcol'}, use_global_device_ids=true, to_apply=%region_16.25 | all-reduce | flops 2048 | bytes 16384 | tf_op jit(solution)/shard_map/psum | solution.py:77
  623.4 13.9 %all_gather.18 = bf16[32,6144]{1,0:T(8,128)(2,1)S(1)} all-gather(bf16[32,768]{1,0:T(8,128)(2,1)S(1)} %get-tuple-element.34), channel_id=1, replica_groups=mesh['brow'=8,'bcol'=16] {'brow'}, dimensions={1}, use_global_device_ids=true | all-gather | bytes 442368 | tf_op jit(solution)/shard_map/all_gather | solution.py:58
  647.4 66.1 %reduce-scatter.12.cloned.1.call-done = bf16[32,768]{1,0:T(8,128)(2,1)} async-done(((bf16[32,12288]{1,0:T(8,128)(2,1)}), bf16[32,768]{1,0:T(8,128)(2,1)}) %reduce-scatter.12.cloned.1.call-update) | async-done | bytes 49168 | tf_op jit(solution)/shard_map/reduce_scatter | solution.py:64
  715.4 144.0 %all-reduce.8.cloned.1.call-done = (f32[96,96]{0,1:T(8,128)}, f32[96,96]{0,1:T(8,128)}) async-done(((f32[96,96]{0,1:T(8,128)}, f32[96,96]{0,1:T(8,128)}), (f32[96,96]{0,1:T(8,128)}, f32[96,96]{0,1:T(8,128)})) %all-reduce.8.cloned.1.call-update) | async-done | bytes 73744 | tf_op jit(solution)/shard_map/psum | solution.py:87
  861.1 8.8 cholesky.134
  871.2 7.4 custom-call.33
  886.2 14.3 %all_gather.19 = bf16[64,6144]{1,0:T(8,128)(2,1)S(1)} all-gather(bf16[64,768]{1,0:T(8,128)(2,1)S(1)} %fusion.79), channel_id=1, replica_groups=mesh['brow'=8,'bcol'=16] {'brow'}, dimensions={1}, use_global_device_ids=true | all-gather | bytes 884736 | tf_op jit(solution)/shard_map/all_gather | solution.py:58
  901.4 5.7 fusion.16
  907.5 6.6 scatter_fusion.4
  915.8 68.6 %reduce-scatter.14.cloned.1.call-done = bf16[64,768]{1,0:T(8,128)(2,1)} async-done(((bf16[64,12288]{1,0:T(8,128)(2,1)}), bf16[64,768]{1,0:T(8,128)(2,1)}) %reduce-scatter.14.cloned.1.call-update) | async-done | bytes 98320 | tf_op jit(solution)/shard_map/reduce_scatter | solution.py:64
  986.2 66.2 %all-reduce = (f32[32,32]{1,0:T(8,128)S(1)}, f32[32,32]{0,1:T(8,128)S(1)}) all-reduce(f32[32,32]{1,0:T(8,128)S(1)} %fusion.82, f32[32,32]{0,1:T(8,128)S(1)} %fusion.180), channel_id=1, replica_groups=mesh['brow'=8,'bcol'=16] {'brow','bcol'}, use_global_device_ids=true, to_apply=%region_25.34 | all-reduce | flops 2048 | bytes 16384 | tf_op jit(solution)/shard_map/psum | solution.py:77
  (174 shorter events, 88.5 us)
Async XLA Ops:
  7.2 19.0 %copy-start.8 = (s32[1,1,40]{2,1,0:T(1,128)S(1)}, s32[1,1,40]{2,1,0:T(1,128)}, u32[]{:S(2)}) copy-start(s32[1,1,40]{2,1,0:T(1,128)} %param.23) | copy-start | bytes 484
  7.2 106.6 %reduce-scatter.6.cloned.1.call-start = ((), (), s32[]{:S(2)}) async-start(), calls=%async_computation.5 | async-start | bytes 1671168 | tf_op jit(solution)/shard_map/reduce_scatter | solution.py:64
  9.2 193.3 %copy-start.5 = (s32[1024]{0:T(1024)}, s32[1024]{0:T(1024)S(1)}, u32[]{:S(2)}) copy-start(s32[1024]{0:T(1024)S(1)} %pad_clamp_fusion) | copy-start | bytes 12292
  41.0 0.9 copy-start
  41.0 73.7 %copy-start.2 = (f32[32,768]{1,0:T(8,128)S(1)}, f32[32,768]{1,0:T(8,128)}, u32[]{:S(2)}) copy-start(f32[32,768]{1,0:T(8,128)} %param.28) | copy-start | bytes 294916
  41.0 73.8 %copy-start.4 = (f32[768]{0:T(1024)S(1)}, f32[768]{0:T(1024)}, u32[]{:S(2)}) copy-start(f32[768]{0:T(1024)} %param.26) | copy-start | bytes 9220
  41.0 237.5 %reduce-scatter.8.cloned.1.call-start = ((), (), s32[]{:S(2)}) async-start(), calls=%async_computation.6 | async-start | bytes 835584 | tf_op jit(solution)/shard_map/reduce_scatter | solution.py:64
  211.4 212.4 %all-reduce.10.cloned.1.call-start = ((), (), s32[]{:S(2)}) async-start(), calls=%async_computation.11 | async-start | bytes 196608 | tf_op jit(solution)/shard_map/psum | solution.py:87
  280.3 268.2 %reduce-scatter.10.cloned.1.call-start = ((), (), s32[]{:S(2)}) async-start(), calls=%async_computation.7 | async-start | bytes 1671168 | tf_op jit(solution)/shard_map/reduce_scatter | solution.py:64
  280.9 169.4 %copy-start.6 = (f32[96]{0:T(128)}, f32[96]{0:T(128)S(1)}, u32[]{:S(2)}) copy-start(f32[96]{0:T(128)S(1)} %compare_convert_fusion) | copy-start | bytes 1156
  479.7 233.9 %reduce-scatter.12.cloned.1.call-start = ((), (), s32[]{:S(2)}) async-start(), calls=%async_computation.8 | async-start | bytes 835584 | tf_op jit(solution)/shard_map/reduce_scatter | solution.py:64
  646.3 213.1 %all-reduce.8.cloned.1.call-start = ((), (), s32[]{:S(2)}) async-start(), calls=%async_computation.10 | async-start | bytes 196608 | tf_op jit(solution)/shard_map/psum | solution.py:87
  715.4 269.0 %reduce-scatter.14.cloned.1.call-start = ((), (), s32[]{:S(2)}) async-start(), calls=%async_computation.9 | async-start | bytes 1671168 | tf_op jit(solution)/shard_map/reduce_scatter | solution.py:64
  879.5 6.1 copy-start.7
  885.9 99.4 %copy-start.3 = (f32[32,768]{1,0:T(8,128)}, f32[32,768]{1,0:T(8,128)S(1)}, u32[]{:S(2)}) copy-start(f32[32,768]{1,0:T(8,128)S(1)} %fusion.111) | copy-start | bytes 294916
  886.2 173.4 %copy-start.1 = (f32[32,768]{1,0:T(8,128)}, f32[32,768]{1,0:T(8,128)S(1)}, u32[]{:S(2)}) copy-start(f32[32,768]{1,0:T(8,128)S(1)} %fusion.112) | copy-start | bytes 294916
Sparse Core Ops, SparseCore 0:
  41.1 72.6 reduce-scatter.5
  211.5 66.9 reduce-scatter.7
  284.0 139.7 all-reduce.9
  479.8 68.7 reduce-scatter.9
  646.5 67.0 reduce-scatter.11
  719.6 139.7 all-reduce.7
  915.7 68.6 reduce-scatter.13
where the time goes:
time: 1080 us; the launch traced here: 1070 us
  waiting for transfers between devices  627 us (58%)
  blocking collectives  271 us (25%)
  other arithmetic  90.4 us (8%)
  matrix products  45.2 us (4%)
  between operations  17.8 us (2%)
  local copies, waits for them, and re-layouts  15.5 us (1%)
    reduce_scatter x5, waiting for transfers between devices, apply_graph(): lax.psum_scatter(partial_value.astype(jnp.bfloat16), 'bcol', scatter_dime...  341 us
    psum x2, waiting for transfers between devices, local(): lax.psum((highest_dot(basis, basis.T), highest_dot(basis, basis_image.T))...  286 us
    psum x3, blocking collectives, local(): lax.psum((highest_dot(vectors, vectors.T), highest_dot(vectors, image_x.T...  199 us
    all_gather x5, blocking collectives, fetch(): return lax.all_gather(scaled, 'brow', axis=1, tiled=True)  71.9 us
    scatter-add x5, other arithmetic, local_partial(): total = empty.at[:, row_index].add(products * kept_mask[None, :, None])  25.5 us
    dot_general x5, matrix products, local_partial(): jnp.einsum('sab,csb->csa', block_set, picked, preferred_element_type=jnp....  25.3 us
  transfers between devices with their start and end apart: 7, of which 7 were waited for; matrix products, arithmetic and copies ran while one was open for 0% of the time, Pallas kernels for 0%

commit v1 on v0

v1 whole, which is shorter than its diff:
```python
import functools

import jax
import jax.numpy as jnp
from jax import lax
from jax.experimental import pallas as pl
from jax.experimental.pallas import tpu as pltpu
from jax.sharding import PartitionSpec as P

ITERS = 2
NS_STEPS = 8
CHUNK = 8
HIGH = lax.Precision.HIGHEST
BF = jnp.bfloat16
F32 = jnp.float32


def nn(a, b):
    return lax.dot_general(a, b, (((1,), (0,)), ((), ())), precision=HIGH, preferred_element_type=F32)


def nt(a, b):
    return lax.dot_general(a, b, (((1,), (1,)), ((), ())), precision=HIGH, preferred_element_type=F32)


def graph_kernel(n_slots, live_ref, rows_ref, cols_ref, near_ref, far_ref, blocks_ref, out_ref,
                 held, panel, acc, sems):
    chunks = n_slots // CHUNK
    live = live_ref[0]

    def fetch(c):
        part = pl.ds(c * CHUNK, CHUNK)
        return pltpu.make_async_copy(blocks_ref.at[part], held.at[part], sems.at[c])

    for c in range(chunks):
        @pl.when(c * CHUNK < live)
        def _():
            fetch(c).start()
    sub = panel.shape[0] // 8
    for s in range(8):
        src = near_ref if s < 4 else far_ref
        for q in range(sub):
            panel[s * sub + q] = src[s % 4, :, q * 256:(q + 1) * 256]
    acc[...] = jnp.zeros_like(acc)
    for c in range(chunks):
        @pl.when(c * CHUNK < live)
        def _():
            fetch(c).wait()
            for t in range(CHUNK):
                s = c * CHUNK + t
                prod = lax.dot_general(panel[cols_ref[s]], held[s], (((1,), (1,)), ((), ())),
                                       preferred_element_type=F32)
                row = rows_ref[s]
                acc[row] = acc[row] + prod
    for j in range(out_ref.shape[0]):
        for q in range(sub):
            out_ref[j, :, q * 256:(q + 1) * 256] = acc[j * sub + q].astype(BF)


def graph_partial(live, rows, cols, near, far, blocks, owners):
    n_slots, side, _ = blocks.shape
    r, width = near.shape[1:]
    sub = width // side
    return pl.pallas_call(
        functools.partial(graph_kernel, n_slots),
        out_shape=jax.ShapeDtypeStruct((owners, r, width), BF),
        in_specs=[pl.BlockSpec(memory_space=pltpu.SMEM)] * 3
        + [pl.BlockSpec(memory_space=pltpu.VMEM)] * 2
        + [pl.BlockSpec(memory_space=pl.ANY)],
        out_specs=pl.BlockSpec(memory_space=pltpu.VMEM),
        scratch_shapes=[
            pltpu.VMEM((n_slots, side, side), BF),
            pltpu.VMEM((8 * sub, r, side), BF),
            pltpu.VMEM((owners * sub + 1, r, side), F32),
            pltpu.SemaphoreType.DMA((n_slots // CHUNK,)),
        ],
        compiler_params=pltpu.CompilerParams(vmem_limit_bytes=32 * 2**20),
        name="graph_partial",
    )(live, rows, cols, near, far, blocks)


def spd_inverse(a):
    n = a.shape[0]
    ri = lax.broadcasted_iota(jnp.int32, (n, n), 0)
    ci = lax.broadcasted_iota(jnp.int32, (n, n), 1)
    r1 = lax.broadcasted_iota(jnp.int32, (n, 1), 0)
    c1 = lax.broadcasted_iota(jnp.int32, (1, n), 1)
    for k in range(n):
        p = 1.0 / a[k:k + 1, k:k + 1]
        row = jnp.where(c1 == k, -1.0, a[k:k + 1, :]) * p
        col = jnp.where(r1 == k, -1.0, a[:, k:k + 1])
        a = jnp.where((ri == k) | (ci == k), 0.0, a) - col * row
    return -a


def residual_coeffs(x, h, shift):
    tx = nn(x, h)
    gram = nt(tx, x)
    moved = shift(x)
    zt = nn(nt(moved, tx), spd_inverse(gram))
    return nn(zt, x) - moved


def ritz_rows(basis, h, cutoff, shift, wanted):
    tb = nn(basis, h)
    moved = shift(basis)
    gram = nt(tb, basis)
    sym = 0.5 * (nt(tb, moved) + nt(moved, tb))
    n = gram.shape[0]
    eye = (lax.broadcasted_iota(jnp.int32, (n, n), 0)
           == lax.broadcasted_iota(jnp.int32, (n, n), 1)).astype(F32)
    s = (cutoff - 1.0) * eye + nn(sym, spd_inverse(gram))
    s2 = nn(s, s)
    total = jnp.sum(jnp.sum(s2 * eye, axis=1, keepdims=True), axis=0, keepdims=True)
    scale = lax.rsqrt(total + 1e-06)
    s = s * scale
    s2 = s2 * (scale * scale)
    s = 1.5 * s - 0.5 * nn(s, s2)
    for _ in range(NS_STEPS - 1):
        s = 1.5 * s - 0.5 * nn(s, nn(s, s))
    return 0.5 * (eye + s)[:wanted]


def small_math(h, cutoff, wanted, shift):
    width = h.shape[0]
    ri = lax.broadcasted_iota(jnp.int32, (wanted, width), 0)
    ci = lax.broadcasted_iota(jnp.int32, (wanted, width), 1)
    x = (ri == ci).astype(F32)
    p = (ri + wanted == ci).astype(F32)
    for _ in range(ITERS):
        r = residual_coeffs(x, h, shift)
        basis = jnp.concatenate([x, r, p], 0)
        rows = ritz_rows(basis, h, cutoff, shift, wanted)
        keep = lax.broadcasted_iota(jnp.int32, rows.shape, 1) >= wanted
        both = nn(jnp.concatenate([rows, jnp.where(keep, rows, 0.0)], 0), basis)
        x, p = both[:wanted], both[wanted:]
    r = residual_coeffs(x, h, shift)
    return jnp.concatenate([x, p, r, p - shift(p)], 0)


def small_kernel(wanted, cut_ref, g_ref, out_ref):
    pieces, cols = g_ref.shape
    width = out_ref.shape[1]
    h = jnp.concatenate([g_ref[...], jnp.zeros((width - pieces, cols), F32)], 0)
    out_ref[...] = small_math(h, cut_ref[0], wanted, lambda v: pltpu.roll(v, 2 * wanted, 1))


def small(cutoff, gram, wanted):
    return pl.pallas_call(
        functools.partial(small_kernel, wanted),
        out_shape=jax.ShapeDtypeStruct((4 * wanted, gram.shape[1]), F32),
        in_specs=[pl.BlockSpec(memory_space=pltpu.SMEM), pl.BlockSpec(memory_space=pltpu.VMEM)],
        out_specs=pl.BlockSpec(memory_space=pltpu.VMEM),
        compiler_params=pltpu.CompilerParams(vmem_limit_bytes=32 * 2**20),
        name="small_matrices",
    )(cutoff, gram)


def z_turn(k):
    return [(i, (i + 2 * k) % 8) for i in range(8)]


def y_turn(k):
    return [(i, (i // 4) * 4 + (i + k) % 4) for i in range(16)]


def x_turn(k):
    return [(i, (i + 4 * k) % 16) for i in range(16)]


CORE = [(i, i ^ 1) for i in range(8)]


def gather_brow(v):
    near = jnp.stack([v] + [lax.ppermute(v, "brow", z_turn(k)) for k in (1, 2, 3)])
    return near, lax.ppermute(near, "brow", CORE)


def sum_all(g):
    half = g.shape[0] // 2
    me = lax.axis_index("brow") % 2
    mine = lax.dynamic_slice_in_dim(g, me * half, half, 0)
    other = lax.dynamic_slice_in_dim(g, (1 - me) * half, half, 0)
    v = mine + lax.ppermute(other, "brow", CORE)
    for axis, turn in (("brow", z_turn), ("bcol", y_turn), ("bcol", x_turn)):
        a, b, c = [lax.ppermute(v, axis, turn(k)) for k in (1, 2, 3)]
        v = (v + a) + (b + c)
    w = lax.ppermute(v, "brow", CORE)
    first = jnp.where(me == 0, v, w)
    second = jnp.where(me == 0, w, v)
    return jnp.concatenate([first, second], 0)


def local(blocks, pattern_rows, pattern_cols, live_count, degree_scale, eigen_block, direction, cutoff):
    block_set = blocks[0, 0]
    n_slots, side, _ = block_set.shape
    wanted, width = eigen_block.shape
    sub = width // side
    owners = lax.axis_size("bcol")
    live = live_count.reshape(1)
    brow = lax.axis_index("brow")
    rows = jnp.where(jnp.arange(n_slots) < live[0], pattern_rows[0, 0], owners * sub)
    col = pattern_cols[0, 0]
    src = col // sub
    cols = ((brow // 2 - src // 2) % 4 + 4 * ((brow - src) % 2)) * sub + col % sub

    def apply_graph(v):
        near, far = gather_brow((degree_scale * v).astype(BF))
        part = graph_partial(live, rows, cols, near, far, block_set, owners)
        got = lax.all_to_all(part, "bcol", 0, 0)
        return degree_scale * jnp.sum(got.astype(F32), axis=0)

    k0 = jnp.concatenate([eigen_block, direction], 0)
    k1 = apply_graph(k0)
    k2 = apply_graph(k1)
    k3 = apply_graph(k2[:wanted])
    krylov = jnp.concatenate([k0, k1, k2, k3, jnp.zeros((wanted, width), F32)], 0)
    gram = nt(krylov[:5 * wanted], krylov)
    gram = sum_all(gram)
    coeffs = small(cutoff, gram, wanted)
    out = nn(coeffs, krylov)
    return out[:wanted], out[wanted:2 * wanted], out[2 * wanted:3 * wanted], out[3 * wanted:]


def solution(mesh):
    docs = P(None, ("brow", "bcol"))
    return jax.shard_map(
        local,
        mesh=mesh,
        in_specs=(
            P("brow", "bcol", None, None, None),
            P("brow", "bcol", None),
            P("brow", "bcol", None),
            P("brow", "bcol"),
            P(("brow", "bcol")),
            docs,
            docs,
            P(),
        ),
        out_specs=(docs, docs, docs, docs),
        check_vma=False,
    )
```

time: 1080 us -> 193 us (0.18); the launches traced: 1070 us -> 193 us
  waiting for transfers between devices: 627 us -> 56.9 us
  blocking collectives: 271 us -> 29.3 us
  other arithmetic: 90.4 us -> 3.51 us
  starting transfers between devices: 0.75 us -> 51.4 us
  matrix products: 45.2 us -> 1.53 us
  Pallas kernels: 0 us -> 42.4 us
  between operations: 17.8 us -> 2.25 us
    reduce_scatter x5 -> x0, waiting for transfers between devices: 341 us -> none  [apply_graph(): lax.psum_scatter(partial_value.astype(jnp.bfloat16), 'bcol', scatter_dime...]
    psum x2 -> x0, waiting for transfers between devices: 286 us -> none  [local(): lax.psum((highest_dot(basis, basis.T), highest_dot(basis, basis_image.T))...]
    psum x3 -> x0, blocking collectives: 199 us -> none  [local(): lax.psum((highest_dot(vectors, vectors.T), highest_dot(vectors, image_x.T...]
    all_gather x5 -> x0, blocking collectives: 71.9 us -> none  [fetch(): return lax.all_gather(scaled, 'brow', axis=1, tiled=True)]
    another operation x23 -> x4, other arithmetic: 53.7 us -> 0.14 us  [gather_brow(): jnp.stack([v] + [lax.ppermute(v, 'brow', z_turn(k)) for k in (1, 2, 3)])]
    pallas_call x0 -> x4, Pallas kernels: none -> 42.4 us  [the longest x1 34.4 us: small(): pl.pallas_call(functools.partial(small_kernel, wanted), out_shape=jax.Sha...]
    ppermute x0 -> x23, starting transfers between devices: none -> 41.7 us  [the longest x9 17.3 us: gather_brow(): lax.ppermute(v, 'brow', z_turn(k))]
    dot_general x56 -> x2, matrix products: 39.8 us -> 1.53 us  [the longest x1 0.95 us: nt(): lax.dot_general(a, b, (((1,), (1,)), ((), ())), precision=HIGH, preferred...]
  transfers between devices with their start and end apart: 7 -> 25, of which waited for: 7 -> 21; matrix products, arithmetic and copies ran while one was open for 0% -> 1% of each run, Pallas kernels for 0% -> 0%
where the time goes in v1:
time: 193 us
  waiting for transfers between devices  56.9 us (29%)
  starting transfers between devices  51.4 us (27%)
  Pallas kernels  42.4 us (22%)
  blocking collectives  29.3 us (15%)
  local copies, waits for them, and re-layouts  5.79 us (3%)
  other arithmetic  3.51 us (2%)
  between operations  2.25 us (1%)
    pallas_call x1, Pallas kernels, small(): pl.pallas_call(functools.partial(small_kernel, wanted), out_shape=jax.Sha...  34.4 us
    all_to_all x2, waiting for transfers between devices, apply_graph(): got = lax.all_to_all(part, 'bcol', 0, 0)  33.2 us
    all_to_all x1, blocking collectives, apply_graph(): got = lax.all_to_all(part, 'bcol', 0, 0)  29.3 us
    ppermute x9, starting transfers between devices, gather_brow(): lax.ppermute(v, 'brow', z_turn(k))  17.3 us
    ppermute x9, waiting for transfers between devices, gather_brow(): lax.ppermute(v, 'brow', z_turn(k))  10.6 us
    ppermute x9, starting transfers between devices, sum_all(): a, b, c = [lax.ppermute(v, axis, turn(k)) for k in (1, 2, 3)]  9.99 us
    all_to_all x2, starting transfers between devices, apply_graph(): got = lax.all_to_all(part, 'bcol', 0, 0)  9.67 us
    ppermute x9, waiting for transfers between devices, sum_all(): a, b, c = [lax.ppermute(v, axis, turn(k)) for k in (1, 2, 3)]  9.48 us
  transfers between devices with their start and end apart: 25, of which 21 were waited for; matrix products, arithmetic and copies ran while one was open for 1% of the time, Pallas kernels for 0%

profile of v1, /device:TPU:1, one launch (start us, length us, event | category | flops | bytes accessed | tf_op | source)
XLA Modules:
  0.0 193.0 jit_solution(6618759782593120933)
XLA Ops:
  1.6 4.7 %collective-permute-start.2 = (bf16[64,768]{1,0:T(8,128)(2,1)S(1)}, bf16[64,768]{1,0:T(8,128)(2,1)S(1)}, u32[]{:S(2)}, u32[]{:S(2)}) collective-permute-start(bf16[64,768]{1,0:T(8,128)(2,1)S(1)} %fusion.3), channel_id=1, source_target_pairs={{0,96},{16,112},{32,0},{48,16},{64,32},{80,48},{96,64},{112,80},{1... | collective-permute-start | bytes 294920 | tf_op jit(solution)/shard_map/ppermute | solution.py:175
  8.5 3.6 %collective-permute-done = bf16[64,768]{1,0:T(8,128)(2,1)S(1)} collective-permute-done((bf16[64,768]{1,0:T(8,128)(2,1)S(1)}, bf16[64,768]{1,0:T(8,128)(2,1)S(1)}, u32[]{:S(2)}, u32[]{:S(2)}) %collective-permute-start) | collective-permute-done | bytes 98336 | tf_op jit(solution)/shard_map/ppermute | solution.py:175
  12.6 2.3 %collective-permute-start.3 = (bf16[4,64,768]{2,1,0:T(8,128)(2,1)S(1)}, bf16[4,64,768]{2,1,0:T(8,128)(2,1)S(1)}, u32[]{:S(2)}, u32[]{:S(2)}) collective-permute-start(bf16[4,64,768]{2,1,0:T(8,128)(2,1)S(1)} %pad_maximum_fusion.6.near_ref), channel_id=1, source_target_pairs={{0,16},{16,0},{32,48},{48,32},{64,80},{80,64},{96,112},{112,96},{1... | collective-permute-start | bytes 1179656 | tf_op jit(solution)/shard_map/ppermute | solution.py:176
  16.3 2.5 %copy-done = bf16[1,1,40,256,256]{4,3,2,1,0:T(8,128)(2,1)S(1)} copy-done((bf16[1,1,40,256,256]{4,3,2,1,0:T(8,128)(2,1)S(1)}, bf16[1,1,40,256,256]{4,3,2,1,0:T(8,128)(2,1)}, u32[]{:S(2)}) %copy-start) | copy-done | bytes 5242904
  18.8 2.1 %graph_partial.3 = bf16[16,64,768]{2,1,0:T(8,128)(2,1)S(1)} custom-call(s32[1]{0:T(128)} %bitcast.42.live_ref, s32[40]{0:T(128)S(1)} %get-tuple-element.14.rows_ref, s32[40]{0:T(128)S(1)} %get-tuple-element.15.cols_ref, bf16[4,64,768]{2,1,0:T(8,128)(2,1)S(1)} %pad_maximum_fusion.6.near_ref, bf16[4,64,768]{2,1,0:T(8,128)(2,1)S(1)} %collective-permute-done.3.far_ref, ...), custom_call_target="tpu_custom_call" | custom-call | tf_op jit(solution)/shard_map/graph_partial/pallas_call | solution.py:64
  20.9 29.3 %all_to_all.15 = bf16[16,64,768]{2,1,0:T(8,128)(2,1)S(1)} all-to-all(bf16[16,64,768]{2,1,0:T(8,128)(2,1)S(1)} %graph_partial.3), channel_id=1, replica_groups=mesh['brow'=8,'bcol'=16] {'bcol'}, dimensions={0} | all-to-all | bytes 3145728 | tf_op jit(solution)/shard_map/all_to_all | solution.py:210
  50.5 2.1 %collective-permute-start.5 = (bf16[64,768]{1,0:T(8,128)(2,1)S(1)}, bf16[64,768]{1,0:T(8,128)(2,1)S(1)}, u32[]{:S(2)}, u32[]{:S(2)}) collective-permute-start(bf16[64,768]{1,0:T(8,128)(2,1)S(1)} %get-tuple-element.6), channel_id=1, source_target_pairs={{0,64},{16,80},{32,96},{48,112},{64,0},{80,16},{96,32},{112,48},{1... | collective-permute-start | bytes 294920 | tf_op jit(solution)/shard_map/ppermute | solution.py:175
  53.7 2.5 %collective-permute-done.4 = bf16[64,768]{1,0:T(8,128)(2,1)S(1)} collective-permute-done((bf16[64,768]{1,0:T(8,128)(2,1)S(1)}, bf16[64,768]{1,0:T(8,128)(2,1)S(1)}, u32[]{:S(2)}, u32[]{:S(2)}) %collective-permute-start.4) | collective-permute-done | bytes 98336 | tf_op jit(solution)/shard_map/ppermute | solution.py:175
  57.1 3.3 %collective-permute-start.7 = (bf16[4,64,768]{2,1,0:T(8,128)(2,1)S(1)}, bf16[4,64,768]{2,1,0:T(8,128)(2,1)S(1)}, u32[]{:S(2)}, u32[]{:S(2)}) collective-permute-start(bf16[4,64,768]{2,1,0:T(8,128)(2,1)S(1)} %pad_maximum_fusion.7.near_ref), channel_id=1, source_target_pairs={{0,16},{16,0},{32,48},{48,32},{64,80},{80,64},{96,112},{112,96},{1... | collective-permute-start | bytes 1179656 | tf_op jit(solution)/shard_map/ppermute | solution.py:176
  61.8 3.2 %graph_partial.4 = bf16[16,64,768]{2,1,0:T(8,128)(2,1)} custom-call(s32[1]{0:T(128)} %bitcast.43.live_ref, s32[40]{0:T(128)S(1)} %get-tuple-element.14.rows_ref, s32[40]{0:T(128)S(1)} %get-tuple-element.15.cols_ref, bf16[4,64,768]{2,1,0:T(8,128)(2,1)S(1)} %pad_maximum_fusion.7.near_ref, bf16[4,64,768]{2,1,0:T(8,128)(2,1)S(1)} %collective-permute-done.7.far_ref, ...), custom_call_target="tpu_custom_call" | custom-call | tf_op jit(solution)/shard_map/graph_partial/pallas_call | solution.py:64
  65.1 3.9 %all-to-all-start.1 = ((bf16[16,64,768]{2,1,0:T(8,128)(2,1)}), bf16[16,64,768]{2,1,0:T(8,128)(2,1)S(1)}, u32[]{:S(2)}, u32[]{:S(2)}) async-start(bf16[16,64,768]{2,1,0:T(8,128)(2,1)} %graph_partial.4), calls=%async_computation.1 | async-start | bytes 3145728 | tf_op jit(solution)/shard_map/all_to_all | solution.py:210
  69.1 20.4 %all-to-all-done.1 = bf16[16,64,768]{2,1,0:T(8,128)(2,1)S(1)} async-done(((bf16[16,64,768]{2,1,0:T(8,128)(2,1)}), bf16[16,64,768]{2,1,0:T(8,128)(2,1)S(1)}, u32[]{:S(2)}, u32[]{:S(2)}) %all-to-all-start.1) | async-done | bytes 1572896 | tf_op jit(solution)/shard_map/all_to_all | solution.py:210
  89.8 2.4 %collective-permute-start.8 = (bf16[32,768]{1,0:T(8,128)(2,1)S(1)}, bf16[32,768]{1,0:T(8,128)(2,1)S(1)}, u32[]{:S(2)}, u32[]{:S(2)}) collective-permute-start(bf16[32,768]{1,0:T(8,128)(2,1)S(1)} %fusion.6), channel_id=1, source_target_pairs={{0,32},{16,48},{32,64},{48,80},{64,96},{80,112},{96,0},{112,16},{1... | collective-permute-start | bytes 147464 | tf_op jit(solution)/shard_map/ppermute | solution.py:175
  92.2 5.6 %collective-permute-start.9 = (bf16[32,768]{1,0:T(8,128)(2,1)S(1)}, bf16[32,768]{1,0:T(8,128)(2,1)S(1)}, u32[]{:S(2)}, u32[]{:S(2)}) collective-permute-start(bf16[32,768]{1,0:T(8,128)(2,1)S(1)} %fusion.6), channel_id=1, source_target_pairs={{0,64},{16,80},{32,96},{48,112},{64,0},{80,16},{96,32},{112,48},{1... | collective-permute-start | bytes 147464 | tf_op jit(solution)/shard_map/ppermute | solution.py:175
  104.0 2.5 %copy-done.2 = bf16[1,1,40,256,256]{4,3,2,1,0:T(8,128)(2,1)S(1)} copy-done((bf16[1,1,40,256,256]{4,3,2,1,0:T(8,128)(2,1)S(1)}, bf16[1,1,40,256,256]{4,3,2,1,0:T(8,128)(2,1)}, u32[]{:S(2)}) %copy-start.2) | copy-done | bytes 5242904
  106.5 2.7 %graph_partial.5 = bf16[16,32,768]{2,1,0:T(8,128)(2,1)} custom-call(s32[1]{0:T(128)} %bitcast.44.live_ref, s32[40]{0:T(128)S(1)} %get-tuple-element.14.rows_ref, s32[40]{0:T(128)S(1)} %get-tuple-element.15.cols_ref, bf16[4,32,768]{2,1,0:T(8,128)(2,1)S(1)} %pad_maximum_fusion.8.near_ref, bf16[4,32,768]{2,1,0:T(8,128)(2,1)S(1)} %collective-permute-done.11.far_ref, ...), custom_call_target="tpu_custom_call" | custom-call | tf_op jit(solution)/shard_map/graph_partial/pallas_call | solution.py:64
  109.2 5.8 %all-to-all-start.2 = ((bf16[16,32,768]{2,1,0:T(8,128)(2,1)}), bf16[16,32,768]{2,1,0:T(8,128)(2,1)S(1)}, u32[]{:S(2)}, u32[]{:S(2)}) async-start(bf16[16,32,768]{2,1,0:T(8,128)(2,1)} %graph_partial.5), calls=%async_computation.2 | async-start | bytes 1572864 | tf_op jit(solution)/shard_map/all_to_all | solution.py:210
  114.9 12.7 %all-to-all-done.2 = bf16[16,32,768]{2,1,0:T(8,128)(2,1)S(1)} async-done(((bf16[16,32,768]{2,1,0:T(8,128)(2,1)}), bf16[16,32,768]{2,1,0:T(8,128)(2,1)S(1)}, u32[]{:S(2)}, u32[]{:S(2)}) %all-to-all-start.2) | async-done | bytes 786464 | tf_op jit(solution)/shard_map/all_to_all | solution.py:210
  128.8 2.9 %collective-permute-start.12 = (f32[80,256]{1,0:T(8,128)S(1)}, f32[80,256]{1,0:T(8,128)S(1)}, u32[]{:S(2)}, u32[]{:S(2)}) collective-permute-start(f32[80,256]{1,0:T(8,128)S(1)} %constant_dynamic-slice_fusion), channel_id=1, source_target_pairs={{0,16},{16,0},{32,48},{48,32},{64,80},{80,64},{96,112},{112,96},{1... | collective-permute-start | bytes 245768 | tf_op jit(solution)/shard_map/ppermute | solution.py:184
  132.8 2.1 %collective-permute-start.14 = (f32[80,256]{1,0:T(8,128)S(1)}, f32[80,256]{1,0:T(8,128)S(1)}, u32[]{:S(2)}, u32[]{:S(2)}) collective-permute-start(f32[80,256]{1,0:T(8,128)S(1)} %dynamic-slice_add_fusion), channel_id=1, source_target_pairs={{0,64},{16,80},{32,96},{48,112},{64,0},{80,16},{96,32},{112,48},{1... | collective-permute-start | bytes 245768 | tf_op jit(solution)/shard_map/ppermute | solution.py:186
  142.6 2.0 %collective-permute-done.16 = f32[80,256]{1,0:T(8,128)S(1)} collective-permute-done((f32[80,256]{1,0:T(8,128)S(1)}, f32[80,256]{1,0:T(8,128)S(1)}, u32[]{:S(2)}, u32[]{:S(2)}) %collective-permute-start.16) | collective-permute-done | bytes 81952 | tf_op jit(solution)/shard_map/ppermute | solution.py:186
  148.9 2.6 %collective-permute-done.19 = f32[80,256]{1,0:T(8,128)S(1)} collective-permute-done((f32[80,256]{1,0:T(8,128)S(1)}, f32[80,256]{1,0:T(8,128)S(1)}, u32[]{:S(2)}, u32[]{:S(2)}) %collective-permute-start.19) | collective-permute-done | bytes 81952 | tf_op jit(solution)/shard_map/ppermute | solution.py:186
  152.2 4.1 %collective-permute-start.22 = (f32[80,256]{1,0:T(8,128)S(1)}, f32[80,256]{1,0:T(8,128)S(1)}, u32[]{:S(2)}, u32[]{:S(2)}) collective-permute-start(f32[80,256]{1,0:T(8,128)S(1)} %add_add_fusion), channel_id=1, source_target_pairs={{0,16},{16,0},{32,48},{48,32},{64,80},{80,64},{96,112},{112,96},{1... | collective-permute-start | bytes 245768 | tf_op jit(solution)/shard_map/ppermute | solution.py:188
  157.3 34.4 %small_matrices.1 = f32[128,256]{1,0:T(8,128)S(1)} custom-call(f32[1]{0:T(128)S(6)} %copy.18.cut_ref, f32[160,256]{1,0:T(8,128)S(1)} %pad_maximum_fusion.9.g_ref), custom_call_target="tpu_custom_call" | custom-call | tf_op jit(solution)/shard_map/small_matrices/pallas_call | solution.py:149
  (72 shorter events, 31.1 us)
Async XLA Ops:
  1.6 6.9 %collective-permute-start.2 = (bf16[64,768]{1,0:T(8,128)(2,1)S(1)}, bf16[64,768]{1,0:T(8,128)(2,1)S(1)}, u32[]{:S(2)}, u32[]{:S(2)}) collective-permute-start(bf16[64,768]{1,0:T(8,128)(2,1)S(1)} %fusion.3), channel_id=1, source_target_pairs={{0,96},{16,112},{32,0},{48,16},{64,32},{80,48},{96,64},{112,80},{1... | collective-permute-start | bytes 294920 | tf_op jit(solution)/shard_map/ppermute | solution.py:175
  6.2 5.9 %collective-permute-start = (bf16[64,768]{1,0:T(8,128)(2,1)S(1)}, bf16[64,768]{1,0:T(8,128)(2,1)S(1)}, u32[]{:S(2)}, u32[]{:S(2)}) collective-permute-start(bf16[64,768]{1,0:T(8,128)(2,1)S(1)} %fusion.3), channel_id=1, source_target_pairs={{0,32},{16,48},{32,64},{48,80},{64,96},{80,112},{96,0},{112,16},{1... | collective-permute-start | bytes 294920 | tf_op jit(solution)/shard_map/ppermute | solution.py:175
  6.3 6.3 %collective-permute-start.1 = (bf16[64,768]{1,0:T(8,128)(2,1)S(1)}, bf16[64,768]{1,0:T(8,128)(2,1)S(1)}, u32[]{:S(2)}, u32[]{:S(2)}) collective-permute-start(bf16[64,768]{1,0:T(8,128)(2,1)S(1)} %fusion.3), channel_id=1, source_target_pairs={{0,64},{16,80},{32,96},{48,112},{64,0},{80,16},{96,32},{112,48},{1... | collective-permute-start | bytes 294920 | tf_op jit(solution)/shard_map/ppermute | solution.py:175
  12.6 3.7 %collective-permute-start.3 = (bf16[4,64,768]{2,1,0:T(8,128)(2,1)S(1)}, bf16[4,64,768]{2,1,0:T(8,128)(2,1)S(1)}, u32[]{:S(2)}, u32[]{:S(2)}) collective-permute-start(bf16[4,64,768]{2,1,0:T(8,128)(2,1)S(1)} %pad_maximum_fusion.6.near_ref), channel_id=1, source_target_pairs={{0,16},{16,0},{32,48},{48,32},{64,80},{80,64},{96,112},{112,96},{1... | collective-permute-start | bytes 1179656 | tf_op jit(solution)/shard_map/ppermute | solution.py:176
  50.4 5.8 %collective-permute-start.4 = (bf16[64,768]{1,0:T(8,128)(2,1)S(1)}, bf16[64,768]{1,0:T(8,128)(2,1)S(1)}, u32[]{:S(2)}, u32[]{:S(2)}) collective-permute-start(bf16[64,768]{1,0:T(8,128)(2,1)S(1)} %get-tuple-element.6), channel_id=1, source_target_pairs={{0,32},{16,48},{32,64},{48,80},{64,96},{80,112},{96,0},{112,16},{1... | collective-permute-start | bytes 294920 | tf_op jit(solution)/shard_map/ppermute | solution.py:175
  50.5 5.7 %collective-permute-start.5 = (bf16[64,768]{1,0:T(8,128)(2,1)S(1)}, bf16[64,768]{1,0:T(8,128)(2,1)S(1)}, u32[]{:S(2)}, u32[]{:S(2)}) collective-permute-start(bf16[64,768]{1,0:T(8,128)(2,1)S(1)} %get-tuple-element.6), channel_id=1, source_target_pairs={{0,64},{16,80},{32,96},{48,112},{64,0},{80,16},{96,32},{112,48},{1... | collective-permute-start | bytes 294920 | tf_op jit(solution)/shard_map/ppermute | solution.py:175
  52.6 4.5 %collective-permute-start.6 = (bf16[64,768]{1,0:T(8,128)(2,1)S(1)}, bf16[64,768]{1,0:T(8,128)(2,1)S(1)}, u32[]{:S(2)}, u32[]{:S(2)}) collective-permute-start(bf16[64,768]{1,0:T(8,128)(2,1)S(1)} %get-tuple-element.6), channel_id=1, source_target_pairs={{0,96},{16,112},{32,0},{48,16},{64,32},{80,48},{96,64},{112,80},{1... | collective-permute-start | bytes 294920 | tf_op jit(solution)/shard_map/ppermute | solution.py:175
  57.1 4.6 %collective-permute-start.7 = (bf16[4,64,768]{2,1,0:T(8,128)(2,1)S(1)}, bf16[4,64,768]{2,1,0:T(8,128)(2,1)S(1)}, u32[]{:S(2)}, u32[]{:S(2)}) collective-permute-start(bf16[4,64,768]{2,1,0:T(8,128)(2,1)S(1)} %pad_maximum_fusion.7.near_ref), channel_id=1, source_target_pairs={{0,16},{16,0},{32,48},{48,32},{64,80},{80,64},{96,112},{112,96},{1... | collective-permute-start | bytes 1179656 | tf_op jit(solution)/shard_map/ppermute | solution.py:176
  65.1 24.4 %all-to-all-start.1 = ((bf16[16,64,768]{2,1,0:T(8,128)(2,1)}), bf16[16,64,768]{2,1,0:T(8,128)(2,1)S(1)}, u32[]{:S(2)}, u32[]{:S(2)}) async-start(bf16[16,64,768]{2,1,0:T(8,128)(2,1)} %graph_partial.4), calls=%async_computation.1 | async-start | bytes 3145728 | tf_op jit(solution)/shard_map/all_to_all | solution.py:210
  89.8 8.3 %collective-permute-start.8 = (bf16[32,768]{1,0:T(8,128)(2,1)S(1)}, bf16[32,768]{1,0:T(8,128)(2,1)S(1)}, u32[]{:S(2)}, u32[]{:S(2)}) collective-permute-start(bf16[32,768]{1,0:T(8,128)(2,1)S(1)} %fusion.6), channel_id=1, source_target_pairs={{0,32},{16,48},{32,64},{48,80},{64,96},{80,112},{96,0},{112,16},{1... | collective-permute-start | bytes 147464 | tf_op jit(solution)/shard_map/ppermute | solution.py:175
  92.2 7.8 %collective-permute-start.9 = (bf16[32,768]{1,0:T(8,128)(2,1)S(1)}, bf16[32,768]{1,0:T(8,128)(2,1)S(1)}, u32[]{:S(2)}, u32[]{:S(2)}) collective-permute-start(bf16[32,768]{1,0:T(8,128)(2,1)S(1)} %fusion.6), channel_id=1, source_target_pairs={{0,64},{16,80},{32,96},{48,112},{64,0},{80,16},{96,32},{112,48},{1... | collective-permute-start | bytes 147464 | tf_op jit(solution)/shard_map/ppermute | solution.py:175
  97.8 3.2 %collective-permute-start.10 = (bf16[32,768]{1,0:T(8,128)(2,1)S(1)}, bf16[32,768]{1,0:T(8,128)(2,1)S(1)}, u32[]{:S(2)}, u32[]{:S(2)}) collective-permute-start(bf16[32,768]{1,0:T(8,128)(2,1)S(1)} %fusion.6), channel_id=1, source_target_pairs={{0,96},{16,112},{32,0},{48,16},{64,32},{80,48},{96,64},{112,80},{1... | collective-permute-start | bytes 147464 | tf_op jit(solution)/shard_map/ppermute | solution.py:175
  109.2 18.5 %all-to-all-start.2 = ((bf16[16,32,768]{2,1,0:T(8,128)(2,1)}), bf16[16,32,768]{2,1,0:T(8,128)(2,1)S(1)}, u32[]{:S(2)}, u32[]{:S(2)}) async-start(bf16[16,32,768]{2,1,0:T(8,128)(2,1)} %graph_partial.5), calls=%async_computation.2 | async-start | bytes 1572864 | tf_op jit(solution)/shard_map/all_to_all | solution.py:210
  128.8 3.8 %collective-permute-start.12 = (f32[80,256]{1,0:T(8,128)S(1)}, f32[80,256]{1,0:T(8,128)S(1)}, u32[]{:S(2)}, u32[]{:S(2)}) collective-permute-start(f32[80,256]{1,0:T(8,128)S(1)} %constant_dynamic-slice_fusion), channel_id=1, source_target_pairs={{0,16},{16,0},{32,48},{48,32},{64,80},{80,64},{96,112},{112,96},{1... | collective-permute-start | bytes 245768 | tf_op jit(solution)/shard_map/ppermute | solution.py:184
  132.6 5.7 %collective-permute-start.13 = (f32[80,256]{1,0:T(8,128)S(1)}, f32[80,256]{1,0:T(8,128)S(1)}, u32[]{:S(2)}, u32[]{:S(2)}) collective-permute-start(f32[80,256]{1,0:T(8,128)S(1)} %dynamic-slice_add_fusion), channel_id=1, source_target_pairs={{0,32},{16,48},{32,64},{48,80},{64,96},{80,112},{96,0},{112,16},{1... | collective-permute-start | bytes 245768 | tf_op jit(solution)/shard_map/ppermute | solution.py:186
  132.8 6.2 %collective-permute-start.14 = (f32[80,256]{1,0:T(8,128)S(1)}, f32[80,256]{1,0:T(8,128)S(1)}, u32[]{:S(2)}, u32[]{:S(2)}) collective-permute-start(f32[80,256]{1,0:T(8,128)S(1)} %dynamic-slice_add_fusion), channel_id=1, source_target_pairs={{0,64},{16,80},{32,96},{48,112},{64,0},{80,16},{96,32},{112,48},{1... | collective-permute-start | bytes 245768 | tf_op jit(solution)/shard_map/ppermute | solution.py:186
  134.9 4.8 %collective-permute-start.15 = (f32[80,256]{1,0:T(8,128)S(1)}, f32[80,256]{1,0:T(8,128)S(1)}, u32[]{:S(2)}, u32[]{:S(2)}) collective-permute-start(f32[80,256]{1,0:T(8,128)S(1)} %dynamic-slice_add_fusion), channel_id=1, source_target_pairs={{0,96},{16,112},{32,0},{48,16},{64,32},{80,48},{96,64},{112,80},{1... | collective-permute-start | bytes 245768 | tf_op jit(solution)/shard_map/ppermute | solution.py:186
  139.8 4.9 %collective-permute-start.16 = (f32[80,256]{1,0:T(8,128)S(1)}, f32[80,256]{1,0:T(8,128)S(1)}, u32[]{:S(2)}, u32[]{:S(2)}) collective-permute-start(f32[80,256]{1,0:T(8,128)S(1)} %add_add_fusion.2), channel_id=1, source_target_pairs={{0,1},{1,2},{2,3},{3,0},{4,5},{5,6},{6,7},{7,4},{8,9},{9,10},{10,1... | collective-permute-start | bytes 245768 | tf_op jit(solution)/shard_map/ppermute | solution.py:186
  140.1 5.7 %collective-permute-start.17 = (f32[80,256]{1,0:T(8,128)S(1)}, f32[80,256]{1,0:T(8,128)S(1)}, u32[]{:S(2)}, u32[]{:S(2)}) collective-permute-start(f32[80,256]{1,0:T(8,128)S(1)} %add_add_fusion.2), channel_id=1, source_target_pairs={{0,2},{1,3},{2,0},{3,1},{4,6},{5,7},{6,4},{7,5},{8,10},{9,11},{10,... | collective-permute-start | bytes 245768 | tf_op jit(solution)/shard_map/ppermute | solution.py:186
  141.1 5.0 %collective-permute-start.18 = (f32[80,256]{1,0:T(8,128)S(1)}, f32[80,256]{1,0:T(8,128)S(1)}, u32[]{:S(2)}, u32[]{:S(2)}) collective-permute-start(f32[80,256]{1,0:T(8,128)S(1)} %add_add_fusion.2), channel_id=1, source_target_pairs={{0,3},{1,0},{2,1},{3,2},{4,7},{5,4},{6,5},{7,6},{8,11},{9,8},{10,9... | collective-permute-start | bytes 245768 | tf_op jit(solution)/shard_map/ppermute | solution.py:186
  146.1 5.4 %collective-permute-start.19 = (f32[80,256]{1,0:T(8,128)S(1)}, f32[80,256]{1,0:T(8,128)S(1)}, u32[]{:S(2)}, u32[]{:S(2)}) collective-permute-start(f32[80,256]{1,0:T(8,128)S(1)} %add_add_fusion.1), channel_id=1, source_target_pairs={{0,4},{1,5},{2,6},{3,7},{4,8},{5,9},{6,10},{7,11},{8,12},{9,13},{1... | collective-permute-start | bytes 245768 | tf_op jit(solution)/shard_map/ppermute | solution.py:186
  146.2 5.4 %collective-permute-start.20 = (f32[80,256]{1,0:T(8,128)S(1)}, f32[80,256]{1,0:T(8,128)S(1)}, u32[]{:S(2)}, u32[]{:S(2)}) collective-permute-start(f32[80,256]{1,0:T(8,128)S(1)} %add_add_fusion.1), channel_id=1, source_target_pairs={{0,8},{1,9},{2,10},{3,11},{4,12},{5,13},{6,14},{7,15},{8,0},{9,1},... | collective-permute-start | bytes 245768 | tf_op jit(solution)/shard_map/ppermute | solution.py:186
  148.0 4.1 %collective-permute-start.21 = (f32[80,256]{1,0:T(8,128)S(1)}, f32[80,256]{1,0:T(8,128)S(1)}, u32[]{:S(2)}, u32[]{:S(2)}) collective-permute-start(f32[80,256]{1,0:T(8,128)S(1)} %add_add_fusion.1), channel_id=1, source_target_pairs={{0,12},{1,13},{2,14},{3,15},{4,0},{5,1},{6,2},{7,3},{8,4},{9,5},{1... | collective-permute-start | bytes 245768 | tf_op jit(solution)/shard_map/ppermute | solution.py:186
  152.2 5.1 %collective-permute-start.22 = (f32[80,256]{1,0:T(8,128)S(1)}, f32[80,256]{1,0:T(8,128)S(1)}, u32[]{:S(2)}, u32[]{:S(2)}) collective-permute-start(f32[80,256]{1,0:T(8,128)S(1)} %add_add_fusion), channel_id=1, source_target_pairs={{0,16},{16,0},{32,48},{48,32},{64,80},{80,64},{96,112},{112,96},{1... | collective-permute-start | bytes 245768 | tf_op jit(solution)/shard_map/ppermute | solution.py:188
  (7 other events, 88.3 us)

commit v2 on v1

--- a/solution.py
+++ b/solution.py
@@ -66,7 +66,7 @@
         out_shape=jax.ShapeDtypeStruct((owners, r, width), BF),
         in_specs=[pl.BlockSpec(memory_space=pltpu.SMEM)] * 3
         + [pl.BlockSpec(memory_space=pltpu.VMEM)] * 2
-        + [pl.BlockSpec(memory_space=pl.ANY)],
+        + [pl.BlockSpec(memory_space=pltpu.HBM)],
         out_specs=pl.BlockSpec(memory_space=pltpu.VMEM),
         scratch_shapes=[
             pltpu.VMEM((n_slots, side, side), BF),
@@ -74,42 +74,92 @@
             pltpu.VMEM((owners * sub + 1, r, side), F32),
             pltpu.SemaphoreType.DMA((n_slots // CHUNK,)),
         ],
-        compiler_params=pltpu.CompilerParams(vmem_limit_bytes=32 * 2**20),
+        compiler_params=pltpu.CompilerParams(vmem_limit_bytes=50 * 2**20),
         name="graph_partial",
     )(live, rows, cols, near, far, blocks)
 
 
-def spd_inverse(a):
-    n = a.shape[0]
+def eye_mask(n):
+    return (lax.broadcasted_iota(jnp.int32, (n, n), 0) == lax.broadcasted_iota(jnp.int32, (n, n), 1))
+
+
+def sweep_inverse(ref):
+    n = ref.shape[0]
     ri = lax.broadcasted_iota(jnp.int32, (n, n), 0)
     ci = lax.broadcasted_iota(jnp.int32, (n, n), 1)
-    r1 = lax.broadcasted_iota(jnp.int32, (n, 1), 0)
-    c1 = lax.broadcasted_iota(jnp.int32, (1, n), 1)
-    for k in range(n):
-        p = 1.0 / a[k:k + 1, k:k + 1]
-        row = jnp.where(c1 == k, -1.0, a[k:k + 1, :]) * p
-        col = jnp.where(r1 == k, -1.0, a[:, k:k + 1])
-        a = jnp.where((ri == k) | (ci == k), 0.0, a) - col * row
-    return -a
-
-
-def residual_coeffs(x, h, shift):
-    tx = nn(x, h)
-    gram = nt(tx, x)
-    moved = shift(x)
-    zt = nn(nt(moved, tx), spd_inverse(gram))
-    return nn(zt, x) - moved
-
-
-def ritz_rows(basis, h, cutoff, shift, wanted):
-    tb = nn(basis, h)
-    moved = shift(basis)
-    gram = nt(tb, basis)
-    sym = 0.5 * (nt(tb, moved) + nt(moved, tb))
-    n = gram.shape[0]
-    eye = (lax.broadcasted_iota(jnp.int32, (n, n), 0)
-           == lax.broadcasted_iota(jnp.int32, (n, n), 1)).astype(F32)
-    s = (cutoff - 1.0) * eye + nn(sym, spd_inverse(gram))
+
+    def step(k, carry):
+        a = ref[...]
+        col = jnp.sum(jnp.where(ci == k, a, 0.0), axis=1, keepdims=True)
+        row = jnp.sum(jnp.where(ri == k, a, 0.0), axis=0, keepdims=True)
+        pivot = jnp.sum(jnp.where(ci[:1] == k, row, 0.0), axis=1, keepdims=True)
+        col = jnp.where(ri[:, :1] == k, -1.0, col)
+        row = jnp.where(ci[:1] == k, -1.0, row) / pivot
+        ref[...] = jnp.where((ri == k) | (ci == k), 0.0, a) - col * row
+        return carry
+
+    lax.fori_loop(0, n, step, 0)
+    ref[...] = -ref[...]
+
+
+def square_sum(a):
+    return jnp.sum(a * a)
+
+
+def spd_inverses(mats, refs):
+    scaled, lefts, rights, errs, sums = [], [], [], [], []
+    for a in mats:
+        eye = eye_mask(a.shape[0])
+        diag = jnp.where(eye, a, 0.0)
+        left = lax.rsqrt(jnp.sum(diag, axis=1, keepdims=True))
+        right = lax.rsqrt(jnp.sum(diag, axis=0, keepdims=True))
+        a = a * left * right
+        rows = jnp.sum(jnp.abs(a), axis=0, keepdims=True)
+        inv = 1.0 / jnp.max(rows, axis=1, keepdims=True)
+        unit = eye.astype(F32)
+        err = unit - a * inv
+        scaled.append(a)
+        lefts.append(left)
+        rights.append(right)
+        errs.append(err)
+        sums.append((unit + err) * inv)
+
+    def levels(errs, sums, count):
+        for _ in range(count):
+            errs = [nn(e, e) for e in errs]
+            sums = [s + nn(s, e) for s, e in zip(sums, errs)]
+        for (err_ref, sum_ref), e, s in zip(refs, errs, sums):
+            err_ref[...] = e
+            sum_ref[...] = s
+        return sum(square_sum(e) for e in errs)
+
+    def body(state):
+        level, _ = state
+        size = levels([r[0][...] for r in refs], [r[1][...] for r in refs], 2)
+        return level + 1, size
+
+    size = levels(errs, sums, 4)
+    _, size = lax.while_loop(lambda s: (s[1] > 1e-16) & (s[0] < 12), body, (jnp.int32(0), size))
+    good = size <= 1e-16
+
+    @pl.when(good)
+    def _():
+        for a, (_, sum_ref) in zip(scaled, refs):
+            s = sum_ref[...]
+            sum_ref[...] = 2.0 * s - nn(s, nn(a, s))
+
+    @pl.when(jnp.logical_not(good))
+    def _():
+        for a, (_, sum_ref) in zip(scaled, refs):
+            sum_ref[...] = a
+            sweep_inverse(sum_ref)
+
+    return [left * r[1][...] * right for left, right, r in zip(lefts, rights, refs)]
+
+
+def sign_rows(sym, inverse, cutoff, wanted):
+    eye = eye_mask(sym.shape[0]).astype(F32)
+    s = (cutoff - 1.0) * eye + nn(sym, inverse)
     s2 = nn(s, s)
     total = jnp.sum(jnp.sum(s2 * eye, axis=1, keepdims=True), axis=0, keepdims=True)
     scale = lax.rsqrt(total + 1e-06)
@@ -121,28 +171,37 @@
     return 0.5 * (eye + s)[:wanted]
 
 
-def small_math(h, cutoff, wanted, shift):
+def small_math(h, cutoff, wanted, shift, refs):
     width = h.shape[0]
     ri = lax.broadcasted_iota(jnp.int32, (wanted, width), 0)
     ci = lax.broadcasted_iota(jnp.int32, (wanted, width), 1)
     x = (ri == ci).astype(F32)
     p = (ri + wanted == ci).astype(F32)
     for _ in range(ITERS):
-        r = residual_coeffs(x, h, shift)
-        basis = jnp.concatenate([x, r, p], 0)
-        rows = ritz_rows(basis, h, cutoff, shift, wanted)
-        keep = lax.broadcasted_iota(jnp.int32, rows.shape, 1) >= wanted
-        both = nn(jnp.concatenate([rows, jnp.where(keep, rows, 0.0)], 0), basis)
-        x, p = both[:wanted], both[wanted:]
-    r = residual_coeffs(x, h, shift)
+        basis = jnp.concatenate([x, shift(x), p], 0)
+        tb = nn(basis, h)
+        moved = shift(basis)
+        gram = nt(tb, basis)
+        sym = 0.5 * (nt(tb, moved) + nt(moved, tb))
+        inverse, inverse_x = spd_inverses([gram, gram[:wanted, :wanted]], refs)
+        zt = nn(gram[wanted:2 * wanted, :wanted], inverse_x)
+        rows = sign_rows(sym, inverse, cutoff, wanted)
+        searched = nn(rows[:, wanted:2 * wanted], zt)
+        x, p = nn(rows, basis), nn(jnp.concatenate([-searched, rows[:, wanted:]], 1), basis)
+    tx = nn(x, h)
+    moved = shift(x)
+    (inverse_x,) = spd_inverses([nt(tx, x)], refs[1:])
+    zt = nn(nt(moved, tx), inverse_x)
+    r = nn(zt, x) - moved
     return jnp.concatenate([x, p, r, p - shift(p)], 0)
 
 
-def small_kernel(wanted, cut_ref, g_ref, out_ref):
+def small_kernel(wanted, cut_ref, g_ref, out_ref, e96, s96, e32, s32):
     pieces, cols = g_ref.shape
     width = out_ref.shape[1]
     h = jnp.concatenate([g_ref[...], jnp.zeros((width - pieces, cols), F32)], 0)
-    out_ref[...] = small_math(h, cut_ref[0], wanted, lambda v: pltpu.roll(v, 2 * wanted, 1))
+    out_ref[...] = small_math(h, cut_ref[0], wanted, lambda v: pltpu.roll(v, 2 * wanted, 1),
+                              [(e96, s96), (e32, s32)])
 
 
 def small(cutoff, gram, wanted):
@@ -151,7 +210,8 @@
         out_shape=jax.ShapeDtypeStruct((4 * wanted, gram.shape[1]), F32),
         in_specs=[pl.BlockSpec(memory_space=pltpu.SMEM), pl.BlockSpec(memory_space=pltpu.VMEM)],
         out_specs=pl.BlockSpec(memory_space=pltpu.VMEM),
-        compiler_params=pltpu.CompilerParams(vmem_limit_bytes=32 * 2**20),
+        scratch_shapes=[pltpu.VMEM((n, n), F32) for n in (3 * wanted, 3 * wanted, wanted, wanted)],
+        compiler_params=pltpu.CompilerParams(vmem_limit_bytes=16 * 2**20),
         name="small_matrices",
     )(cutoff, gram)
 

time: 193 us -> 174 us (0.902)
  Pallas kernels: 42.4 us -> 30.6 us
  local copies, waits for them, and re-layouts: 5.79 us -> 1.28 us
  starting transfers between devices: 51.4 us -> 49.4 us
    pallas_call x1, Pallas kernels: 34.4 us -> 20 us  [small(): pl.pallas_call(functools.partial(small_kernel, wanted), out_shape=jax.Sha...]
    unnamed x15 -> x9, local copies, waits for them, and re-layouts: 5.02 us -> 0.51 us
    pallas_call x3, Pallas kernels: 8.01 us -> 10.5 us  [graph_partial(): pl.pallas_call(functools.partial(graph_kernel, n_slots), out_shape=jax.Sh...]
    ppermute x9, waiting for transfers between devices: 10.6 us -> 8.19 us  [gather_brow(): lax.ppermute(v, 'brow', z_turn(k))]
    all_to_all x2, starting transfers between devices: 9.67 us -> 7.48 us  [apply_graph(): got = lax.all_to_all(part, 'bcol', 0, 0)]
    ppermute x3, starting transfers between devices: 7.47 us -> 9.56 us  [gather_brow(): return (near, lax.ppermute(near, 'brow', CORE))]
    all_to_all x2, waiting for transfers between devices: 33.2 us -> 35.1 us  [apply_graph(): got = lax.all_to_all(part, 'bcol', 0, 0)]
  transfers between devices with their start and end apart: 25 -> 25, of which waited for: 21 -> 20; matrix products, arithmetic and copies ran while one was open for 1% -> 1% of each run, Pallas kernels for 0% -> 0%
where the time goes in v2:
time: 174 us
  waiting for transfers between devices  57.3 us (33%)
  starting transfers between devices  49.4 us (28%)
  Pallas kernels  30.6 us (18%)
  blocking collectives  28.2 us (16%)
  other arithmetic  3.51 us (2%)
  between operations  2.23 us (1%)
    all_to_all x2, waiting for transfers between devices, apply_graph(): got = lax.all_to_all(part, 'bcol', 0, 0)  35.1 us
    all_to_all x1, blocking collectives, apply_graph(): got = lax.all_to_all(part, 'bcol', 0, 0)  28.2 us
    pallas_call x1, Pallas kernels, small(): pl.pallas_call(functools.partial(small_kernel, wanted), out_shape=jax.Sha...  20 us
    ppermute x9, starting transfers between devices, gather_brow(): lax.ppermute(v, 'brow', z_turn(k))  15.7 us
    pallas_call x3, Pallas kernels, graph_partial(): pl.pallas_call(functools.partial(graph_kernel, n_slots), out_shape=jax.Sh...  10.5 us
    ppermute x9, waiting for transfers between devices, sum_all(): a, b, c = [lax.ppermute(v, axis, turn(k)) for k in (1, 2, 3)]  10.4 us
    ppermute x9, starting transfers between devices, sum_all(): a, b, c = [lax.ppermute(v, axis, turn(k)) for k in (1, 2, 3)]  9.9 us
    ppermute x3, starting transfers between devices, gather_brow(): return (near, lax.ppermute(near, 'brow', CORE))  9.56 us
  transfers between devices with their start and end apart: 25, of which 20 were waited for; matrix products, arithmetic and copies ran while one was open for 1% of the time, Pallas kernels for 0%

profile of v2, /device:TPU:1, one launch (start us, length us, event | category | flops | bytes accessed | tf_op | source)
XLA Modules:
  0.0 174.1 jit_solution(9308954373516167277)
XLA Ops:
  1.6 4.7 %collective-permute-start.2 = (bf16[64,768]{1,0:T(8,128)(2,1)S(1)}, bf16[64,768]{1,0:T(8,128)(2,1)S(1)}, u32[]{:S(2)}, u32[]{:S(2)}) collective-permute-start(bf16[64,768]{1,0:T(8,128)(2,1)S(1)} %fusion.3), channel_id=1, source_target_pairs={{0,96},{16,112},{32,0},{48,16},{64,32},{80,48},{96,64},{112,80},{1... | collective-permute-start | bytes 294920 | tf_op jit(solution)/shard_map/ppermute | solution.py:235
  8.5 3.6 %collective-permute-done = bf16[64,768]{1,0:T(8,128)(2,1)S(1)} collective-permute-done((bf16[64,768]{1,0:T(8,128)(2,1)S(1)}, bf16[64,768]{1,0:T(8,128)(2,1)S(1)}, u32[]{:S(2)}, u32[]{:S(2)}) %collective-permute-start) | collective-permute-done | bytes 98336 | tf_op jit(solution)/shard_map/ppermute | solution.py:235
  12.6 2.3 %collective-permute-start.3 = (bf16[4,64,768]{2,1,0:T(8,128)(2,1)S(1)}, bf16[4,64,768]{2,1,0:T(8,128)(2,1)S(1)}, u32[]{:S(2)}, u32[]{:S(2)}) collective-permute-start(bf16[4,64,768]{2,1,0:T(8,128)(2,1)S(1)} %pad_maximum_fusion.6.near_ref), channel_id=1, source_target_pairs={{0,16},{16,0},{32,48},{48,32},{64,80},{80,64},{96,112},{112,96},{1... | collective-permute-start | bytes 1179656 | tf_op jit(solution)/shard_map/ppermute | solution.py:236
  16.3 2.9 %graph_partial.3 = bf16[16,64,768]{2,1,0:T(8,128)(2,1)S(1)} custom-call(s32[1]{0:T(128)} %bitcast.42.live_ref, s32[40]{0:T(128)S(1)} %get-tuple-element.14.rows_ref, s32[40]{0:T(128)S(1)} %get-tuple-element.15.cols_ref, bf16[4,64,768]{2,1,0:T(8,128)(2,1)S(1)} %pad_maximum_fusion.6.near_ref, bf16[4,64,768]{2,1,0:T(8,128)(2,1)S(1)} %collective-permute-done.3.far_ref, ...), custom_call_target="tpu_custom_call" | custom-call | tf_op jit(solution)/shard_map/graph_partial/pallas_call | solution.py:64
  19.2 28.2 %all_to_all.15 = bf16[16,64,768]{2,1,0:T(8,128)(2,1)S(1)} all-to-all(bf16[16,64,768]{2,1,0:T(8,128)(2,1)S(1)} %graph_partial.3), channel_id=1, replica_groups=mesh['brow'=8,'bcol'=16] {'bcol'}, dimensions={0} | all-to-all | bytes 3145728 | tf_op jit(solution)/shard_map/all_to_all | solution.py:270
  48.2 3.2 %collective-permute-start.5 = (bf16[64,768]{1,0:T(8,128)(2,1)S(1)}, bf16[64,768]{1,0:T(8,128)(2,1)S(1)}, u32[]{:S(2)}, u32[]{:S(2)}) collective-permute-start(bf16[64,768]{1,0:T(8,128)(2,1)S(1)} %get-tuple-element.6), channel_id=1, source_target_pairs={{0,64},{16,80},{32,96},{48,112},{64,0},{80,16},{96,32},{112,48},{1... | collective-permute-start | bytes 294920 | tf_op jit(solution)/shard_map/ppermute | solution.py:235
  52.9 1.6 collective-permute-done.5
  55.2 3.6 %collective-permute-start.7 = (bf16[4,64,768]{2,1,0:T(8,128)(2,1)S(1)}, bf16[4,64,768]{2,1,0:T(8,128)(2,1)S(1)}, u32[]{:S(2)}, u32[]{:S(2)}) collective-permute-start(bf16[4,64,768]{2,1,0:T(8,128)(2,1)S(1)} %pad_maximum_fusion.7.near_ref), channel_id=1, source_target_pairs={{0,16},{16,0},{32,48},{48,32},{64,80},{80,64},{96,112},{112,96},{1... | collective-permute-start | bytes 1179656 | tf_op jit(solution)/shard_map/ppermute | solution.py:236
  60.2 4.0 %graph_partial.4 = bf16[16,64,768]{2,1,0:T(8,128)(2,1)} custom-call(s32[1]{0:T(128)} %bitcast.43.live_ref, s32[40]{0:T(128)S(1)} %get-tuple-element.14.rows_ref, s32[40]{0:T(128)S(1)} %get-tuple-element.15.cols_ref, bf16[4,64,768]{2,1,0:T(8,128)(2,1)S(1)} %pad_maximum_fusion.7.near_ref, bf16[4,64,768]{2,1,0:T(8,128)(2,1)S(1)} %collective-permute-done.7.far_ref, ...), custom_call_target="tpu_custom_call" | custom-call | tf_op jit(solution)/shard_map/graph_partial/pallas_call | solution.py:64
  64.2 3.9 %all-to-all-start.1 = ((bf16[16,64,768]{2,1,0:T(8,128)(2,1)}), bf16[16,64,768]{2,1,0:T(8,128)(2,1)S(1)}, u32[]{:S(2)}, u32[]{:S(2)}) async-start(bf16[16,64,768]{2,1,0:T(8,128)(2,1)} %graph_partial.4), calls=%async_computation.1 | async-start | bytes 3145728 | tf_op jit(solution)/shard_map/all_to_all | solution.py:270
  68.2 22.4 %all-to-all-done.1 = bf16[16,64,768]{2,1,0:T(8,128)(2,1)S(1)} async-done(((bf16[16,64,768]{2,1,0:T(8,128)(2,1)}), bf16[16,64,768]{2,1,0:T(8,128)(2,1)S(1)}, u32[]{:S(2)}, u32[]{:S(2)}) %all-to-all-start.1) | async-done | bytes 1572896 | tf_op jit(solution)/shard_map/all_to_all | solution.py:270
  91.0 3.5 %collective-permute-start.9 = (bf16[32,768]{1,0:T(8,128)(2,1)S(1)}, bf16[32,768]{1,0:T(8,128)(2,1)S(1)}, u32[]{:S(2)}, u32[]{:S(2)}) collective-permute-start(bf16[32,768]{1,0:T(8,128)(2,1)S(1)} %fusion.6), channel_id=1, source_target_pairs={{0,64},{16,80},{32,96},{48,112},{64,0},{80,16},{96,32},{112,48},{1... | collective-permute-start | bytes 147464 | tf_op jit(solution)/shard_map/ppermute | solution.py:235
  97.8 3.7 %collective-permute-start.11 = (bf16[4,32,768]{2,1,0:T(8,128)(2,1)S(1)}, bf16[4,32,768]{2,1,0:T(8,128)(2,1)S(1)}, u32[]{:S(2)}, u32[]{:S(2)}) collective-permute-start(bf16[4,32,768]{2,1,0:T(8,128)(2,1)S(1)} %pad_maximum_fusion.8.near_ref), channel_id=1, source_target_pairs={{0,16},{16,0},{32,48},{48,32},{64,80},{80,64},{96,112},{112,96},{1... | collective-permute-start | bytes 589832 | tf_op jit(solution)/shard_map/ppermute | solution.py:236
  102.5 3.6 %graph_partial.5 = bf16[16,32,768]{2,1,0:T(8,128)(2,1)} custom-call(s32[1]{0:T(128)} %bitcast.44.live_ref, s32[40]{0:T(128)S(1)} %get-tuple-element.14.rows_ref, s32[40]{0:T(128)S(1)} %get-tuple-element.15.cols_ref, bf16[4,32,768]{2,1,0:T(8,128)(2,1)S(1)} %pad_maximum_fusion.8.near_ref, bf16[4,32,768]{2,1,0:T(8,128)(2,1)S(1)} %collective-permute-done.11.far_ref, ...), custom_call_target="tpu_custom_call" | custom-call | tf_op jit(solution)/shard_map/graph_partial/pallas_call | solution.py:64
  106.2 3.6 %all-to-all-start.2 = ((bf16[16,32,768]{2,1,0:T(8,128)(2,1)}), bf16[16,32,768]{2,1,0:T(8,128)(2,1)S(1)}, u32[]{:S(2)}, u32[]{:S(2)}) async-start(bf16[16,32,768]{2,1,0:T(8,128)(2,1)} %graph_partial.5), calls=%async_computation.2 | async-start | bytes 1572864 | tf_op jit(solution)/shard_map/all_to_all | solution.py:270
  109.8 12.7 %all-to-all-done.2 = bf16[16,32,768]{2,1,0:T(8,128)(2,1)S(1)} async-done(((bf16[16,32,768]{2,1,0:T(8,128)(2,1)}), bf16[16,32,768]{2,1,0:T(8,128)(2,1)S(1)}, u32[]{:S(2)}, u32[]{:S(2)}) %all-to-all-start.2) | async-done | bytes 786464 | tf_op jit(solution)/shard_map/all_to_all | solution.py:270
  123.6 2.7 %collective-permute-start.12 = (f32[80,256]{1,0:T(8,128)S(1)}, f32[80,256]{1,0:T(8,128)S(1)}, u32[]{:S(2)}, u32[]{:S(2)}) collective-permute-start(f32[80,256]{1,0:T(8,128)S(1)} %constant_dynamic-slice_fusion), channel_id=1, source_target_pairs={{0,16},{16,0},{32,48},{48,32},{64,80},{80,64},{96,112},{112,96},{1... | collective-permute-start | bytes 245768 | tf_op jit(solution)/shard_map/ppermute | solution.py:244
  127.5 3.9 %collective-permute-start.14 = (f32[80,256]{1,0:T(8,128)S(1)}, f32[80,256]{1,0:T(8,128)S(1)}, u32[]{:S(2)}, u32[]{:S(2)}) collective-permute-start(f32[80,256]{1,0:T(8,128)S(1)} %dynamic-slice_add_fusion), channel_id=1, source_target_pairs={{0,64},{16,80},{32,96},{48,112},{64,0},{80,16},{96,32},{112,48},{1... | collective-permute-start | bytes 245768 | tf_op jit(solution)/shard_map/ppermute | solution.py:246
  132.5 2.8 %collective-permute-done.14 = f32[80,256]{1,0:T(8,128)S(1)} collective-permute-done((f32[80,256]{1,0:T(8,128)S(1)}, f32[80,256]{1,0:T(8,128)S(1)}, u32[]{:S(2)}, u32[]{:S(2)}) %collective-permute-start.14) | collective-permute-done | bytes 81952 | tf_op jit(solution)/shard_map/ppermute | solution.py:246
  138.2 2.0 %collective-permute-done.16 = f32[80,256]{1,0:T(8,128)S(1)} collective-permute-done((f32[80,256]{1,0:T(8,128)S(1)}, f32[80,256]{1,0:T(8,128)S(1)}, u32[]{:S(2)}, u32[]{:S(2)}) %collective-permute-start.16) | collective-permute-done | bytes 81952 | tf_op jit(solution)/shard_map/ppermute | solution.py:246
  141.8 1.8 %collective-permute-start.20 = (f32[80,256]{1,0:T(8,128)S(1)}, f32[80,256]{1,0:T(8,128)S(1)}, u32[]{:S(2)}, u32[]{:S(2)}) collective-permute-start(f32[80,256]{1,0:T(8,128)S(1)} %add_add_fusion.1), channel_id=1, source_target_pairs={{0,8},{1,9},{2,10},{3,11},{4,12},{5,13},{6,14},{7,15},{8,0},{9,1},... | collective-permute-start | bytes 245768 | tf_op jit(solution)/shard_map/ppermute | solution.py:246
  144.5 2.6 %collective-permute-done.19 = f32[80,256]{1,0:T(8,128)S(1)} collective-permute-done((f32[80,256]{1,0:T(8,128)S(1)}, f32[80,256]{1,0:T(8,128)S(1)}, u32[]{:S(2)}, u32[]{:S(2)}) %collective-permute-start.19) | collective-permute-done | bytes 81952 | tf_op jit(solution)/shard_map/ppermute | solution.py:246
  147.7 4.0 %collective-permute-start.22 = (f32[80,256]{1,0:T(8,128)S(1)}, f32[80,256]{1,0:T(8,128)S(1)}, u32[]{:S(2)}, u32[]{:S(2)}) collective-permute-start(f32[80,256]{1,0:T(8,128)S(1)} %add_add_fusion), channel_id=1, source_target_pairs={{0,16},{16,0},{32,48},{48,32},{64,80},{80,64},{96,112},{112,96},{1... | collective-permute-start | bytes 245768 | tf_op jit(solution)/shard_map/ppermute | solution.py:248
  152.7 20.0 %small_matrices.1 = f32[128,256]{1,0:T(8,128)S(1)} custom-call(f32[1]{0:T(128)S(6)} %copy.18.cut_ref, f32[160,256]{1,0:T(8,128)S(1)} %pad_maximum_fusion.9.g_ref), custom_call_target="tpu_custom_call" | custom-call | tf_op jit(solution)/shard_map/small_matrices/pallas_call | solution.py:208
  (66 shorter events, 24.3 us)
Async XLA Ops:
  1.6 6.9 %collective-permute-start.2 = (bf16[64,768]{1,0:T(8,128)(2,1)S(1)}, bf16[64,768]{1,0:T(8,128)(2,1)S(1)}, u32[]{:S(2)}, u32[]{:S(2)}) collective-permute-start(bf16[64,768]{1,0:T(8,128)(2,1)S(1)} %fusion.3), channel_id=1, source_target_pairs={{0,96},{16,112},{32,0},{48,16},{64,32},{80,48},{96,64},{112,80},{1... | collective-permute-start | bytes 294920 | tf_op jit(solution)/shard_map/ppermute | solution.py:235
  6.2 5.9 %collective-permute-start = (bf16[64,768]{1,0:T(8,128)(2,1)S(1)}, bf16[64,768]{1,0:T(8,128)(2,1)S(1)}, u32[]{:S(2)}, u32[]{:S(2)}) collective-permute-start(bf16[64,768]{1,0:T(8,128)(2,1)S(1)} %fusion.3), channel_id=1, source_target_pairs={{0,32},{16,48},{32,64},{48,80},{64,96},{80,112},{96,0},{112,16},{1... | collective-permute-start | bytes 294920 | tf_op jit(solution)/shard_map/ppermute | solution.py:235
  6.3 6.3 %collective-permute-start.1 = (bf16[64,768]{1,0:T(8,128)(2,1)S(1)}, bf16[64,768]{1,0:T(8,128)(2,1)S(1)}, u32[]{:S(2)}, u32[]{:S(2)}) collective-permute-start(bf16[64,768]{1,0:T(8,128)(2,1)S(1)} %fusion.3), channel_id=1, source_target_pairs={{0,64},{16,80},{32,96},{48,112},{64,0},{80,16},{96,32},{112,48},{1... | collective-permute-start | bytes 294920 | tf_op jit(solution)/shard_map/ppermute | solution.py:235
  12.6 3.7 %collective-permute-start.3 = (bf16[4,64,768]{2,1,0:T(8,128)(2,1)S(1)}, bf16[4,64,768]{2,1,0:T(8,128)(2,1)S(1)}, u32[]{:S(2)}, u32[]{:S(2)}) collective-permute-start(bf16[4,64,768]{2,1,0:T(8,128)(2,1)S(1)} %pad_maximum_fusion.6.near_ref), channel_id=1, source_target_pairs={{0,16},{16,0},{32,48},{48,32},{64,80},{80,64},{96,112},{112,96},{1... | collective-permute-start | bytes 1179656 | tf_op jit(solution)/shard_map/ppermute | solution.py:236
  48.1 4.7 %collective-permute-start.4 = (bf16[64,768]{1,0:T(8,128)(2,1)S(1)}, bf16[64,768]{1,0:T(8,128)(2,1)S(1)}, u32[]{:S(2)}, u32[]{:S(2)}) collective-permute-start(bf16[64,768]{1,0:T(8,128)(2,1)S(1)} %get-tuple-element.6), channel_id=1, source_target_pairs={{0,32},{16,48},{32,64},{48,80},{64,96},{80,112},{96,0},{112,16},{1... | collective-permute-start | bytes 294920 | tf_op jit(solution)/shard_map/ppermute | solution.py:235
  48.2 6.3 %collective-permute-start.5 = (bf16[64,768]{1,0:T(8,128)(2,1)S(1)}, bf16[64,768]{1,0:T(8,128)(2,1)S(1)}, u32[]{:S(2)}, u32[]{:S(2)}) collective-permute-start(bf16[64,768]{1,0:T(8,128)(2,1)S(1)} %get-tuple-element.6), channel_id=1, source_target_pairs={{0,64},{16,80},{32,96},{48,112},{64,0},{80,16},{96,32},{112,48},{1... | collective-permute-start | bytes 294920 | tf_op jit(solution)/shard_map/ppermute | solution.py:235
  51.4 3.8 %collective-permute-start.6 = (bf16[64,768]{1,0:T(8,128)(2,1)S(1)}, bf16[64,768]{1,0:T(8,128)(2,1)S(1)}, u32[]{:S(2)}, u32[]{:S(2)}) collective-permute-start(bf16[64,768]{1,0:T(8,128)(2,1)S(1)} %get-tuple-element.6), channel_id=1, source_target_pairs={{0,96},{16,112},{32,0},{48,16},{64,32},{80,48},{96,64},{112,80},{1... | collective-permute-start | bytes 294920 | tf_op jit(solution)/shard_map/ppermute | solution.py:235
  55.2 4.9 %collective-permute-start.7 = (bf16[4,64,768]{2,1,0:T(8,128)(2,1)S(1)}, bf16[4,64,768]{2,1,0:T(8,128)(2,1)S(1)}, u32[]{:S(2)}, u32[]{:S(2)}) collective-permute-start(bf16[4,64,768]{2,1,0:T(8,128)(2,1)S(1)} %pad_maximum_fusion.7.near_ref), channel_id=1, source_target_pairs={{0,16},{16,0},{32,48},{48,32},{64,80},{80,64},{96,112},{112,96},{1... | collective-permute-start | bytes 1179656 | tf_op jit(solution)/shard_map/ppermute | solution.py:236
  64.2 26.4 %all-to-all-start.1 = ((bf16[16,64,768]{2,1,0:T(8,128)(2,1)}), bf16[16,64,768]{2,1,0:T(8,128)(2,1)S(1)}, u32[]{:S(2)}, u32[]{:S(2)}) async-start(bf16[16,64,768]{2,1,0:T(8,128)(2,1)} %graph_partial.4), calls=%async_computation.1 | async-start | bytes 3145728 | tf_op jit(solution)/shard_map/all_to_all | solution.py:270
  90.9 5.1 %collective-permute-start.8 = (bf16[32,768]{1,0:T(8,128)(2,1)S(1)}, bf16[32,768]{1,0:T(8,128)(2,1)S(1)}, u32[]{:S(2)}, u32[]{:S(2)}) collective-permute-start(bf16[32,768]{1,0:T(8,128)(2,1)S(1)} %fusion.6), channel_id=1, source_target_pairs={{0,32},{16,48},{32,64},{48,80},{64,96},{80,112},{96,0},{112,16},{1... | collective-permute-start | bytes 147464 | tf_op jit(solution)/shard_map/ppermute | solution.py:235
  91.0 5.5 %collective-permute-start.9 = (bf16[32,768]{1,0:T(8,128)(2,1)S(1)}, bf16[32,768]{1,0:T(8,128)(2,1)S(1)}, u32[]{:S(2)}, u32[]{:S(2)}) collective-permute-start(bf16[32,768]{1,0:T(8,128)(2,1)S(1)} %fusion.6), channel_id=1, source_target_pairs={{0,64},{16,80},{32,96},{48,112},{64,0},{80,16},{96,32},{112,48},{1... | collective-permute-start | bytes 147464 | tf_op jit(solution)/shard_map/ppermute | solution.py:235
  97.8 4.8 %collective-permute-start.11 = (bf16[4,32,768]{2,1,0:T(8,128)(2,1)S(1)}, bf16[4,32,768]{2,1,0:T(8,128)(2,1)S(1)}, u32[]{:S(2)}, u32[]{:S(2)}) collective-permute-start(bf16[4,32,768]{2,1,0:T(8,128)(2,1)S(1)} %pad_maximum_fusion.8.near_ref), channel_id=1, source_target_pairs={{0,16},{16,0},{32,48},{48,32},{64,80},{80,64},{96,112},{112,96},{1... | collective-permute-start | bytes 589832 | tf_op jit(solution)/shard_map/ppermute | solution.py:236
  106.2 16.3 %all-to-all-start.2 = ((bf16[16,32,768]{2,1,0:T(8,128)(2,1)}), bf16[16,32,768]{2,1,0:T(8,128)(2,1)S(1)}, u32[]{:S(2)}, u32[]{:S(2)}) async-start(bf16[16,32,768]{2,1,0:T(8,128)(2,1)} %graph_partial.5), calls=%async_computation.2 | async-start | bytes 1572864 | tf_op jit(solution)/shard_map/all_to_all | solution.py:270
  123.6 3.7 %collective-permute-start.12 = (f32[80,256]{1,0:T(8,128)S(1)}, f32[80,256]{1,0:T(8,128)S(1)}, u32[]{:S(2)}, u32[]{:S(2)}) collective-permute-start(f32[80,256]{1,0:T(8,128)S(1)} %constant_dynamic-slice_fusion), channel_id=1, source_target_pairs={{0,16},{16,0},{32,48},{48,32},{64,80},{80,64},{96,112},{112,96},{1... | collective-permute-start | bytes 245768 | tf_op jit(solution)/shard_map/ppermute | solution.py:244
  127.3 5.1 %collective-permute-start.13 = (f32[80,256]{1,0:T(8,128)S(1)}, f32[80,256]{1,0:T(8,128)S(1)}, u32[]{:S(2)}, u32[]{:S(2)}) collective-permute-start(f32[80,256]{1,0:T(8,128)S(1)} %dynamic-slice_add_fusion), channel_id=1, source_target_pairs={{0,32},{16,48},{32,64},{48,80},{64,96},{80,112},{96,0},{112,16},{1... | collective-permute-start | bytes 245768 | tf_op jit(solution)/shard_map/ppermute | solution.py:246
  127.5 7.8 %collective-permute-start.14 = (f32[80,256]{1,0:T(8,128)S(1)}, f32[80,256]{1,0:T(8,128)S(1)}, u32[]{:S(2)}, u32[]{:S(2)}) collective-permute-start(f32[80,256]{1,0:T(8,128)S(1)} %dynamic-slice_add_fusion), channel_id=1, source_target_pairs={{0,64},{16,80},{32,96},{48,112},{64,0},{80,16},{96,32},{112,48},{1... | collective-permute-start | bytes 245768 | tf_op jit(solution)/shard_map/ppermute | solution.py:246
  131.3 4.0 %collective-permute-start.15 = (f32[80,256]{1,0:T(8,128)S(1)}, f32[80,256]{1,0:T(8,128)S(1)}, u32[]{:S(2)}, u32[]{:S(2)}) collective-permute-start(f32[80,256]{1,0:T(8,128)S(1)} %dynamic-slice_add_fusion), channel_id=1, source_target_pairs={{0,96},{16,112},{32,0},{48,16},{64,32},{80,48},{96,64},{112,80},{1... | collective-permute-start | bytes 245768 | tf_op jit(solution)/shard_map/ppermute | solution.py:246
  135.3 4.9 %collective-permute-start.16 = (f32[80,256]{1,0:T(8,128)S(1)}, f32[80,256]{1,0:T(8,128)S(1)}, u32[]{:S(2)}, u32[]{:S(2)}) collective-permute-start(f32[80,256]{1,0:T(8,128)S(1)} %add_add_fusion.2), channel_id=1, source_target_pairs={{0,1},{1,2},{2,3},{3,0},{4,5},{5,6},{6,7},{7,4},{8,9},{9,10},{10,1... | collective-permute-start | bytes 245768 | tf_op jit(solution)/shard_map/ppermute | solution.py:246
  135.7 5.6 %collective-permute-start.17 = (f32[80,256]{1,0:T(8,128)S(1)}, f32[80,256]{1,0:T(8,128)S(1)}, u32[]{:S(2)}, u32[]{:S(2)}) collective-permute-start(f32[80,256]{1,0:T(8,128)S(1)} %add_add_fusion.2), channel_id=1, source_target_pairs={{0,2},{1,3},{2,0},{3,1},{4,6},{5,7},{6,4},{7,5},{8,10},{9,11},{10,... | collective-permute-start | bytes 245768 | tf_op jit(solution)/shard_map/ppermute | solution.py:246
  136.6 5.0 %collective-permute-start.18 = (f32[80,256]{1,0:T(8,128)S(1)}, f32[80,256]{1,0:T(8,128)S(1)}, u32[]{:S(2)}, u32[]{:S(2)}) collective-permute-start(f32[80,256]{1,0:T(8,128)S(1)} %add_add_fusion.2), channel_id=1, source_target_pairs={{0,3},{1,0},{2,1},{3,2},{4,7},{5,4},{6,5},{7,6},{8,11},{9,8},{10,9... | collective-permute-start | bytes 245768 | tf_op jit(solution)/shard_map/ppermute | solution.py:246
  141.7 5.4 %collective-permute-start.19 = (f32[80,256]{1,0:T(8,128)S(1)}, f32[80,256]{1,0:T(8,128)S(1)}, u32[]{:S(2)}, u32[]{:S(2)}) collective-permute-start(f32[80,256]{1,0:T(8,128)S(1)} %add_add_fusion.1), channel_id=1, source_target_pairs={{0,4},{1,5},{2,6},{3,7},{4,8},{5,9},{6,10},{7,11},{8,12},{9,13},{1... | collective-permute-start | bytes 245768 | tf_op jit(solution)/shard_map/ppermute | solution.py:246
  141.8 5.4 %collective-permute-start.20 = (f32[80,256]{1,0:T(8,128)S(1)}, f32[80,256]{1,0:T(8,128)S(1)}, u32[]{:S(2)}, u32[]{:S(2)}) collective-permute-start(f32[80,256]{1,0:T(8,128)S(1)} %add_add_fusion.1), channel_id=1, source_target_pairs={{0,8},{1,9},{2,10},{3,11},{4,12},{5,13},{6,14},{7,15},{8,0},{9,1},... | collective-permute-start | bytes 245768 | tf_op jit(solution)/shard_map/ppermute | solution.py:246
  143.5 4.2 %collective-permute-start.21 = (f32[80,256]{1,0:T(8,128)S(1)}, f32[80,256]{1,0:T(8,128)S(1)}, u32[]{:S(2)}, u32[]{:S(2)}) collective-permute-start(f32[80,256]{1,0:T(8,128)S(1)} %add_add_fusion.1), channel_id=1, source_target_pairs={{0,12},{1,13},{2,14},{3,15},{4,0},{5,1},{6,2},{7,3},{8,4},{9,5},{1... | collective-permute-start | bytes 245768 | tf_op jit(solution)/shard_map/ppermute | solution.py:246
  147.7 5.0 %collective-permute-start.22 = (f32[80,256]{1,0:T(8,128)S(1)}, f32[80,256]{1,0:T(8,128)S(1)}, u32[]{:S(2)}, u32[]{:S(2)}) collective-permute-start(f32[80,256]{1,0:T(8,128)S(1)} %add_add_fusion), channel_id=1, source_target_pairs={{0,16},{16,0},{32,48},{48,32},{64,80},{80,64},{96,112},{112,96},{1... | collective-permute-start | bytes 245768 | tf_op jit(solution)/shard_map/ppermute | solution.py:248
  (4 other events, 11.7 us)

commit v3 on v2

v3 whole, which is shorter than its diff:
```python
import functools

import jax
import jax.numpy as jnp
from jax import lax
from jax.experimental import pallas as pl
from jax.experimental.pallas import tpu as pltpu
from jax.sharding import PartitionSpec as P

ITERS = 2
NS_STEPS = 8
CHUNK = 8
HIGH = lax.Precision.HIGHEST
BF = jnp.bfloat16
F32 = jnp.float32
SMEM = pl.BlockSpec(memory_space=pltpu.SMEM)
VMEM = pl.BlockSpec(memory_space=pltpu.VMEM)


def nn(a, b):
    return lax.dot_general(a, b, (((1,), (0,)), ((), ())), precision=HIGH, preferred_element_type=F32)


def nt(a, b):
    return lax.dot_general(a, b, (((1,), (1,)), ((), ())), precision=HIGH, preferred_element_type=F32)


def graph_kernel(place_ref, rows_ref, cols_ref, near_ref, far_ref, blocks_ref, out_ref, panel, acc, *own):
    live, brow = place_ref[0], place_ref[1]
    n_slots = blocks_ref.shape[0]
    sub = panel.shape[0] // 8
    chunks = n_slots // CHUNK
    held = own[0] if own else blocks_ref

    def fetch(c):
        part = pl.ds(c * CHUNK, CHUNK)
        return pltpu.make_async_copy(blocks_ref.at[part], held.at[part], own[1].at[c])

    for c in range(chunks if own else 0):
        @pl.when(c * CHUNK < live)
        def _():
            fetch(c).start()

    for s in range(8):
        src = near_ref if s < 4 else far_ref
        for q in range(sub):
            panel[s * sub + q] = src[s % 4, :, q * 256:(q + 1) * 256]
    acc[...] = jnp.zeros_like(acc)

    def spot(slot):
        source = lax.div(cols_ref[slot], sub)
        turn = jnp.bitwise_and(lax.div(brow, 2) - lax.div(source, 2), 3)
        side = jnp.bitwise_and(brow - source, 1)
        return (turn + 4 * side) * sub + lax.rem(cols_ref[slot], sub)

    for c in range(chunks):
        @pl.when(c * CHUNK < live)
        def _():
            if own:
                fetch(c).wait()
            slots = range(c * CHUNK, (c + 1) * CHUNK)
            prods = [lax.dot_general(panel[spot(s)], held[s], (((1,), (1,)), ((), ())),
                                     preferred_element_type=F32) for s in slots]
            for s, prod in zip(slots, prods):
                row = jnp.where(s < live, rows_ref[s], acc.shape[0] - 1)
                acc[row] = acc[row] + prod
    for j in range(out_ref.shape[0]):
        for q in range(sub):
            out_ref[j, :, q * 256:(q + 1) * 256] = acc[j * sub + q].astype(BF)


def graph_partial(place, rows, cols, near, far, blocks, owners, fetched):
    n_slots, side, _ = blocks.shape
    r, width = near.shape[1:]
    sub = width // side
    own = [pltpu.VMEM((n_slots, side, side), BF), pltpu.SemaphoreType.DMA((n_slots // CHUNK,))]
    return pl.pallas_call(
        graph_kernel,
        out_shape=jax.ShapeDtypeStruct((owners, r, width), BF),
        in_specs=[SMEM] * 3 + [VMEM] * 2 + [pl.BlockSpec(memory_space=pltpu.HBM) if fetched else VMEM],
        out_specs=VMEM,
        scratch_shapes=[
            pltpu.VMEM((8 * sub, r, side), BF),
            pltpu.VMEM((owners * sub + 1, r, side), F32),
        ] + (own if fetched else []),
        compiler_params=pltpu.CompilerParams(vmem_limit_bytes=(50 if fetched else 14) * 2**20),
        name="graph_partial",
    )(place, rows, cols, near, far, blocks)


def halves(a):
    top = a.astype(BF)
    return top, (a - top.astype(F32)).astype(BF)


def three(a, b):
    ah, al = halves(a)
    bh, bl = halves(b)

    def dot(u, v):
        return lax.dot_general(u, v, (((1,), (0,)), ((), ())), preferred_element_type=F32)

    return dot(ah, bh) + (dot(ah, bl) + dot(al, bh))


def eye_mask(n):
    return (lax.broadcasted_iota(jnp.int32, (n, n), 0) == lax.broadcasted_iota(jnp.int32, (n, n), 1))


def sweep_inverse(ref):
    n = ref.shape[0]
    ri = lax.broadcasted_iota(jnp.int32, (n, n), 0)
    ci = lax.broadcasted_iota(jnp.int32, (n, n), 1)

    def step(k, carry):
        a = ref[...]
        col = jnp.sum(jnp.where(ci == k, a, 0.0), axis=1, keepdims=True)
        row = jnp.sum(jnp.where(ri == k, a, 0.0), axis=0, keepdims=True)
        pivot = jnp.sum(jnp.where(ci[:1] == k, row, 0.0), axis=1, keepdims=True)
        col = jnp.where(ri[:, :1] == k, -1.0, col)
        row = jnp.where(ci[:1] == k, -1.0, row) / pivot
        ref[...] = jnp.where((ri == k) | (ci == k), 0.0, a) - col * row
        return carry

    lax.fori_loop(0, n, step, 0)
    ref[...] = -ref[...]


def square_sum(a):
    return jnp.sum(a * a)


def spd_inverses(mats, refs):
    scaled, lefts, rights, errs, sums = [], [], [], [], []
    for a in mats:
        eye = eye_mask(a.shape[0])
        diag = jnp.where(eye, a, 0.0)
        left = lax.rsqrt(jnp.sum(diag, axis=1, keepdims=True))
        right = lax.rsqrt(jnp.sum(diag, axis=0, keepdims=True))
        a = a * left * right
        rows = jnp.sum(jnp.abs(a), axis=0, keepdims=True)
        inv = 1.0 / jnp.max(rows, axis=1, keepdims=True)
        unit = eye.astype(F32)
        err = unit - a * inv
        scaled.append(a)
        lefts.append(left)
        rights.append(right)
        errs.append(err)
        sums.append((unit + err) * inv)

    def levels(errs, sums, count):
        for _ in range(count):
            errs = [nn(e, e) for e in errs]
            sums = [s + nn(s, e) for s, e in zip(sums, errs)]
        for (err_ref, sum_ref), e, s in zip(refs, errs, sums):
            err_ref[...] = e
            sum_ref[...] = s
        return sum(square_sum(e) for e in errs)

    def body(state):
        level, _ = state
        size = levels([r[0][...] for r in refs], [r[1][...] for r in refs], 2)
        return level + 1, size

    size = levels(errs, sums, 4)
    _, size = lax.while_loop(lambda s: (s[1] > 1e-8) & (s[0] < 12), body, (jnp.int32(0), size))
    good = size <= 1e-8

    @pl.when(jnp.logical_not(good))
    def _():
        for a, (_, sum_ref) in zip(scaled, refs):
            sum_ref[...] = a
            sweep_inverse(sum_ref)

    return [left * r[1][...] * right for left, right, r in zip(lefts, rights, refs)]


def sign_rows(sym, inverse, cutoff, wanted):
    eye = eye_mask(sym.shape[0]).astype(F32)
    s = (cutoff - 1.0) * eye + nn(sym, inverse)
    s2 = nn(s, s)
    total = jnp.sum(jnp.sum(s2 * eye, axis=1, keepdims=True), axis=0, keepdims=True)
    scale = lax.rsqrt(total + 1e-06)
    s = s * scale
    s2 = s2 * (scale * scale)
    s = 1.5 * s - 0.5 * three(s, s2)
    for _ in range(NS_STEPS - 1):
        s = 1.5 * s - 0.5 * three(s, three(s, s))
    return 0.5 * (eye + s)[:wanted]


def shift(v, wanted):
    return pltpu.roll(v, 2 * wanted, 1)


def fill_gram(packed, full, w):
    full[...] = jnp.zeros_like(full)

    def put(i, j, block):
        full[i * w:(i + 1) * w, j * w:(j + 1) * w] = block
        if i != j:
            full[j * w:(j + 1) * w, i * w:(i + 1) * w] = block.T

    for row, i in enumerate((0, 4, 5, 6)):
        for j in range(4):
            put(i, j, packed[row * w:(row + 1) * w, j * w:(j + 1) * w])
    for row, spots in ((4, ((1, 1), (1, 2), (1, 3), (4, 4))), (5, ((2, 2), (2, 3), (3, 3), (5, 4)))):
        for place, (i, j) in enumerate(spots):
            put(i, j, packed[row * w:(row + 1) * w, place * w:(place + 1) * w])
    q = w // 4
    put(6, 4, jnp.concatenate([packed[6 * w:6 * w + q, n * w:(n + 1) * w] for n in range(4)], 0))


def next_block(rows, basis, gram, inverse_x, w):
    zt = nn(gram[2 * w:, :w], inverse_x)
    x = nn(rows, basis)
    return x, x - nn(rows[:, :w] + nn(rows[:, 2 * w:], zt), basis[:w])


def small_kernel(w, cut_ref, core_ref, mine_ref, other_ref, *rest):
    parts, outs, (full, e96, s96, e32, s32) = rest[:7], rest[7:11], rest[11:]
    refs = [(e96, s96), (e32, s32)]
    mine, other = mine_ref[...], other_ref[...]
    first = core_ref[0] == 0
    fill_gram(jnp.concatenate([jnp.where(first, mine, other), jnp.where(first, other, mine)], 0), full, w)
    width = full.shape[0]
    gram = full[:3 * w, :3 * w]
    sym = 0.5 * (full[:3 * w, 2 * w:5 * w] + full[2 * w:5 * w, :3 * w])
    basis = (lax.broadcasted_iota(jnp.int32, (3 * w, width), 0)
             == lax.broadcasted_iota(jnp.int32, (3 * w, width), 1)).astype(F32)
    for _ in range(ITERS - 1):
        inverse, inverse_x = spd_inverses([gram, gram[:w, :w]], refs)
        rows = sign_rows(sym, inverse, cut_ref[0], w)
        x, p = next_block(rows, basis, gram, inverse_x, w)
        basis = jnp.concatenate([x, p, shift(x, w)], 0)
        tb = nn(basis, full[...])
        moved = shift(basis, w)
        gram = nt(tb, basis)
        sym = 0.5 * (nt(tb, moved) + nt(moved, tb))
    inverse, inverse_x = spd_inverses([gram, gram[:w, :w]], refs)
    rows = sign_rows(sym, inverse, cut_ref[0], w)
    x, p = next_block(rows, basis, gram, inverse_x, w)
    tx = nn(rows, tb)
    moved = shift(x, w)
    (inverse_x,) = spd_inverses([nt(tx, x)], refs[1:])
    zt = nn(nt(moved, tx), inverse_x)
    coeffs = jnp.concatenate([x, p, nn(zt, x) - moved, p - shift(p, w)], 0)
    krylov = jnp.concatenate([r[...] for r in parts] + [jnp.zeros_like(parts[0])], 0)
    found = nn(coeffs, krylov)
    for n, out_ref in enumerate(outs):
        out_ref[...] = found[n * w:(n + 1) * w]


def small(cutoff, core, mine, other, parts):
    w = parts[0].shape[0]
    return pl.pallas_call(
        functools.partial(small_kernel, w),
        out_shape=[jax.ShapeDtypeStruct(parts[0].shape, F32)] * 4,
        in_specs=[SMEM, SMEM] + [VMEM] * 9,
        out_specs=[VMEM] * 4,
        scratch_shapes=[pltpu.VMEM((n, n), F32) for n in (8 * w, 3 * w, 3 * w, w, w)],
        compiler_params=pltpu.CompilerParams(vmem_limit_bytes=16 * 2**20),
        name="small_matrices",
    )(cutoff, core, mine, other, *parts)


def gram_kernel(*refs):
    k = [r[...] for r in refs[:-1]]
    out_ref = refs[-1]
    w = k[0].shape[0]
    out_ref[:4 * w] = nt(jnp.concatenate([k[0], k[4], k[5], k[6]], 0), jnp.concatenate(k[:4], 0))
    inner = jnp.concatenate(k[1:4], 0)
    inner = nt(inner, inner)
    outer = nt(jnp.concatenate(k[4:], 0), k[4])
    out_ref[4 * w:5 * w] = jnp.concatenate([inner[:w], outer[:w]], 1)
    out_ref[5 * w:6 * w] = jnp.concatenate([inner[w:2 * w, w:], inner[2 * w:, 2 * w:], outer[w:2 * w]], 1)
    q = w // 4
    last = outer[2 * w:]
    out_ref[6 * w:6 * w + q] = jnp.concatenate([last[n * q:(n + 1) * q] for n in range(4)], 1)
    out_ref[6 * w + q:] = jnp.zeros_like(out_ref[6 * w + q:])


def packed_gram(blocks):
    w = blocks[0].shape[0]
    return pl.pallas_call(
        gram_kernel,
        out_shape=jax.ShapeDtypeStruct((6 * w + w // 2, 4 * w), F32),
        in_specs=[VMEM] * len(blocks),
        out_specs=VMEM,
        compiler_params=pltpu.CompilerParams(vmem_limit_bytes=16 * 2**20),
        name="packed_gram",
    )(*blocks)


def z_turn(k):
    return [(i, (i + 2 * k) % 8) for i in range(8)]


def y_turn(k):
    return [(i, (i // 4) * 4 + (i + k) % 4) for i in range(16)]


def x_turn(k):
    return [(i, (i + 4 * k) % 16) for i in range(16)]


CORE = [(i, i ^ 1) for i in range(8)]


def gather_brow(v):
    near = jnp.stack([v] + [lax.ppermute(v, "brow", z_turn(k)) for k in (1, 2, 3)])
    return near, lax.ppermute(near, "brow", CORE)


def sum_all(g):
    half = g.shape[0] // 2
    me = lax.axis_index("brow") % 2
    mine = lax.dynamic_slice_in_dim(g, me * half, half, 0)
    other = lax.dynamic_slice_in_dim(g, (1 - me) * half, half, 0)
    v = mine + lax.ppermute(other, "brow", CORE)
    for axis, turn in (("brow", z_turn), ("bcol", y_turn), ("bcol", x_turn)):
        a, b, c = [lax.ppermute(v, axis, turn(k)) for k in (1, 2, 3)]
        v = (v + a) + (b + c)
    return v, lax.ppermute(v, "brow", CORE)


def local(blocks, pattern_rows, pattern_cols, live_count, degree_scale, eigen_block, direction, cutoff):
    block_set = blocks[0, 0]
    wanted = eigen_block.shape[0]
    owners = lax.axis_size("bcol")
    brow = lax.axis_index("brow")
    place = jnp.stack([live_count[0, 0], brow])
    rows, cols = pattern_rows[0, 0], pattern_cols[0, 0]

    def apply_graph(v, fetched=False):
        near, far = gather_brow((degree_scale * v).astype(BF))
        part = graph_partial(place, rows, cols, near, far, block_set, owners, fetched)
        got = lax.all_to_all(part, "bcol", 0, 0)
        return degree_scale * jnp.sum(got.astype(F32), axis=0)

    k1 = apply_graph(jnp.concatenate([eigen_block, direction], 0), True)
    k2 = apply_graph(k1)
    k3 = apply_graph(k2[:wanted])
    parts = [eigen_block, direction, k1[:wanted], k1[wanted:], k2[:wanted], k2[wanted:], k3]
    mine, other = sum_all(packed_gram(parts))
    return tuple(small(cutoff, (brow % 2).reshape(1), mine, other, parts))


def solution(mesh):
    docs = P(None, ("brow", "bcol"))
    return jax.shard_map(
        local,
        mesh=mesh,
        in_specs=(
            P("brow", "bcol", None, None, None),
            P("brow", "bcol", None),
            P("brow", "bcol", None),
            P("brow", "bcol"),
            P(("brow", "bcol")),
            docs,
            docs,
            P(),
        ),
        out_specs=(docs, docs, docs, docs),
        check_vma=False,
    )
```

time: 174 us -> 167 us (0.960)
  blocking collectives: 28.2 us -> 51.7 us
  waiting for transfers between devices: 57.3 us -> 34.1 us
  starting transfers between devices: 49.4 us -> 43.9 us
  Pallas kernels: 30.6 us -> 28.8 us
    all_to_all x1 -> x2, blocking collectives: 28.2 us -> 51.7 us  [apply_graph(): got = lax.all_to_all(part, 'bcol', 0, 0)]
    all_to_all x2 -> x1, waiting for transfers between devices: 35.1 us -> 14.9 us  [apply_graph(): got = lax.all_to_all(part, 'bcol', 0, 0)]
    all_to_all x2 -> x1, starting transfers between devices: 7.48 us -> 3.74 us  [apply_graph(): got = lax.all_to_all(part, 'bcol', 0, 0)]
    ppermute x9, waiting for transfers between devices: 8.19 us -> 6.32 us  [gather_brow(): lax.ppermute(v, 'brow', z_turn(k))]
    ppermute x1, starting transfers between devices: 2.74 us -> 0.89 us  [sum_all(): v = mine + lax.ppermute(other, 'brow', CORE)]
    pallas_call x4 -> x5, Pallas kernels: 30.6 us -> 28.8 us  [the longest x1 17.9 us: small(): pl.pallas_call(functools.partial(small_kernel, w), out_shape=[jax.ShapeDt...]
  transfers between devices with their start and end apart: 25 -> 24, of which waited for: 20 -> 19; matrix products, arithmetic and copies ran while one was open for 1% -> 1% of each run, Pallas kernels for 0% -> 0%
where the time goes in v3:
time: 167 us; the launch traced here: 166 us
  blocking collectives  51.7 us (31%)
  starting transfers between devices  43.9 us (26%)
  waiting for transfers between devices  34.1 us (20%)
  Pallas kernels  28.8 us (17%)
  other arithmetic  2.82 us (2%)
  local copies, waits for them, and re-layouts  2.14 us (1%)
  between operations  2.13 us (1%)
    all_to_all x2, blocking collectives, apply_graph(): got = lax.all_to_all(part, 'bcol', 0, 0)  51.7 us
    pallas_call x1, Pallas kernels, small(): pl.pallas_call(functools.partial(small_kernel, w), out_shape=[jax.ShapeDt...  17.9 us
    ppermute x9, starting transfers between devices, gather_brow(): lax.ppermute(v, 'brow', z_turn(k))  16.2 us
    all_to_all x1, waiting for transfers between devices, apply_graph(): got = lax.all_to_all(part, 'bcol', 0, 0)  14.9 us
    pallas_call x3, Pallas kernels, graph_partial(): pl.pallas_call(graph_kernel, out_shape=jax.ShapeDtypeStruct((owners, r, w...  9.84 us
    ppermute x3, starting transfers between devices, gather_brow(): return (near, lax.ppermute(near, 'brow', CORE))  9.66 us
    ppermute x9, starting transfers between devices, sum_all(): a, b, c = [lax.ppermute(v, axis, turn(k)) for k in (1, 2, 3)]  8.95 us
    ppermute x9, waiting for transfers between devices, sum_all(): a, b, c = [lax.ppermute(v, axis, turn(k)) for k in (1, 2, 3)]  8.75 us
  transfers between devices with their start and end apart: 24, of which 19 were waited for; matrix products, arithmetic and copies ran while one was open for 1% of the time, Pallas kernels for 0%

profile of v3, /device:TPU:1, one launch (start us, length us, event | category | flops | bytes accessed | tf_op | source)
XLA Modules:
  0.0 165.6 jit_solution(11331546654048324414)
XLA Ops:
  1.6 2.5 %collective-permute-start = (bf16[64,768]{1,0:T(8,128)(2,1)S(1)}, bf16[64,768]{1,0:T(8,128)(2,1)S(1)}, u32[]{:S(2)}, u32[]{:S(2)}) collective-permute-start(bf16[64,768]{1,0:T(8,128)(2,1)S(1)} %fusion.1), channel_id=1, source_target_pairs={{0,32},{16,48},{32,64},{48,80},{64,96},{80,112},{96,0},{112,16},{1... | collective-permute-start | bytes 294920 | tf_op jit(solution)/shard_map/ppermute | solution.py:311
  4.1 3.3 %collective-permute-start.1 = (bf16[64,768]{1,0:T(8,128)(2,1)S(1)}, bf16[64,768]{1,0:T(8,128)(2,1)S(1)}, u32[]{:S(2)}, u32[]{:S(2)}) collective-permute-start(bf16[64,768]{1,0:T(8,128)(2,1)S(1)} %fusion.1), channel_id=1, source_target_pairs={{0,64},{16,80},{32,96},{48,112},{64,0},{80,16},{96,32},{112,48},{1... | collective-permute-start | bytes 294920 | tf_op jit(solution)/shard_map/ppermute | solution.py:311
  9.1 2.3 %collective-permute-done.1 = bf16[64,768]{1,0:T(8,128)(2,1)S(1)} collective-permute-done((bf16[64,768]{1,0:T(8,128)(2,1)S(1)}, bf16[64,768]{1,0:T(8,128)(2,1)S(1)}, u32[]{:S(2)}, u32[]{:S(2)}) %collective-permute-start.1) | collective-permute-done | bytes 98336 | tf_op jit(solution)/shard_map/ppermute | solution.py:311
  11.5 1.9 %collective-permute-start.3 = (bf16[4,64,768]{2,1,0:T(8,128)(2,1)S(1)}, bf16[4,64,768]{2,1,0:T(8,128)(2,1)S(1)}, u32[]{:S(2)}, u32[]{:S(2)}) collective-permute-start(bf16[4,64,768]{2,1,0:T(8,128)(2,1)S(1)} %pad_maximum_fusion.near_ref), channel_id=1, source_target_pairs={{0,16},{16,0},{32,48},{48,32},{64,80},{80,64},{96,112},{112,96},{1... | collective-permute-start | bytes 1179656 | tf_op jit(solution)/shard_map/ppermute | solution.py:312
  16.4 3.8 %graph_partial.3 = bf16[16,64,768]{2,1,0:T(8,128)(2,1)S(1)} custom-call(s32[2]{0:T(128)S(1)} %pad_add_fusion.place_ref, s32[40]{0:T(128)S(1)} %bitcast.32, s32[40]{0:T(128)S(1)} %bitcast.35, bf16[4,64,768]{2,1,0:T(8,128)(2,1)S(1)} %pad_maximum_fusion.near_ref, bf16[4,64,768]{2,1,0:T(8,128)(2,1)S(1)} %collective-permute-done.3.far_ref, ...), custom_call_target="tpu_custom_call" | custom-call | tf_op jit(solution)/shard_map/graph_partial/pallas_call | solution.py:77
  20.2 27.5 %all_to_all.15 = bf16[16,64,768]{2,1,0:T(8,128)(2,1)S(1)} all-to-all(bf16[16,64,768]{2,1,0:T(8,128)(2,1)S(1)} %graph_partial.3), channel_id=1, replica_groups=mesh['brow'=8,'bcol'=16] {'bcol'}, dimensions={0} | all-to-all | bytes 3145728 | tf_op jit(solution)/shard_map/all_to_all | solution.py:338
  48.5 2.5 %collective-permute-start.5 = (bf16[64,768]{1,0:T(8,128)(2,1)S(1)}, bf16[64,768]{1,0:T(8,128)(2,1)S(1)}, u32[]{:S(2)}, u32[]{:S(2)}) collective-permute-start(bf16[64,768]{1,0:T(8,128)(2,1)S(1)} %get-tuple-element.4), channel_id=1, source_target_pairs={{0,64},{16,80},{32,96},{48,112},{64,0},{80,16},{96,32},{112,48},{1... | collective-permute-start | bytes 294920 | tf_op jit(solution)/shard_map/ppermute | solution.py:311
  51.0 2.0 %collective-permute-start.6 = (bf16[64,768]{1,0:T(8,128)(2,1)S(1)}, bf16[64,768]{1,0:T(8,128)(2,1)S(1)}, u32[]{:S(2)}, u32[]{:S(2)}) collective-permute-start(bf16[64,768]{1,0:T(8,128)(2,1)S(1)} %get-tuple-element.4), channel_id=1, source_target_pairs={{0,96},{16,112},{32,0},{48,16},{64,32},{80,48},{96,64},{112,80},{1... | collective-permute-start | bytes 294920 | tf_op jit(solution)/shard_map/ppermute | solution.py:311
  54.9 3.9 %collective-permute-start.7 = (bf16[4,64,768]{2,1,0:T(8,128)(2,1)S(1)}, bf16[4,64,768]{2,1,0:T(8,128)(2,1)S(1)}, u32[]{:S(2)}, u32[]{:S(2)}) collective-permute-start(bf16[4,64,768]{2,1,0:T(8,128)(2,1)S(1)} %pad_maximum_fusion.1.near_ref), channel_id=1, source_target_pairs={{0,16},{16,0},{32,48},{48,32},{64,80},{80,64},{96,112},{112,96},{1... | collective-permute-start | bytes 1179656 | tf_op jit(solution)/shard_map/ppermute | solution.py:312
  60.1 2.7 %graph_partial.4 = bf16[16,64,768]{2,1,0:T(8,128)(2,1)S(1)} custom-call(s32[2]{0:T(128)S(1)} %pad_add_fusion.place_ref, s32[40]{0:T(128)S(1)} %bitcast.33, s32[40]{0:T(128)S(1)} %bitcast.36, bf16[4,64,768]{2,1,0:T(8,128)(2,1)S(1)} %pad_maximum_fusion.1.near_ref, bf16[4,64,768]{2,1,0:T(8,128)(2,1)S(1)} %collective-permute-done.7.far_ref, ...), custom_call_target="tpu_custom_call" | custom-call | tf_op jit(solution)/shard_map/graph_partial/pallas_call | solution.py:77
  62.9 24.2 %all_to_all.16 = bf16[16,64,768]{2,1,0:T(8,128)(2,1)S(1)} all-to-all(bf16[16,64,768]{2,1,0:T(8,128)(2,1)S(1)} %graph_partial.4), channel_id=1, replica_groups=mesh['brow'=8,'bcol'=16] {'bcol'}, dimensions={0} | all-to-all | bytes 3145728 | tf_op jit(solution)/shard_map/all_to_all | solution.py:338
  87.3 1.8 %collective-permute-start.8 = (bf16[32,768]{1,0:T(8,128)(2,1)S(1)}, bf16[32,768]{1,0:T(8,128)(2,1)S(1)}, u32[]{:S(2)}, u32[]{:S(2)}) collective-permute-start(bf16[32,768]{1,0:T(8,128)(2,1)S(1)} %get-tuple-element.6), channel_id=1, source_target_pairs={{0,32},{16,48},{32,64},{48,80},{64,96},{80,112},{96,0},{112,16},{1... | collective-permute-start | bytes 147464 | tf_op jit(solution)/shard_map/ppermute | solution.py:311
  89.1 2.4 %collective-permute-start.9 = (bf16[32,768]{1,0:T(8,128)(2,1)S(1)}, bf16[32,768]{1,0:T(8,128)(2,1)S(1)}, u32[]{:S(2)}, u32[]{:S(2)}) collective-permute-start(bf16[32,768]{1,0:T(8,128)(2,1)S(1)} %get-tuple-element.6), channel_id=1, source_target_pairs={{0,64},{16,80},{32,96},{48,112},{64,0},{80,16},{96,32},{112,48},{1... | collective-permute-start | bytes 147464 | tf_op jit(solution)/shard_map/ppermute | solution.py:311
  94.6 3.8 %collective-permute-start.11 = (bf16[4,32,768]{2,1,0:T(8,128)(2,1)S(1)}, bf16[4,32,768]{2,1,0:T(8,128)(2,1)S(1)}, u32[]{:S(2)}, u32[]{:S(2)}) collective-permute-start(bf16[4,32,768]{2,1,0:T(8,128)(2,1)S(1)} %pad_maximum_fusion.2.near_ref), channel_id=1, source_target_pairs={{0,16},{16,0},{32,48},{48,32},{64,80},{80,64},{96,112},{112,96},{1... | collective-permute-start | bytes 589832 | tf_op jit(solution)/shard_map/ppermute | solution.py:312
  99.5 3.3 %graph_partial.5 = bf16[16,32,768]{2,1,0:T(8,128)(2,1)} custom-call(s32[2]{0:T(128)S(1)} %pad_add_fusion.place_ref, s32[40]{0:T(128)S(1)} %bitcast.34, s32[40]{0:T(128)S(1)} %bitcast.37, bf16[4,32,768]{2,1,0:T(8,128)(2,1)S(1)} %pad_maximum_fusion.2.near_ref, bf16[4,32,768]{2,1,0:T(8,128)(2,1)S(1)} %collective-permute-done.11.far_ref, ...), custom_call_target="tpu_custom_call" | custom-call | tf_op jit(solution)/shard_map/graph_partial/pallas_call | solution.py:77
  102.9 3.7 %all-to-all-start.2 = ((bf16[16,32,768]{2,1,0:T(8,128)(2,1)}), bf16[16,32,768]{2,1,0:T(8,128)(2,1)S(1)}, u32[]{:S(2)}, u32[]{:S(2)}) async-start(bf16[16,32,768]{2,1,0:T(8,128)(2,1)} %graph_partial.5), calls=%async_computation.2 | async-start | bytes 1572864 | tf_op jit(solution)/shard_map/all_to_all | solution.py:338
  106.7 14.9 %all-to-all-done.2 = bf16[16,32,768]{2,1,0:T(8,128)(2,1)S(1)} async-done(((bf16[16,32,768]{2,1,0:T(8,128)(2,1)}), bf16[16,32,768]{2,1,0:T(8,128)(2,1)S(1)}, u32[]{:S(2)}, u32[]{:S(2)}) %all-to-all-start.2) | async-done | bytes 786464 | tf_op jit(solution)/shard_map/all_to_all | solution.py:338
  124.8 3.1 %collective-permute-start.14 = (f32[104,128]{1,0:T(8,128)S(1)}, f32[104,128]{1,0:T(8,128)S(1)}, u32[]{:S(2)}, u32[]{:S(2)}) collective-permute-start(f32[104,128]{1,0:T(8,128)S(1)} %dynamic-slice_add_fusion), channel_id=1, source_target_pairs={{0,64},{16,80},{32,96},{48,112},{64,0},{80,16},{96,32},{112,48},{1... | collective-permute-start | bytes 159752 | tf_op jit(solution)/shard_map/ppermute | solution.py:322
  132.6 1.7 %collective-permute-start.18 = (f32[104,128]{1,0:T(8,128)S(1)}, f32[104,128]{1,0:T(8,128)S(1)}, u32[]{:S(2)}, u32[]{:S(2)}) collective-permute-start(f32[104,128]{1,0:T(8,128)S(1)} %add_add_fusion.2), channel_id=1, source_target_pairs={{0,3},{1,0},{2,1},{3,2},{4,7},{5,4},{6,5},{7,6},{8,11},{9,8},{10,9... | collective-permute-start | bytes 159752 | tf_op jit(solution)/shard_map/ppermute | solution.py:322
  134.3 1.4 collective-permute-done.16
  136.9 1.8 %collective-permute-start.20 = (f32[104,128]{1,0:T(8,128)S(1)}, f32[104,128]{1,0:T(8,128)S(1)}, u32[]{:S(2)}, u32[]{:S(2)}) collective-permute-start(f32[104,128]{1,0:T(8,128)S(1)} %add_add_fusion.1), channel_id=1, source_target_pairs={{0,8},{1,9},{2,10},{3,11},{4,12},{5,13},{6,14},{7,15},{8,0},{9,1},... | collective-permute-start | bytes 159752 | tf_op jit(solution)/shard_map/ppermute | solution.py:322
  139.6 2.1 %collective-permute-done.19 = f32[104,128]{1,0:T(8,128)S(1)} collective-permute-done((f32[104,128]{1,0:T(8,128)S(1)}, f32[104,128]{1,0:T(8,128)S(1)}, u32[]{:S(2)}, u32[]{:S(2)}) %collective-permute-start.19) | collective-permute-done | bytes 53280 | tf_op jit(solution)/shard_map/ppermute | solution.py:322
  142.3 4.5 %collective-permute-start.22 = (f32[104,128]{1,0:T(8,128)S(1)}, f32[104,128]{1,0:T(8,128)S(1)}, u32[]{:S(2)}, u32[]{:S(2)}) collective-permute-start(f32[104,128]{1,0:T(8,128)S(1)} %add_add_fusion.mine_ref), channel_id=1, source_target_pairs={{0,16},{16,0},{32,48},{48,32},{64,80},{80,64},{96,112},{112,96},{1... | collective-permute-start | bytes 159752 | tf_op jit(solution)/shard_map/ppermute | solution.py:324
  147.6 17.9 %small_matrices.1 = (f32[32,768]{1,0:T(8,128)}, f32[32,768]{1,0:T(8,128)}, f32[32,768]{1,0:T(8,128)}, f32[32,768]{1,0:T(8,128)}) custom-call(f32[1]{0:T(128)S(6)} %copy.13.cut_ref, s32[1]{0:T(128)} %bitcast.core_ref, f32[104,128]{1,0:T(8,128)S(1)} %add_add_fusion.mine_ref, f32[104,128]{1,0:T(8,128)S(1)} %collective-permute-done.22.other_ref, ...), custom_call_target="tpu_custom_call" | custom-call | tf_op jit(solution)/shard_map/small_matrices/pallas_call | solution.py:256
  (66 shorter events, 24.4 us)
Async XLA Ops:
  1.6 7.5 %collective-permute-start = (bf16[64,768]{1,0:T(8,128)(2,1)S(1)}, bf16[64,768]{1,0:T(8,128)(2,1)S(1)}, u32[]{:S(2)}, u32[]{:S(2)}) collective-permute-start(bf16[64,768]{1,0:T(8,128)(2,1)S(1)} %fusion.1), channel_id=1, source_target_pairs={{0,32},{16,48},{32,64},{48,80},{64,96},{80,112},{96,0},{112,16},{1... | collective-permute-start | bytes 294920 | tf_op jit(solution)/shard_map/ppermute | solution.py:311
  4.1 7.3 %collective-permute-start.1 = (bf16[64,768]{1,0:T(8,128)(2,1)S(1)}, bf16[64,768]{1,0:T(8,128)(2,1)S(1)}, u32[]{:S(2)}, u32[]{:S(2)}) collective-permute-start(bf16[64,768]{1,0:T(8,128)(2,1)S(1)} %fusion.1), channel_id=1, source_target_pairs={{0,64},{16,80},{32,96},{48,112},{64,0},{80,16},{96,32},{112,48},{1... | collective-permute-start | bytes 294920 | tf_op jit(solution)/shard_map/ppermute | solution.py:311
  7.4 4.0 %collective-permute-start.2 = (bf16[64,768]{1,0:T(8,128)(2,1)S(1)}, bf16[64,768]{1,0:T(8,128)(2,1)S(1)}, u32[]{:S(2)}, u32[]{:S(2)}) collective-permute-start(bf16[64,768]{1,0:T(8,128)(2,1)S(1)} %fusion.1), channel_id=1, source_target_pairs={{0,96},{16,112},{32,0},{48,16},{64,32},{80,48},{96,64},{112,80},{1... | collective-permute-start | bytes 294920 | tf_op jit(solution)/shard_map/ppermute | solution.py:311
  11.5 3.3 %collective-permute-start.3 = (bf16[4,64,768]{2,1,0:T(8,128)(2,1)S(1)}, bf16[4,64,768]{2,1,0:T(8,128)(2,1)S(1)}, u32[]{:S(2)}, u32[]{:S(2)}) collective-permute-start(bf16[4,64,768]{2,1,0:T(8,128)(2,1)S(1)} %pad_maximum_fusion.near_ref), channel_id=1, source_target_pairs={{0,16},{16,0},{32,48},{48,32},{64,80},{80,64},{96,112},{112,96},{1... | collective-permute-start | bytes 1179656 | tf_op jit(solution)/shard_map/ppermute | solution.py:312
  48.4 5.8 %collective-permute-start.4 = (bf16[64,768]{1,0:T(8,128)(2,1)S(1)}, bf16[64,768]{1,0:T(8,128)(2,1)S(1)}, u32[]{:S(2)}, u32[]{:S(2)}) collective-permute-start(bf16[64,768]{1,0:T(8,128)(2,1)S(1)} %get-tuple-element.4), channel_id=1, source_target_pairs={{0,32},{16,48},{32,64},{48,80},{64,96},{80,112},{96,0},{112,16},{1... | collective-permute-start | bytes 294920 | tf_op jit(solution)/shard_map/ppermute | solution.py:311
  48.5 5.7 %collective-permute-start.5 = (bf16[64,768]{1,0:T(8,128)(2,1)S(1)}, bf16[64,768]{1,0:T(8,128)(2,1)S(1)}, u32[]{:S(2)}, u32[]{:S(2)}) collective-permute-start(bf16[64,768]{1,0:T(8,128)(2,1)S(1)} %get-tuple-element.4), channel_id=1, source_target_pairs={{0,64},{16,80},{32,96},{48,112},{64,0},{80,16},{96,32},{112,48},{1... | collective-permute-start | bytes 294920 | tf_op jit(solution)/shard_map/ppermute | solution.py:311
  51.0 3.8 %collective-permute-start.6 = (bf16[64,768]{1,0:T(8,128)(2,1)S(1)}, bf16[64,768]{1,0:T(8,128)(2,1)S(1)}, u32[]{:S(2)}, u32[]{:S(2)}) collective-permute-start(bf16[64,768]{1,0:T(8,128)(2,1)S(1)} %get-tuple-element.4), channel_id=1, source_target_pairs={{0,96},{16,112},{32,0},{48,16},{64,32},{80,48},{96,64},{112,80},{1... | collective-permute-start | bytes 294920 | tf_op jit(solution)/shard_map/ppermute | solution.py:311
  54.9 5.3 %collective-permute-start.7 = (bf16[4,64,768]{2,1,0:T(8,128)(2,1)S(1)}, bf16[4,64,768]{2,1,0:T(8,128)(2,1)S(1)}, u32[]{:S(2)}, u32[]{:S(2)}) collective-permute-start(bf16[4,64,768]{2,1,0:T(8,128)(2,1)S(1)} %pad_maximum_fusion.1.near_ref), channel_id=1, source_target_pairs={{0,16},{16,0},{32,48},{48,32},{64,80},{80,64},{96,112},{112,96},{1... | collective-permute-start | bytes 1179656 | tf_op jit(solution)/shard_map/ppermute | solution.py:312
  87.3 5.1 %collective-permute-start.8 = (bf16[32,768]{1,0:T(8,128)(2,1)S(1)}, bf16[32,768]{1,0:T(8,128)(2,1)S(1)}, u32[]{:S(2)}, u32[]{:S(2)}) collective-permute-start(bf16[32,768]{1,0:T(8,128)(2,1)S(1)} %get-tuple-element.6), channel_id=1, source_target_pairs={{0,32},{16,48},{32,64},{48,80},{64,96},{80,112},{96,0},{112,16},{1... | collective-permute-start | bytes 147464 | tf_op jit(solution)/shard_map/ppermute | solution.py:311
  89.1 4.4 %collective-permute-start.9 = (bf16[32,768]{1,0:T(8,128)(2,1)S(1)}, bf16[32,768]{1,0:T(8,128)(2,1)S(1)}, u32[]{:S(2)}, u32[]{:S(2)}) collective-permute-start(bf16[32,768]{1,0:T(8,128)(2,1)S(1)} %get-tuple-element.6), channel_id=1, source_target_pairs={{0,64},{16,80},{32,96},{48,112},{64,0},{80,16},{96,32},{112,48},{1... | collective-permute-start | bytes 147464 | tf_op jit(solution)/shard_map/ppermute | solution.py:311
  91.5 3.1 %collective-permute-start.10 = (bf16[32,768]{1,0:T(8,128)(2,1)S(1)}, bf16[32,768]{1,0:T(8,128)(2,1)S(1)}, u32[]{:S(2)}, u32[]{:S(2)}) collective-permute-start(bf16[32,768]{1,0:T(8,128)(2,1)S(1)} %get-tuple-element.6), channel_id=1, source_target_pairs={{0,96},{16,112},{32,0},{48,16},{64,32},{80,48},{96,64},{112,80},{1... | collective-permute-start | bytes 147464 | tf_op jit(solution)/shard_map/ppermute | solution.py:311
  94.6 4.9 %collective-permute-start.11 = (bf16[4,32,768]{2,1,0:T(8,128)(2,1)S(1)}, bf16[4,32,768]{2,1,0:T(8,128)(2,1)S(1)}, u32[]{:S(2)}, u32[]{:S(2)}) collective-permute-start(bf16[4,32,768]{2,1,0:T(8,128)(2,1)S(1)} %pad_maximum_fusion.2.near_ref), channel_id=1, source_target_pairs={{0,16},{16,0},{32,48},{48,32},{64,80},{80,64},{96,112},{112,96},{1... | collective-permute-start | bytes 589832 | tf_op jit(solution)/shard_map/ppermute | solution.py:312
  102.9 18.7 %all-to-all-start.2 = ((bf16[16,32,768]{2,1,0:T(8,128)(2,1)}), bf16[16,32,768]{2,1,0:T(8,128)(2,1)S(1)}, u32[]{:S(2)}, u32[]{:S(2)}) async-start(bf16[16,32,768]{2,1,0:T(8,128)(2,1)} %graph_partial.5), calls=%async_computation.2 | async-start | bytes 1572864 | tf_op jit(solution)/shard_map/all_to_all | solution.py:338
  122.7 1.8 %collective-permute-start.12 = (f32[104,128]{1,0:T(8,128)S(1)}, f32[104,128]{1,0:T(8,128)S(1)}, u32[]{:S(2)}, u32[]{:S(2)}) collective-permute-start(f32[104,128]{1,0:T(8,128)S(1)} %constant_dynamic-slice_fusion), channel_id=1, source_target_pairs={{0,16},{16,0},{32,48},{48,32},{64,80},{80,64},{96,112},{112,96},{1... | collective-permute-start | bytes 159752 | tf_op jit(solution)/shard_map/ppermute | solution.py:320
  124.5 4.4 %collective-permute-start.13 = (f32[104,128]{1,0:T(8,128)S(1)}, f32[104,128]{1,0:T(8,128)S(1)}, u32[]{:S(2)}, u32[]{:S(2)}) collective-permute-start(f32[104,128]{1,0:T(8,128)S(1)} %dynamic-slice_add_fusion), channel_id=1, source_target_pairs={{0,32},{16,48},{32,64},{48,80},{64,96},{80,112},{96,0},{112,16},{1... | collective-permute-start | bytes 159752 | tf_op jit(solution)/shard_map/ppermute | solution.py:322
  124.8 5.6 %collective-permute-start.14 = (f32[104,128]{1,0:T(8,128)S(1)}, f32[104,128]{1,0:T(8,128)S(1)}, u32[]{:S(2)}, u32[]{:S(2)}) collective-permute-start(f32[104,128]{1,0:T(8,128)S(1)} %dynamic-slice_add_fusion), channel_id=1, source_target_pairs={{0,64},{16,80},{32,96},{48,112},{64,0},{80,16},{96,32},{112,48},{1... | collective-permute-start | bytes 159752 | tf_op jit(solution)/shard_map/ppermute | solution.py:322
  127.9 3.5 %collective-permute-start.15 = (f32[104,128]{1,0:T(8,128)S(1)}, f32[104,128]{1,0:T(8,128)S(1)}, u32[]{:S(2)}, u32[]{:S(2)}) collective-permute-start(f32[104,128]{1,0:T(8,128)S(1)} %dynamic-slice_add_fusion), channel_id=1, source_target_pairs={{0,96},{16,112},{32,0},{48,16},{64,32},{80,48},{96,64},{112,80},{1... | collective-permute-start | bytes 159752 | tf_op jit(solution)/shard_map/ppermute | solution.py:322
  131.4 4.3 %collective-permute-start.16 = (f32[104,128]{1,0:T(8,128)S(1)}, f32[104,128]{1,0:T(8,128)S(1)}, u32[]{:S(2)}, u32[]{:S(2)}) collective-permute-start(f32[104,128]{1,0:T(8,128)S(1)} %add_add_fusion.2), channel_id=1, source_target_pairs={{0,1},{1,2},{2,3},{3,0},{4,5},{5,6},{6,7},{7,4},{8,9},{9,10},{10,1... | collective-permute-start | bytes 159752 | tf_op jit(solution)/shard_map/ppermute | solution.py:322
  131.8 5.0 %collective-permute-start.17 = (f32[104,128]{1,0:T(8,128)S(1)}, f32[104,128]{1,0:T(8,128)S(1)}, u32[]{:S(2)}, u32[]{:S(2)}) collective-permute-start(f32[104,128]{1,0:T(8,128)S(1)} %add_add_fusion.2), channel_id=1, source_target_pairs={{0,2},{1,3},{2,0},{3,1},{4,6},{5,7},{6,4},{7,5},{8,10},{9,11},{10,... | collective-permute-start | bytes 159752 | tf_op jit(solution)/shard_map/ppermute | solution.py:322
  132.6 4.3 %collective-permute-start.18 = (f32[104,128]{1,0:T(8,128)S(1)}, f32[104,128]{1,0:T(8,128)S(1)}, u32[]{:S(2)}, u32[]{:S(2)}) collective-permute-start(f32[104,128]{1,0:T(8,128)S(1)} %add_add_fusion.2), channel_id=1, source_target_pairs={{0,3},{1,0},{2,1},{3,2},{4,7},{5,4},{6,5},{7,6},{8,11},{9,8},{10,9... | collective-permute-start | bytes 159752 | tf_op jit(solution)/shard_map/ppermute | solution.py:322
  136.8 4.8 %collective-permute-start.19 = (f32[104,128]{1,0:T(8,128)S(1)}, f32[104,128]{1,0:T(8,128)S(1)}, u32[]{:S(2)}, u32[]{:S(2)}) collective-permute-start(f32[104,128]{1,0:T(8,128)S(1)} %add_add_fusion.1), channel_id=1, source_target_pairs={{0,4},{1,5},{2,6},{3,7},{4,8},{5,9},{6,10},{7,11},{8,12},{9,13},{1... | collective-permute-start | bytes 159752 | tf_op jit(solution)/shard_map/ppermute | solution.py:322
  136.9 4.8 %collective-permute-start.20 = (f32[104,128]{1,0:T(8,128)S(1)}, f32[104,128]{1,0:T(8,128)S(1)}, u32[]{:S(2)}, u32[]{:S(2)}) collective-permute-start(f32[104,128]{1,0:T(8,128)S(1)} %add_add_fusion.1), channel_id=1, source_target_pairs={{0,8},{1,9},{2,10},{3,11},{4,12},{5,13},{6,14},{7,15},{8,0},{9,1},... | collective-permute-start | bytes 159752 | tf_op jit(solution)/shard_map/ppermute | solution.py:322
  138.7 3.6 %collective-permute-start.21 = (f32[104,128]{1,0:T(8,128)S(1)}, f32[104,128]{1,0:T(8,128)S(1)}, u32[]{:S(2)}, u32[]{:S(2)}) collective-permute-start(f32[104,128]{1,0:T(8,128)S(1)} %add_add_fusion.1), channel_id=1, source_target_pairs={{0,12},{1,13},{2,14},{3,15},{4,0},{5,1},{6,2},{7,3},{8,4},{9,5},{1... | collective-permute-start | bytes 159752 | tf_op jit(solution)/shard_map/ppermute | solution.py:322
  142.3 5.3 %collective-permute-start.22 = (f32[104,128]{1,0:T(8,128)S(1)}, f32[104,128]{1,0:T(8,128)S(1)}, u32[]{:S(2)}, u32[]{:S(2)}) collective-permute-start(f32[104,128]{1,0:T(8,128)S(1)} %add_add_fusion.mine_ref), channel_id=1, source_target_pairs={{0,16},{16,0},{32,48},{48,32},{64,80},{80,64},{96,112},{112,96},{1... | collective-permute-start | bytes 159752 | tf_op jit(solution)/shard_map/ppermute | solution.py:324
  (7 other events, 129.0 us)

commit v4 on v3

--- a/solution.py
+++ b/solution.py
@@ -25,9 +25,9 @@
     return lax.dot_general(a, b, (((1,), (1,)), ((), ())), precision=HIGH, preferred_element_type=F32)
 
 
-def graph_kernel(place_ref, rows_ref, cols_ref, near_ref, far_ref, blocks_ref, out_ref, panel, acc, *own):
-    live, brow = place_ref[0], place_ref[1]
+def graph_kernel(table_ref, near_ref, far_ref, blocks_ref, out_ref, panel, acc, *own):
     n_slots = blocks_ref.shape[0]
+    live = table_ref[2 * n_slots]
     sub = panel.shape[0] // 8
     chunks = n_slots // CHUNK
     held = own[0] if own else blocks_ref
@@ -46,12 +46,6 @@
         for q in range(sub):
             panel[s * sub + q] = src[s % 4, :, q * 256:(q + 1) * 256]
     acc[...] = jnp.zeros_like(acc)
-
-    def spot(slot):
-        source = lax.div(cols_ref[slot], sub)
-        turn = jnp.bitwise_and(lax.div(brow, 2) - lax.div(source, 2), 3)
-        side = jnp.bitwise_and(brow - source, 1)
-        return (turn + 4 * side) * sub + lax.rem(cols_ref[slot], sub)
 
     for c in range(chunks):
         @pl.when(c * CHUNK < live)
@@ -59,17 +53,17 @@
             if own:
                 fetch(c).wait()
             slots = range(c * CHUNK, (c + 1) * CHUNK)
-            prods = [lax.dot_general(panel[spot(s)], held[s], (((1,), (1,)), ((), ())),
+            prods = [lax.dot_general(panel[table_ref[n_slots + s]], held[s], (((1,), (1,)), ((), ())),
                                      preferred_element_type=F32) for s in slots]
             for s, prod in zip(slots, prods):
-                row = jnp.where(s < live, rows_ref[s], acc.shape[0] - 1)
+                row = table_ref[s]
                 acc[row] = acc[row] + prod
     for j in range(out_ref.shape[0]):
         for q in range(sub):
             out_ref[j, :, q * 256:(q + 1) * 256] = acc[j * sub + q].astype(BF)
 
 
-def graph_partial(place, rows, cols, near, far, blocks, owners, fetched):
+def graph_partial(table, near, far, blocks, owners, fetched):
     n_slots, side, _ = blocks.shape
     r, width = near.shape[1:]
     sub = width // side
@@ -77,7 +71,7 @@
     return pl.pallas_call(
         graph_kernel,
         out_shape=jax.ShapeDtypeStruct((owners, r, width), BF),
-        in_specs=[SMEM] * 3 + [VMEM] * 2 + [pl.BlockSpec(memory_space=pltpu.HBM) if fetched else VMEM],
+        in_specs=[SMEM] + [VMEM] * 2 + [pl.BlockSpec(memory_space=pltpu.HBM) if fetched else VMEM],
         out_specs=VMEM,
         scratch_shapes=[
             pltpu.VMEM((8 * sub, r, side), BF),
@@ -85,7 +79,7 @@
         ] + (own if fetched else []),
         compiler_params=pltpu.CompilerParams(vmem_limit_bytes=(50 if fetched else 14) * 2**20),
         name="graph_partial",
-    )(place, rows, cols, near, far, blocks)
+    )(table, near, far, blocks)
 
 
 def halves(a):
@@ -211,10 +205,14 @@
     put(6, 4, jnp.concatenate([packed[6 * w:6 * w + q, n * w:(n + 1) * w] for n in range(4)], 0))
 
 
-def next_block(rows, basis, gram, inverse_x, w):
+def next_block(rows, basis, gram, inverse_x, width, w):
     zt = nn(gram[2 * w:, :w], inverse_x)
-    x = nn(rows, basis)
-    return x, x - nn(rows[:, :w] + nn(rows[:, 2 * w:], zt), basis[:w])
+    both = jnp.concatenate([rows, jnp.concatenate([-nn(rows[:, 2 * w:], zt), rows[:, w:]], 1)], 0)
+    if basis is None:
+        both = jnp.concatenate([both, jnp.zeros((2 * w, width - 3 * w), F32)], 1)
+    else:
+        both = nn(both, basis)
+    return both[:w], both[w:]
 
 
 def small_kernel(w, cut_ref, core_ref, mine_ref, other_ref, *rest):
@@ -226,12 +224,11 @@
     width = full.shape[0]
     gram = full[:3 * w, :3 * w]
     sym = 0.5 * (full[:3 * w, 2 * w:5 * w] + full[2 * w:5 * w, :3 * w])
-    basis = (lax.broadcasted_iota(jnp.int32, (3 * w, width), 0)
-             == lax.broadcasted_iota(jnp.int32, (3 * w, width), 1)).astype(F32)
+    basis = None
     for _ in range(ITERS - 1):
         inverse, inverse_x = spd_inverses([gram, gram[:w, :w]], refs)
         rows = sign_rows(sym, inverse, cut_ref[0], w)
-        x, p = next_block(rows, basis, gram, inverse_x, w)
+        x, p = next_block(rows, basis, gram, inverse_x, width, w)
         basis = jnp.concatenate([x, p, shift(x, w)], 0)
         tb = nn(basis, full[...])
         moved = shift(basis, w)
@@ -239,7 +236,7 @@
         sym = 0.5 * (nt(tb, moved) + nt(moved, tb))
     inverse, inverse_x = spd_inverses([gram, gram[:w, :w]], refs)
     rows = sign_rows(sym, inverse, cut_ref[0], w)
-    x, p = next_block(rows, basis, gram, inverse_x, w)
+    x, p = next_block(rows, basis, gram, inverse_x, width, w)
     tx = nn(rows, tb)
     moved = shift(x, w)
     (inverse_x,) = spd_inverses([nt(tx, x)], refs[1:])
@@ -308,7 +305,8 @@
 
 
 def gather_brow(v):
-    near = jnp.stack([v] + [lax.ppermute(v, "brow", z_turn(k)) for k in (1, 2, 3)])
+    got = {k: lax.ppermute(v, "brow", z_turn(k)) for k in (3, 2, 1)}
+    near = jnp.stack([v, got[3], got[1], got[2]])
     return near, lax.ppermute(near, "brow", CORE)
 
 
@@ -319,7 +317,7 @@
     other = lax.dynamic_slice_in_dim(g, (1 - me) * half, half, 0)
     v = mine + lax.ppermute(other, "brow", CORE)
     for axis, turn in (("brow", z_turn), ("bcol", y_turn), ("bcol", x_turn)):
-        a, b, c = [lax.ppermute(v, axis, turn(k)) for k in (1, 2, 3)]
+        a, b, c = [lax.ppermute(v, axis, turn(k)) for k in (3, 2, 1)]
         v = (v + a) + (b + c)
     return v, lax.ppermute(v, "brow", CORE)
 
@@ -329,12 +327,17 @@
     wanted = eigen_block.shape[0]
     owners = lax.axis_size("bcol")
     brow = lax.axis_index("brow")
-    place = jnp.stack([live_count[0, 0], brow])
-    rows, cols = pattern_rows[0, 0], pattern_cols[0, 0]
+    sub = eigen_block.shape[1] // block_set.shape[-1]
+    rows, source, live = pattern_rows[0, 0], pattern_cols[0, 0] // sub, live_count[0, 0]
+    rows = jnp.where(jnp.arange(rows.shape[0]) < live, rows, owners * sub)
+    turn = (brow // 2 - source // 2) % 4
+    place = jnp.where(turn > 0, turn % 3 + 1, 0)
+    spots = (place + 4 * ((brow - source) % 2)) * sub + pattern_cols[0, 0] % sub
+    table = jnp.concatenate([rows, spots, live.reshape(1)])
 
     def apply_graph(v, fetched=False):
         near, far = gather_brow((degree_scale * v).astype(BF))
-        part = graph_partial(place, rows, cols, near, far, block_set, owners, fetched)
+        part = graph_partial(table, near, far, block_set, owners, fetched)
         got = lax.all_to_all(part, "bcol", 0, 0)
         return degree_scale * jnp.sum(got.astype(F32), axis=0)
 

time: 167 us -> 162 us (0.970)
  waiting for transfers between devices: 34.1 us -> 29.7 us
    ppermute x18, waiting for transfers between devices: 15.1 us -> 11.5 us  [the longest x9 6.21 us: gather_brow(): got = {k: lax.ppermute(v, 'brow', z_turn(k)) for k in (3, 2, 1)}]
    ppermute x18, starting transfers between devices: 25.1 us -> 26.9 us  [the longest x9 15.5 us: gather_brow(): got = {k: lax.ppermute(v, 'brow', z_turn(k)) for k in (3, 2, 1)}]
  transfers between devices with their start and end apart: 24 -> 24, of which waited for: 19 -> 18; matrix products, arithmetic and copies ran while one was open for 1% -> 1% of each run, Pallas kernels for 0% -> 0%
where the time goes in v4:
time: 162 us
  blocking collectives  52.3 us (32%)
  starting transfers between devices  44.6 us (28%)
  waiting for transfers between devices  29.7 us (18%)
  Pallas kernels  29 us (18%)
  other arithmetic  3.53 us (2%)
  between operations  2.12 us (1%)
    all_to_all x2, blocking collectives, apply_graph(): got = lax.all_to_all(part, 'bcol', 0, 0)  52.3 us
    pallas_call x1, Pallas kernels, small(): pl.pallas_call(functools.partial(small_kernel, w), out_shape=[jax.ShapeDt...  18 us
    ppermute x9, starting transfers between devices, gather_brow(): got = {k: lax.ppermute(v, 'brow', z_turn(k)) for k in (3, 2, 1)}  15.5 us
    all_to_all x1, waiting for transfers between devices, apply_graph(): got = lax.all_to_all(part, 'bcol', 0, 0)  14.6 us
    ppermute x9, starting transfers between devices, sum_all(): a, b, c = [lax.ppermute(v, axis, turn(k)) for k in (3, 2, 1)]  11.4 us
    pallas_call x3, Pallas kernels, graph_partial(): pl.pallas_call(graph_kernel, out_shape=jax.ShapeDtypeStruct((owners, r, w...  10.1 us
    ppermute x3, starting transfers between devices, gather_brow(): return (near, lax.ppermute(near, 'brow', CORE))  8.45 us
    ppermute x9, waiting for transfers between devices, gather_brow(): got = {k: lax.ppermute(v, 'brow', z_turn(k)) for k in (3, 2, 1)}  6.21 us
  transfers between devices with their start and end apart: 24, of which 18 were waited for; matrix products, arithmetic and copies ran while one was open for 1% of the time, Pallas kernels for 0%

profile of v4, /device:TPU:1, one launch (start us, length us, event | category | flops | bytes accessed | tf_op | source)
XLA Modules:
  0.0 161.7 jit_solution(1763998686051798170)
XLA Ops:
  1.6 4.5 %collective-permute-start.2 = (bf16[64,768]{1,0:T(8,128)(2,1)S(1)}, bf16[64,768]{1,0:T(8,128)(2,1)S(1)}, u32[]{:S(2)}, u32[]{:S(2)}) collective-permute-start(bf16[64,768]{1,0:T(8,128)(2,1)S(1)} %fusion.1), channel_id=1, source_target_pairs={{0,64},{16,80},{32,96},{48,112},{64,0},{80,16},{96,32},{112,48},{1... | collective-permute-start | bytes 294920 | tf_op jit(solution)/shard_map/ppermute | solution.py:308
  6.8 1.9 %collective-permute-start = (bf16[64,768]{1,0:T(8,128)(2,1)S(1)}, bf16[64,768]{1,0:T(8,128)(2,1)S(1)}, u32[]{:S(2)}, u32[]{:S(2)}) collective-permute-start(bf16[64,768]{1,0:T(8,128)(2,1)S(1)} %fusion.1), channel_id=1, source_target_pairs={{0,96},{16,112},{32,0},{48,16},{64,32},{80,48},{96,64},{112,80},{1... | collective-permute-start | bytes 294920 | tf_op jit(solution)/shard_map/ppermute | solution.py:308
  11.4 1.6 %collective-permute-start.3 = (bf16[4,64,768]{2,1,0:T(8,128)(2,1)S(1)}, bf16[4,64,768]{2,1,0:T(8,128)(2,1)S(1)}, u32[]{:S(2)}, u32[]{:S(2)}) collective-permute-start(bf16[4,64,768]{2,1,0:T(8,128)(2,1)S(1)} %pad_maximum_fusion.near_ref), channel_id=1, source_target_pairs={{0,16},{16,0},{32,48},{48,32},{64,80},{80,64},{96,112},{112,96},{1... | collective-permute-start | bytes 1179656 | tf_op jit(solution)/shard_map/ppermute | solution.py:310
  14.5 4.0 %graph_partial.3 = bf16[16,64,768]{2,1,0:T(8,128)(2,1)S(1)} custom-call(s32[81]{0:T(128)S(1)} %pad_add_fusion.table_ref, bf16[4,64,768]{2,1,0:T(8,128)(2,1)S(1)} %pad_maximum_fusion.near_ref, bf16[4,64,768]{2,1,0:T(8,128)(2,1)S(1)} %collective-permute-done.3.far_ref, bf16[40,256,256]{2,1,0:T(8,128)(2,1)} %bitcast.41), custom_call_target="tpu_custom_call" | custom-call | tf_op jit(solution)/shard_map/graph_partial/pallas_call | solution.py:71
  18.5 27.9 %all_to_all.15 = bf16[16,64,768]{2,1,0:T(8,128)(2,1)S(1)} all-to-all(bf16[16,64,768]{2,1,0:T(8,128)(2,1)S(1)} %graph_partial.3), channel_id=1, replica_groups=mesh['brow'=8,'bcol'=16] {'bcol'}, dimensions={0} | all-to-all | bytes 3145728 | tf_op jit(solution)/shard_map/all_to_all | solution.py:341
  48.4 2.1 %collective-permute-start.5 = (bf16[64,768]{1,0:T(8,128)(2,1)S(1)}, bf16[64,768]{1,0:T(8,128)(2,1)S(1)}, u32[]{:S(2)}, u32[]{:S(2)}) collective-permute-start(bf16[64,768]{1,0:T(8,128)(2,1)S(1)} %get-tuple-element.4), channel_id=1, source_target_pairs={{0,32},{16,48},{32,64},{48,80},{64,96},{80,112},{96,0},{112,16},{1... | collective-permute-start | bytes 294920 | tf_op jit(solution)/shard_map/ppermute | solution.py:308
  54.3 3.5 %collective-permute-start.7 = (bf16[4,64,768]{2,1,0:T(8,128)(2,1)S(1)}, bf16[4,64,768]{2,1,0:T(8,128)(2,1)S(1)}, u32[]{:S(2)}, u32[]{:S(2)}) collective-permute-start(bf16[4,64,768]{2,1,0:T(8,128)(2,1)S(1)} %pad_maximum_fusion.1.near_ref), channel_id=1, source_target_pairs={{0,16},{16,0},{32,48},{48,32},{64,80},{80,64},{96,112},{112,96},{1... | collective-permute-start | bytes 1179656 | tf_op jit(solution)/shard_map/ppermute | solution.py:310
  57.8 1.3 collective-permute-done.7.far_ref
  59.1 2.7 %graph_partial.4 = bf16[16,64,768]{2,1,0:T(8,128)(2,1)S(1)} custom-call(s32[81]{0:T(128)S(1)} %pad_add_fusion.table_ref, bf16[4,64,768]{2,1,0:T(8,128)(2,1)S(1)} %pad_maximum_fusion.1.near_ref, bf16[4,64,768]{2,1,0:T(8,128)(2,1)S(1)} %collective-permute-done.7.far_ref, bf16[40,256,256]{2,1,0:T(8,128)(2,1)S(1)} %bitcast.44), custom_call_target="tpu_custom_call" | custom-call | tf_op jit(solution)/shard_map/graph_partial/pallas_call | solution.py:71
  61.9 24.3 %all_to_all.16 = bf16[16,64,768]{2,1,0:T(8,128)(2,1)S(1)} all-to-all(bf16[16,64,768]{2,1,0:T(8,128)(2,1)S(1)} %graph_partial.4), channel_id=1, replica_groups=mesh['brow'=8,'bcol'=16] {'bcol'}, dimensions={0} | all-to-all | bytes 3145728 | tf_op jit(solution)/shard_map/all_to_all | solution.py:341
  86.5 1.8 %collective-permute-start.10 = (bf16[32,768]{1,0:T(8,128)(2,1)S(1)}, bf16[32,768]{1,0:T(8,128)(2,1)S(1)}, u32[]{:S(2)}, u32[]{:S(2)}) collective-permute-start(bf16[32,768]{1,0:T(8,128)(2,1)S(1)} %get-tuple-element.6), channel_id=1, source_target_pairs={{0,64},{16,80},{32,96},{48,112},{64,0},{80,16},{96,32},{112,48},{1... | collective-permute-start | bytes 147464 | tf_op jit(solution)/shard_map/ppermute | solution.py:308
  89.0 1.9 %collective-permute-start.8 = (bf16[32,768]{1,0:T(8,128)(2,1)S(1)}, bf16[32,768]{1,0:T(8,128)(2,1)S(1)}, u32[]{:S(2)}, u32[]{:S(2)}) collective-permute-start(bf16[32,768]{1,0:T(8,128)(2,1)S(1)} %get-tuple-element.6), channel_id=1, source_target_pairs={{0,96},{16,112},{32,0},{48,16},{64,32},{80,48},{96,64},{112,80},{1... | collective-permute-start | bytes 147464 | tf_op jit(solution)/shard_map/ppermute | solution.py:308
  91.0 1.4 collective-permute-done.9
  92.4 3.3 %collective-permute-start.11 = (bf16[4,32,768]{2,1,0:T(8,128)(2,1)S(1)}, bf16[4,32,768]{2,1,0:T(8,128)(2,1)S(1)}, u32[]{:S(2)}, u32[]{:S(2)}) collective-permute-start(bf16[4,32,768]{2,1,0:T(8,128)(2,1)S(1)} %pad_maximum_fusion.2.near_ref), channel_id=1, source_target_pairs={{0,16},{16,0},{32,48},{48,32},{64,80},{80,64},{96,112},{112,96},{1... | collective-permute-start | bytes 589832 | tf_op jit(solution)/shard_map/ppermute | solution.py:310
  96.8 3.3 %graph_partial.5 = bf16[16,32,768]{2,1,0:T(8,128)(2,1)} custom-call(s32[81]{0:T(128)S(1)} %pad_add_fusion.table_ref, bf16[4,32,768]{2,1,0:T(8,128)(2,1)S(1)} %pad_maximum_fusion.2.near_ref, bf16[4,32,768]{2,1,0:T(8,128)(2,1)S(1)} %collective-permute-done.11.far_ref, bf16[40,256,256]{2,1,0:T(8,128)(2,1)S(1)} %bitcast.45), custom_call_target="tpu_custom_call" | custom-call | tf_op jit(solution)/shard_map/graph_partial/pallas_call | solution.py:71
  100.2 3.7 %all-to-all-start.2 = ((bf16[16,32,768]{2,1,0:T(8,128)(2,1)}), bf16[16,32,768]{2,1,0:T(8,128)(2,1)S(1)}, u32[]{:S(2)}, u32[]{:S(2)}) async-start(bf16[16,32,768]{2,1,0:T(8,128)(2,1)} %graph_partial.5), calls=%async_computation.2 | async-start | bytes 1572864 | tf_op jit(solution)/shard_map/all_to_all | solution.py:341
  103.9 14.6 %all-to-all-done.2 = bf16[16,32,768]{2,1,0:T(8,128)(2,1)S(1)} async-done(((bf16[16,32,768]{2,1,0:T(8,128)(2,1)}), bf16[16,32,768]{2,1,0:T(8,128)(2,1)S(1)}, u32[]{:S(2)}, u32[]{:S(2)}) %all-to-all-start.2) | async-done | bytes 786464 | tf_op jit(solution)/shard_map/all_to_all | solution.py:341
  121.7 1.6 collective-permute-start.14
  124.2 1.8 %collective-permute-start.13 = (f32[104,128]{1,0:T(8,128)S(1)}, f32[104,128]{1,0:T(8,128)S(1)}, u32[]{:S(2)}, u32[]{:S(2)}) collective-permute-start(f32[104,128]{1,0:T(8,128)S(1)} %dynamic-slice_add_fusion), channel_id=1, source_target_pairs={{0,96},{16,112},{32,0},{48,16},{64,32},{80,48},{96,64},{112,80},{1... | collective-permute-start | bytes 159752 | tf_op jit(solution)/shard_map/ppermute | solution.py:320
  126.3 1.6 collective-permute-done.15
  128.5 2.7 %collective-permute-start.16 = (f32[104,128]{1,0:T(8,128)S(1)}, f32[104,128]{1,0:T(8,128)S(1)}, u32[]{:S(2)}, u32[]{:S(2)}) collective-permute-start(f32[104,128]{1,0:T(8,128)S(1)} %add_add_fusion.2), channel_id=1, source_target_pairs={{0,3},{1,0},{2,1},{3,2},{4,7},{5,4},{6,5},{7,6},{8,11},{9,8},{10,9... | collective-permute-start | bytes 159752 | tf_op jit(solution)/shard_map/ppermute | solution.py:320
  134.4 2.5 %collective-permute-start.19 = (f32[104,128]{1,0:T(8,128)S(1)}, f32[104,128]{1,0:T(8,128)S(1)}, u32[]{:S(2)}, u32[]{:S(2)}) collective-permute-start(f32[104,128]{1,0:T(8,128)S(1)} %add_add_fusion.1), channel_id=1, source_target_pairs={{0,12},{1,13},{2,14},{3,15},{4,0},{5,1},{6,2},{7,3},{8,4},{9,5},{1... | collective-permute-start | bytes 159752 | tf_op jit(solution)/shard_map/ppermute | solution.py:320
  138.5 4.4 %collective-permute-start.22 = (f32[104,128]{1,0:T(8,128)S(1)}, f32[104,128]{1,0:T(8,128)S(1)}, u32[]{:S(2)}, u32[]{:S(2)}) collective-permute-start(f32[104,128]{1,0:T(8,128)S(1)} %add_add_fusion.mine_ref), channel_id=1, source_target_pairs={{0,16},{16,0},{32,48},{48,32},{64,80},{80,64},{96,112},{112,96},{1... | collective-permute-start | bytes 159752 | tf_op jit(solution)/shard_map/ppermute | solution.py:322
  143.7 18.0 %small_matrices.1 = (f32[32,768]{1,0:T(8,128)}, f32[32,768]{1,0:T(8,128)}, f32[32,768]{1,0:T(8,128)}, f32[32,768]{1,0:T(8,128)}) custom-call(f32[1]{0:T(128)S(6)} %copy.13.cut_ref, s32[1]{0:T(128)} %bitcast.core_ref, f32[104,128]{1,0:T(8,128)S(1)} %add_add_fusion.mine_ref, f32[104,128]{1,0:T(8,128)S(1)} %collective-permute-done.22.other_ref, ...), custom_call_target="tpu_custom_call" | custom-call | tf_op jit(solution)/shard_map/small_matrices/pallas_call | solution.py:253
  (63 shorter events, 23.1 us)
Async XLA Ops:
  1.6 8.1 %collective-permute-start.2 = (bf16[64,768]{1,0:T(8,128)(2,1)S(1)}, bf16[64,768]{1,0:T(8,128)(2,1)S(1)}, u32[]{:S(2)}, u32[]{:S(2)}) collective-permute-start(bf16[64,768]{1,0:T(8,128)(2,1)S(1)} %fusion.1), channel_id=1, source_target_pairs={{0,64},{16,80},{32,96},{48,112},{64,0},{80,16},{96,32},{112,48},{1... | collective-permute-start | bytes 294920 | tf_op jit(solution)/shard_map/ppermute | solution.py:308
  6.1 4.7 %collective-permute-start.1 = (bf16[64,768]{1,0:T(8,128)(2,1)S(1)}, bf16[64,768]{1,0:T(8,128)(2,1)S(1)}, u32[]{:S(2)}, u32[]{:S(2)}) collective-permute-start(bf16[64,768]{1,0:T(8,128)(2,1)S(1)} %fusion.1), channel_id=1, source_target_pairs={{0,32},{16,48},{32,64},{48,80},{64,96},{80,112},{96,0},{112,16},{1... | collective-permute-start | bytes 294920 | tf_op jit(solution)/shard_map/ppermute | solution.py:308
  6.8 4.5 %collective-permute-start = (bf16[64,768]{1,0:T(8,128)(2,1)S(1)}, bf16[64,768]{1,0:T(8,128)(2,1)S(1)}, u32[]{:S(2)}, u32[]{:S(2)}) collective-permute-start(bf16[64,768]{1,0:T(8,128)(2,1)S(1)} %fusion.1), channel_id=1, source_target_pairs={{0,96},{16,112},{32,0},{48,16},{64,32},{80,48},{96,64},{112,80},{1... | collective-permute-start | bytes 294920 | tf_op jit(solution)/shard_map/ppermute | solution.py:308
  11.4 3.1 %collective-permute-start.3 = (bf16[4,64,768]{2,1,0:T(8,128)(2,1)S(1)}, bf16[4,64,768]{2,1,0:T(8,128)(2,1)S(1)}, u32[]{:S(2)}, u32[]{:S(2)}) collective-permute-start(bf16[4,64,768]{2,1,0:T(8,128)(2,1)S(1)} %pad_maximum_fusion.near_ref), channel_id=1, source_target_pairs={{0,16},{16,0},{32,48},{48,32},{64,80},{80,64},{96,112},{112,96},{1... | collective-permute-start | bytes 1179656 | tf_op jit(solution)/shard_map/ppermute | solution.py:310
  47.2 5.1 %collective-permute-start.6 = (bf16[64,768]{1,0:T(8,128)(2,1)S(1)}, bf16[64,768]{1,0:T(8,128)(2,1)S(1)}, u32[]{:S(2)}, u32[]{:S(2)}) collective-permute-start(bf16[64,768]{1,0:T(8,128)(2,1)S(1)} %get-tuple-element.4), channel_id=1, source_target_pairs={{0,64},{16,80},{32,96},{48,112},{64,0},{80,16},{96,32},{112,48},{1... | collective-permute-start | bytes 294920 | tf_op jit(solution)/shard_map/ppermute | solution.py:308
  48.4 4.9 %collective-permute-start.5 = (bf16[64,768]{1,0:T(8,128)(2,1)S(1)}, bf16[64,768]{1,0:T(8,128)(2,1)S(1)}, u32[]{:S(2)}, u32[]{:S(2)}) collective-permute-start(bf16[64,768]{1,0:T(8,128)(2,1)S(1)} %get-tuple-element.4), channel_id=1, source_target_pairs={{0,32},{16,48},{32,64},{48,80},{64,96},{80,112},{96,0},{112,16},{1... | collective-permute-start | bytes 294920 | tf_op jit(solution)/shard_map/ppermute | solution.py:308
  50.4 3.8 %collective-permute-start.4 = (bf16[64,768]{1,0:T(8,128)(2,1)S(1)}, bf16[64,768]{1,0:T(8,128)(2,1)S(1)}, u32[]{:S(2)}, u32[]{:S(2)}) collective-permute-start(bf16[64,768]{1,0:T(8,128)(2,1)S(1)} %get-tuple-element.4), channel_id=1, source_target_pairs={{0,96},{16,112},{32,0},{48,16},{64,32},{80,48},{96,64},{112,80},{1... | collective-permute-start | bytes 294920 | tf_op jit(solution)/shard_map/ppermute | solution.py:308
  54.3 4.8 %collective-permute-start.7 = (bf16[4,64,768]{2,1,0:T(8,128)(2,1)S(1)}, bf16[4,64,768]{2,1,0:T(8,128)(2,1)S(1)}, u32[]{:S(2)}, u32[]{:S(2)}) collective-permute-start(bf16[4,64,768]{2,1,0:T(8,128)(2,1)S(1)} %pad_maximum_fusion.1.near_ref), channel_id=1, source_target_pairs={{0,16},{16,0},{32,48},{48,32},{64,80},{80,64},{96,112},{112,96},{1... | collective-permute-start | bytes 1179656 | tf_op jit(solution)/shard_map/ppermute | solution.py:310
  86.5 4.5 %collective-permute-start.10 = (bf16[32,768]{1,0:T(8,128)(2,1)S(1)}, bf16[32,768]{1,0:T(8,128)(2,1)S(1)}, u32[]{:S(2)}, u32[]{:S(2)}) collective-permute-start(bf16[32,768]{1,0:T(8,128)(2,1)S(1)} %get-tuple-element.6), channel_id=1, source_target_pairs={{0,64},{16,80},{32,96},{48,112},{64,0},{80,16},{96,32},{112,48},{1... | collective-permute-start | bytes 147464 | tf_op jit(solution)/shard_map/ppermute | solution.py:308
  88.2 4.2 %collective-permute-start.9 = (bf16[32,768]{1,0:T(8,128)(2,1)S(1)}, bf16[32,768]{1,0:T(8,128)(2,1)S(1)}, u32[]{:S(2)}, u32[]{:S(2)}) collective-permute-start(bf16[32,768]{1,0:T(8,128)(2,1)S(1)} %get-tuple-element.6), channel_id=1, source_target_pairs={{0,32},{16,48},{32,64},{48,80},{64,96},{80,112},{96,0},{112,16},{1... | collective-permute-start | bytes 147464 | tf_op jit(solution)/shard_map/ppermute | solution.py:308
  89.0 3.4 %collective-permute-start.8 = (bf16[32,768]{1,0:T(8,128)(2,1)S(1)}, bf16[32,768]{1,0:T(8,128)(2,1)S(1)}, u32[]{:S(2)}, u32[]{:S(2)}) collective-permute-start(bf16[32,768]{1,0:T(8,128)(2,1)S(1)} %get-tuple-element.6), channel_id=1, source_target_pairs={{0,96},{16,112},{32,0},{48,16},{64,32},{80,48},{96,64},{112,80},{1... | collective-permute-start | bytes 147464 | tf_op jit(solution)/shard_map/ppermute | solution.py:308
  92.4 4.4 %collective-permute-start.11 = (bf16[4,32,768]{2,1,0:T(8,128)(2,1)S(1)}, bf16[4,32,768]{2,1,0:T(8,128)(2,1)S(1)}, u32[]{:S(2)}, u32[]{:S(2)}) collective-permute-start(bf16[4,32,768]{2,1,0:T(8,128)(2,1)S(1)} %pad_maximum_fusion.2.near_ref), channel_id=1, source_target_pairs={{0,16},{16,0},{32,48},{48,32},{64,80},{80,64},{96,112},{112,96},{1... | collective-permute-start | bytes 589832 | tf_op jit(solution)/shard_map/ppermute | solution.py:310
  100.2 18.4 %all-to-all-start.2 = ((bf16[16,32,768]{2,1,0:T(8,128)(2,1)}), bf16[16,32,768]{2,1,0:T(8,128)(2,1)S(1)}, u32[]{:S(2)}, u32[]{:S(2)}) async-start(bf16[16,32,768]{2,1,0:T(8,128)(2,1)} %graph_partial.5), calls=%async_computation.2 | async-start | bytes 1572864 | tf_op jit(solution)/shard_map/all_to_all | solution.py:341
  119.7 2.0 %collective-permute-start.12 = (f32[104,128]{1,0:T(8,128)S(1)}, f32[104,128]{1,0:T(8,128)S(1)}, u32[]{:S(2)}, u32[]{:S(2)}) collective-permute-start(f32[104,128]{1,0:T(8,128)S(1)} %constant_dynamic-slice_fusion), channel_id=1, source_target_pairs={{0,16},{16,0},{32,48},{48,32},{64,80},{80,64},{96,112},{112,96},{1... | collective-permute-start | bytes 159752 | tf_op jit(solution)/shard_map/ppermute | solution.py:318
  121.7 4.6 %collective-permute-start.14 = (f32[104,128]{1,0:T(8,128)S(1)}, f32[104,128]{1,0:T(8,128)S(1)}, u32[]{:S(2)}, u32[]{:S(2)}) collective-permute-start(f32[104,128]{1,0:T(8,128)S(1)} %dynamic-slice_add_fusion), channel_id=1, source_target_pairs={{0,64},{16,80},{32,96},{48,112},{64,0},{80,16},{96,32},{112,48},{1... | collective-permute-start | bytes 159752 | tf_op jit(solution)/shard_map/ppermute | solution.py:320
  123.3 4.6 %collective-permute-start.15 = (f32[104,128]{1,0:T(8,128)S(1)}, f32[104,128]{1,0:T(8,128)S(1)}, u32[]{:S(2)}, u32[]{:S(2)}) collective-permute-start(f32[104,128]{1,0:T(8,128)S(1)} %dynamic-slice_add_fusion), channel_id=1, source_target_pairs={{0,32},{16,48},{32,64},{48,80},{64,96},{80,112},{96,0},{112,16},{1... | collective-permute-start | bytes 159752 | tf_op jit(solution)/shard_map/ppermute | solution.py:320
  124.2 3.6 %collective-permute-start.13 = (f32[104,128]{1,0:T(8,128)S(1)}, f32[104,128]{1,0:T(8,128)S(1)}, u32[]{:S(2)}, u32[]{:S(2)}) collective-permute-start(f32[104,128]{1,0:T(8,128)S(1)} %dynamic-slice_add_fusion), channel_id=1, source_target_pairs={{0,96},{16,112},{32,0},{48,16},{64,32},{80,48},{96,64},{112,80},{1... | collective-permute-start | bytes 159752 | tf_op jit(solution)/shard_map/ppermute | solution.py:320
  127.9 4.6 %collective-permute-start.17 = (f32[104,128]{1,0:T(8,128)S(1)}, f32[104,128]{1,0:T(8,128)S(1)}, u32[]{:S(2)}, u32[]{:S(2)}) collective-permute-start(f32[104,128]{1,0:T(8,128)S(1)} %add_add_fusion.2), channel_id=1, source_target_pairs={{0,2},{1,3},{2,0},{3,1},{4,6},{5,7},{6,4},{7,5},{8,10},{9,11},{10,... | collective-permute-start | bytes 159752 | tf_op jit(solution)/shard_map/ppermute | solution.py:320
  128.5 4.6 %collective-permute-start.18 = (f32[104,128]{1,0:T(8,128)S(1)}, f32[104,128]{1,0:T(8,128)S(1)}, u32[]{:S(2)}, u32[]{:S(2)}) collective-permute-start(f32[104,128]{1,0:T(8,128)S(1)} %add_add_fusion.2), channel_id=1, source_target_pairs={{0,1},{1,2},{2,3},{3,0},{4,5},{5,6},{6,7},{7,4},{8,9},{9,10},{10,1... | collective-permute-start | bytes 159752 | tf_op jit(solution)/shard_map/ppermute | solution.py:320
  128.5 4.6 %collective-permute-start.16 = (f32[104,128]{1,0:T(8,128)S(1)}, f32[104,128]{1,0:T(8,128)S(1)}, u32[]{:S(2)}, u32[]{:S(2)}) collective-permute-start(f32[104,128]{1,0:T(8,128)S(1)} %add_add_fusion.2), channel_id=1, source_target_pairs={{0,3},{1,0},{2,1},{3,2},{4,7},{5,4},{6,5},{7,6},{8,11},{9,8},{10,9... | collective-permute-start | bytes 159752 | tf_op jit(solution)/shard_map/ppermute | solution.py:320
  133.0 4.6 %collective-permute-start.20 = (f32[104,128]{1,0:T(8,128)S(1)}, f32[104,128]{1,0:T(8,128)S(1)}, u32[]{:S(2)}, u32[]{:S(2)}) collective-permute-start(f32[104,128]{1,0:T(8,128)S(1)} %add_add_fusion.1), channel_id=1, source_target_pairs={{0,8},{1,9},{2,10},{3,11},{4,12},{5,13},{6,14},{7,15},{8,0},{9,1},... | collective-permute-start | bytes 159752 | tf_op jit(solution)/shard_map/ppermute | solution.py:320
  134.3 4.2 %collective-permute-start.21 = (f32[104,128]{1,0:T(8,128)S(1)}, f32[104,128]{1,0:T(8,128)S(1)}, u32[]{:S(2)}, u32[]{:S(2)}) collective-permute-start(f32[104,128]{1,0:T(8,128)S(1)} %add_add_fusion.1), channel_id=1, source_target_pairs={{0,4},{1,5},{2,6},{3,7},{4,8},{5,9},{6,10},{7,11},{8,12},{9,13},{1... | collective-permute-start | bytes 159752 | tf_op jit(solution)/shard_map/ppermute | solution.py:320
  134.4 4.0 %collective-permute-start.19 = (f32[104,128]{1,0:T(8,128)S(1)}, f32[104,128]{1,0:T(8,128)S(1)}, u32[]{:S(2)}, u32[]{:S(2)}) collective-permute-start(f32[104,128]{1,0:T(8,128)S(1)} %add_add_fusion.1), channel_id=1, source_target_pairs={{0,12},{1,13},{2,14},{3,15},{4,0},{5,1},{6,2},{7,3},{8,4},{9,5},{1... | collective-permute-start | bytes 159752 | tf_op jit(solution)/shard_map/ppermute | solution.py:320
  138.5 5.2 %collective-permute-start.22 = (f32[104,128]{1,0:T(8,128)S(1)}, f32[104,128]{1,0:T(8,128)S(1)}, u32[]{:S(2)}, u32[]{:S(2)}) collective-permute-start(f32[104,128]{1,0:T(8,128)S(1)} %add_add_fusion.mine_ref), channel_id=1, source_target_pairs={{0,16},{16,0},{32,48},{48,32},{64,80},{80,64},{96,112},{112,96},{1... | collective-permute-start | bytes 159752 | tf_op jit(solution)/shard_map/ppermute | solution.py:322
  (5 other events, 127.1 us)

commit v5 on v4

--- a/solution.py
+++ b/solution.py
@@ -153,11 +153,11 @@
 
     def body(state):
         level, _ = state
-        size = levels([r[0][...] for r in refs], [r[1][...] for r in refs], 2)
+        size = levels([r[0][...] for r in refs], [r[1][...] for r in refs], 1)
         return level + 1, size
 
     size = levels(errs, sums, 4)
-    _, size = lax.while_loop(lambda s: (s[1] > 1e-8) & (s[0] < 12), body, (jnp.int32(0), size))
+    _, size = lax.while_loop(lambda s: (s[1] > 1e-8) & (s[0] < 24), body, (jnp.int32(0), size))
     good = size <= 1e-8
 
     @pl.when(jnp.logical_not(good))
@@ -265,28 +265,42 @@
     k = [r[...] for r in refs[:-1]]
     out_ref = refs[-1]
     w = k[0].shape[0]
-    out_ref[:4 * w] = nt(jnp.concatenate([k[0], k[4], k[5], k[6]], 0), jnp.concatenate(k[:4], 0))
+    out_ref[:3 * w] = nt(jnp.concatenate([k[0], k[4], k[5]], 0), jnp.concatenate(k[:4], 0))
     inner = jnp.concatenate(k[1:4], 0)
     inner = nt(inner, inner)
     outer = nt(jnp.concatenate(k[4:], 0), k[4])
-    out_ref[4 * w:5 * w] = jnp.concatenate([inner[:w], outer[:w]], 1)
-    out_ref[5 * w:6 * w] = jnp.concatenate([inner[w:2 * w, w:], inner[2 * w:, 2 * w:], outer[w:2 * w]], 1)
+    out_ref[3 * w:4 * w] = jnp.concatenate([inner[:w], outer[:w]], 1)
+    out_ref[4 * w:] = jnp.concatenate([inner[w:2 * w, w:], inner[2 * w:, 2 * w:], outer[w:]], 1)
+
+
+def last_gram_kernel(*refs):
+    k = [r[...] for r in refs[:6]]
+    found_ref, out_ref = refs[6:]
+    w = k[0].shape[0]
+    last = nt(k[5], jnp.concatenate(k[:5], 0))
+    out_ref[:3 * w] = found_ref[:3 * w]
+    out_ref[3 * w:4 * w] = last[:, :4 * w]
+    out_ref[4 * w:6 * w] = found_ref[3 * w:]
     q = w // 4
-    last = outer[2 * w:]
-    out_ref[6 * w:6 * w + q] = jnp.concatenate([last[n * q:(n + 1) * q] for n in range(4)], 1)
+    out_ref[6 * w:6 * w + q] = jnp.concatenate([last[n * q:(n + 1) * q, 4 * w:] for n in range(4)], 1)
     out_ref[6 * w + q:] = jnp.zeros_like(out_ref[6 * w + q:])
+
+
+def gram_call(kernel, name, rows, *arrays):
+    return pl.pallas_call(
+        kernel,
+        out_shape=jax.ShapeDtypeStruct((rows, 4 * arrays[0].shape[0]), F32),
+        in_specs=[VMEM] * len(arrays),
+        out_specs=VMEM,
+        compiler_params=pltpu.CompilerParams(vmem_limit_bytes=16 * 2**20),
+        name=name,
+    )(*arrays)
 
 
 def packed_gram(blocks):
     w = blocks[0].shape[0]
-    return pl.pallas_call(
-        gram_kernel,
-        out_shape=jax.ShapeDtypeStruct((6 * w + w // 2, 4 * w), F32),
-        in_specs=[VMEM] * len(blocks),
-        out_specs=VMEM,
-        compiler_params=pltpu.CompilerParams(vmem_limit_bytes=16 * 2**20),
-        name="packed_gram",
-    )(*blocks)
+    found = gram_call(gram_kernel, "first_gram", 5 * w, *blocks[:6])
+    return gram_call(last_gram_kernel, "packed_gram", 6 * w + w // 2, *blocks[:5], blocks[6], found)
 
 
 def z_turn(k):
@@ -316,7 +330,7 @@
     mine = lax.dynamic_slice_in_dim(g, me * half, half, 0)
     other = lax.dynamic_slice_in_dim(g, (1 - me) * half, half, 0)
     v = mine + lax.ppermute(other, "brow", CORE)
-    for axis, turn in (("brow", z_turn), ("bcol", y_turn), ("bcol", x_turn)):
+    for axis, turn in (("bcol", x_turn), ("brow", z_turn), ("bcol", y_turn)):
         a, b, c = [lax.ppermute(v, axis, turn(k)) for k in (3, 2, 1)]
         v = (v + a) + (b + c)
     return v, lax.ppermute(v, "brow", CORE)

time: 162 us -> 162 us (level)
  blocking collectives: 52.3 us -> 54.5 us
  Pallas kernels: 29 us -> 27.1 us
    all_to_all x1, waiting for transfers between devices: 14.6 us -> 11.8 us  [apply_graph(): got = lax.all_to_all(part, 'bcol', 0, 0)]
    pallas_call x3, Pallas kernels: 10.1 us -> 7.44 us  [graph_partial(): pl.pallas_call(graph_kernel, out_shape=jax.ShapeDtypeStruct((owners, r, w...]
    all_to_all x2, blocking collectives: 52.3 us -> 54.5 us  [apply_graph(): got = lax.all_to_all(part, 'bcol', 0, 0)]
    ppermute x9, starting transfers between devices: 15.5 us -> 13.6 us  [gather_brow(): got = {k: lax.ppermute(v, 'brow', z_turn(k)) for k in (3, 2, 1)}]
    ppermute x1, starting transfers between devices: 1.1 us -> 2.84 us  [sum_all(): v = mine + lax.ppermute(other, 'brow', CORE)]
  transfers between devices with their start and end apart: 24 -> 24, of which waited for: 18 -> 18; matrix products, arithmetic and copies ran while one was open for 1% -> 1% of each run, Pallas kernels for 0% -> 1%
where the time goes in v5:
time: 162 us
  blocking collectives  54.5 us (34%)
  starting transfers between devices  45.3 us (28%)
  waiting for transfers between devices  28.6 us (18%)
  Pallas kernels  27.1 us (17%)
  other arithmetic  3.53 us (2%)
  between operations  2.12 us (1%)
    all_to_all x2, blocking collectives, apply_graph(): got = lax.all_to_all(part, 'bcol', 0, 0)  54.5 us
    pallas_call x1, Pallas kernels, small(): pl.pallas_call(functools.partial(small_kernel, w), out_shape=[jax.ShapeDt...  18.2 us
    ppermute x9, starting transfers between devices, gather_brow(): got = {k: lax.ppermute(v, 'brow', z_turn(k)) for k in (3, 2, 1)}  13.6 us
    ppermute x9, starting transfers between devices, sum_all(): a, b, c = [lax.ppermute(v, axis, turn(k)) for k in (3, 2, 1)]  12.3 us
    all_to_all x1, waiting for transfers between devices, apply_graph(): got = lax.all_to_all(part, 'bcol', 0, 0)  11.8 us
    ppermute x3, starting transfers between devices, gather_brow(): return (near, lax.ppermute(near, 'brow', CORE))  8.88 us
    ppermute x9, waiting for transfers between devices, gather_brow(): got = {k: lax.ppermute(v, 'brow', z_turn(k)) for k in (3, 2, 1)}  7.58 us
    pallas_call x3, Pallas kernels, graph_partial(): pl.pallas_call(graph_kernel, out_shape=jax.ShapeDtypeStruct((owners, r, w...  7.44 us
  transfers between devices with their start and end apart: 24, of which 18 were waited for; matrix products, arithmetic and copies ran while one was open for 1% of the time, Pallas kernels for 1%

profile of v5, /device:TPU:1, one launch (start us, length us, event | category | flops | bytes accessed | tf_op | source)
XLA Modules:
  0.0 161.6 jit_solution(8712454527539275424)
XLA Ops:
  1.6 4.5 %collective-permute-start.2 = (bf16[64,768]{1,0:T(8,128)(2,1)S(1)}, bf16[64,768]{1,0:T(8,128)(2,1)S(1)}, u32[]{:S(2)}, u32[]{:S(2)}) collective-permute-start(bf16[64,768]{1,0:T(8,128)(2,1)S(1)} %fusion.1), channel_id=1, source_target_pairs={{0,64},{16,80},{32,96},{48,112},{64,0},{80,16},{96,32},{112,48},{1... | collective-permute-start | bytes 294920 | tf_op jit(solution)/shard_map/ppermute | solution.py:322
  6.8 1.9 %collective-permute-start = (bf16[64,768]{1,0:T(8,128)(2,1)S(1)}, bf16[64,768]{1,0:T(8,128)(2,1)S(1)}, u32[]{:S(2)}, u32[]{:S(2)}) collective-permute-start(bf16[64,768]{1,0:T(8,128)(2,1)S(1)} %fusion.1), channel_id=1, source_target_pairs={{0,96},{16,112},{32,0},{48,16},{64,32},{80,48},{96,64},{112,80},{1... | collective-permute-start | bytes 294920 | tf_op jit(solution)/shard_map/ppermute | solution.py:322
  11.4 1.6 %collective-permute-start.3 = (bf16[4,64,768]{2,1,0:T(8,128)(2,1)S(1)}, bf16[4,64,768]{2,1,0:T(8,128)(2,1)S(1)}, u32[]{:S(2)}, u32[]{:S(2)}) collective-permute-start(bf16[4,64,768]{2,1,0:T(8,128)(2,1)S(1)} %pad_maximum_fusion.near_ref), channel_id=1, source_target_pairs={{0,16},{16,0},{32,48},{48,32},{64,80},{80,64},{96,112},{112,96},{1... | collective-permute-start | bytes 1179656 | tf_op jit(solution)/shard_map/ppermute | solution.py:324
  14.5 3.1 %graph_partial.3 = bf16[16,64,768]{2,1,0:T(8,128)(2,1)S(1)} custom-call(s32[81]{0:T(128)S(1)} %pad_add_fusion.table_ref, bf16[4,64,768]{2,1,0:T(8,128)(2,1)S(1)} %pad_maximum_fusion.near_ref, bf16[4,64,768]{2,1,0:T(8,128)(2,1)S(1)} %collective-permute-done.3.far_ref, bf16[40,256,256]{2,1,0:T(8,128)(2,1)} %bitcast.41), custom_call_target="tpu_custom_call" | custom-call | tf_op jit(solution)/shard_map/graph_partial/pallas_call | solution.py:71
  17.6 29.5 %all_to_all.15 = bf16[16,64,768]{2,1,0:T(8,128)(2,1)S(1)} all-to-all(bf16[16,64,768]{2,1,0:T(8,128)(2,1)S(1)} %graph_partial.3), channel_id=1, replica_groups=mesh['brow'=8,'bcol'=16] {'bcol'}, dimensions={0} | all-to-all | bytes 3145728 | tf_op jit(solution)/shard_map/all_to_all | solution.py:355
  48.0 2.8 %collective-permute-start.5 = (bf16[64,768]{1,0:T(8,128)(2,1)S(1)}, bf16[64,768]{1,0:T(8,128)(2,1)S(1)}, u32[]{:S(2)}, u32[]{:S(2)}) collective-permute-start(bf16[64,768]{1,0:T(8,128)(2,1)S(1)} %get-tuple-element.4), channel_id=1, source_target_pairs={{0,32},{16,48},{32,64},{48,80},{64,96},{80,112},{96,0},{112,16},{1... | collective-permute-start | bytes 294920 | tf_op jit(solution)/shard_map/ppermute | solution.py:322
  50.8 2.2 %collective-permute-done.6 = bf16[64,768]{1,0:T(8,128)(2,1)S(1)} collective-permute-done((bf16[64,768]{1,0:T(8,128)(2,1)S(1)}, bf16[64,768]{1,0:T(8,128)(2,1)S(1)}, u32[]{:S(2)}, u32[]{:S(2)}) %collective-permute-start.6) | collective-permute-done | bytes 98336 | tf_op jit(solution)/shard_map/ppermute | solution.py:322
  54.8 3.2 %collective-permute-start.7 = (bf16[4,64,768]{2,1,0:T(8,128)(2,1)S(1)}, bf16[4,64,768]{2,1,0:T(8,128)(2,1)S(1)}, u32[]{:S(2)}, u32[]{:S(2)}) collective-permute-start(bf16[4,64,768]{2,1,0:T(8,128)(2,1)S(1)} %pad_maximum_fusion.1.near_ref), channel_id=1, source_target_pairs={{0,16},{16,0},{32,48},{48,32},{64,80},{80,64},{96,112},{112,96},{1... | collective-permute-start | bytes 1179656 | tf_op jit(solution)/shard_map/ppermute | solution.py:324
  58.0 1.3 collective-permute-done.7.far_ref
  59.3 1.8 %graph_partial.4 = bf16[16,64,768]{2,1,0:T(8,128)(2,1)S(1)} custom-call(s32[81]{0:T(128)S(1)} %pad_add_fusion.table_ref, bf16[4,64,768]{2,1,0:T(8,128)(2,1)S(1)} %pad_maximum_fusion.1.near_ref, bf16[4,64,768]{2,1,0:T(8,128)(2,1)S(1)} %collective-permute-done.7.far_ref, bf16[40,256,256]{2,1,0:T(8,128)(2,1)S(1)} %bitcast.44), custom_call_target="tpu_custom_call" | custom-call | tf_op jit(solution)/shard_map/graph_partial/pallas_call | solution.py:71
  61.2 25.0 %all_to_all.16 = bf16[16,64,768]{2,1,0:T(8,128)(2,1)S(1)} all-to-all(bf16[16,64,768]{2,1,0:T(8,128)(2,1)S(1)} %graph_partial.4), channel_id=1, replica_groups=mesh['brow'=8,'bcol'=16] {'bcol'}, dimensions={0} | all-to-all | bytes 3145728 | tf_op jit(solution)/shard_map/all_to_all | solution.py:355
  87.2 1.8 %collective-permute-start.9 = (bf16[32,768]{1,0:T(8,128)(2,1)S(1)}, bf16[32,768]{1,0:T(8,128)(2,1)S(1)}, u32[]{:S(2)}, u32[]{:S(2)}) collective-permute-start(bf16[32,768]{1,0:T(8,128)(2,1)S(1)} %get-tuple-element.7), channel_id=1, source_target_pairs={{0,32},{16,48},{32,64},{48,80},{64,96},{80,112},{96,0},{112,16},{1... | collective-permute-start | bytes 147464 | tf_op jit(solution)/shard_map/ppermute | solution.py:322
  92.0 4.1 %collective-permute-start.11 = (bf16[4,32,768]{2,1,0:T(8,128)(2,1)S(1)}, bf16[4,32,768]{2,1,0:T(8,128)(2,1)S(1)}, u32[]{:S(2)}, u32[]{:S(2)}) collective-permute-start(bf16[4,32,768]{2,1,0:T(8,128)(2,1)S(1)} %pad_maximum_fusion.2.near_ref), channel_id=1, source_target_pairs={{0,16},{16,0},{32,48},{48,32},{64,80},{80,64},{96,112},{112,96},{1... | collective-permute-start | bytes 589832 | tf_op jit(solution)/shard_map/ppermute | solution.py:324
  97.2 2.5 %graph_partial.5 = bf16[16,32,768]{2,1,0:T(8,128)(2,1)} custom-call(s32[81]{0:T(128)S(1)} %pad_add_fusion.table_ref, bf16[4,32,768]{2,1,0:T(8,128)(2,1)S(1)} %pad_maximum_fusion.2.near_ref, bf16[4,32,768]{2,1,0:T(8,128)(2,1)S(1)} %collective-permute-done.11.far_ref, bf16[40,256,256]{2,1,0:T(8,128)(2,1)S(1)} %bitcast.45), custom_call_target="tpu_custom_call" | custom-call | tf_op jit(solution)/shard_map/graph_partial/pallas_call | solution.py:71
  99.6 3.8 %all-to-all-start.2 = ((bf16[16,32,768]{2,1,0:T(8,128)(2,1)}), bf16[16,32,768]{2,1,0:T(8,128)(2,1)S(1)}, u32[]{:S(2)}, u32[]{:S(2)}) async-start(bf16[16,32,768]{2,1,0:T(8,128)(2,1)} %graph_partial.5), calls=%async_computation.2 | async-start | bytes 1572864 | tf_op jit(solution)/shard_map/all_to_all | solution.py:355
  104.4 11.8 %all-to-all-done.2 = bf16[16,32,768]{2,1,0:T(8,128)(2,1)S(1)} async-done(((bf16[16,32,768]{2,1,0:T(8,128)(2,1)}), bf16[16,32,768]{2,1,0:T(8,128)(2,1)S(1)}, u32[]{:S(2)}, u32[]{:S(2)}) %all-to-all-start.2) | async-done | bytes 786464 | tf_op jit(solution)/shard_map/all_to_all | solution.py:355
  116.9 2.8 %collective-permute-start.12 = (f32[104,128]{1,0:T(8,128)S(1)}, f32[104,128]{1,0:T(8,128)S(1)}, u32[]{:S(2)}, u32[]{:S(2)}) collective-permute-start(f32[104,128]{1,0:T(8,128)S(1)} %constant_dynamic-slice_fusion), channel_id=1, source_target_pairs={{0,16},{16,0},{32,48},{48,32},{64,80},{80,64},{96,112},{112,96},{1... | collective-permute-start | bytes 159752 | tf_op jit(solution)/shard_map/ppermute | solution.py:332
  122.1 2.2 %collective-permute-start.13 = (f32[104,128]{1,0:T(8,128)S(1)}, f32[104,128]{1,0:T(8,128)S(1)}, u32[]{:S(2)}, u32[]{:S(2)}) collective-permute-start(f32[104,128]{1,0:T(8,128)S(1)} %dynamic-slice_add_fusion), channel_id=1, source_target_pairs={{0,12},{1,13},{2,14},{3,15},{4,0},{5,1},{6,2},{7,3},{8,4},{9,5},{1... | collective-permute-start | bytes 159752 | tf_op jit(solution)/shard_map/ppermute | solution.py:334
  126.7 2.4 %collective-permute-start.17 = (f32[104,128]{1,0:T(8,128)S(1)}, f32[104,128]{1,0:T(8,128)S(1)}, u32[]{:S(2)}, u32[]{:S(2)}) collective-permute-start(f32[104,128]{1,0:T(8,128)S(1)} %add_add_fusion.2), channel_id=1, source_target_pairs={{0,64},{16,80},{32,96},{48,112},{64,0},{80,16},{96,32},{112,48},{1... | collective-permute-start | bytes 159752 | tf_op jit(solution)/shard_map/ppermute | solution.py:334
  130.1 1.6 %collective-permute-start.16 = (f32[104,128]{1,0:T(8,128)S(1)}, f32[104,128]{1,0:T(8,128)S(1)}, u32[]{:S(2)}, u32[]{:S(2)}) collective-permute-start(f32[104,128]{1,0:T(8,128)S(1)} %add_add_fusion.2), channel_id=1, source_target_pairs={{0,96},{16,112},{32,0},{48,16},{64,32},{80,48},{96,64},{112,80},{1... | collective-permute-start | bytes 159752 | tf_op jit(solution)/shard_map/ppermute | solution.py:334
  131.8 1.7 %collective-permute-done.18 = f32[104,128]{1,0:T(8,128)S(1)} collective-permute-done((f32[104,128]{1,0:T(8,128)S(1)}, f32[104,128]{1,0:T(8,128)S(1)}, u32[]{:S(2)}, u32[]{:S(2)}) %collective-permute-start.18) | collective-permute-done | bytes 53280 | tf_op jit(solution)/shard_map/ppermute | solution.py:334
  134.4 2.7 %collective-permute-start.19 = (f32[104,128]{1,0:T(8,128)S(1)}, f32[104,128]{1,0:T(8,128)S(1)}, u32[]{:S(2)}, u32[]{:S(2)}) collective-permute-start(f32[104,128]{1,0:T(8,128)S(1)} %add_add_fusion.1), channel_id=1, source_target_pairs={{0,3},{1,0},{2,1},{3,2},{4,7},{5,4},{6,5},{7,6},{8,11},{9,8},{10,9... | collective-permute-start | bytes 159752 | tf_op jit(solution)/shard_map/ppermute | solution.py:334
  138.7 3.9 %collective-permute-start.22 = (f32[104,128]{1,0:T(8,128)S(1)}, f32[104,128]{1,0:T(8,128)S(1)}, u32[]{:S(2)}, u32[]{:S(2)}) collective-permute-start(f32[104,128]{1,0:T(8,128)S(1)} %add_add_fusion.mine_ref), channel_id=1, source_target_pairs={{0,16},{16,0},{32,48},{48,32},{64,80},{80,64},{96,112},{112,96},{1... | collective-permute-start | bytes 159752 | tf_op jit(solution)/shard_map/ppermute | solution.py:336
  143.4 18.2 %small_matrices.1 = (f32[32,768]{1,0:T(8,128)}, f32[32,768]{1,0:T(8,128)}, f32[32,768]{1,0:T(8,128)}, f32[32,768]{1,0:T(8,128)}) custom-call(f32[1]{0:T(128)S(6)} %copy.13.cut_ref, s32[1]{0:T(128)} %bitcast.core_ref, f32[104,128]{1,0:T(8,128)S(1)} %add_add_fusion.mine_ref, f32[104,128]{1,0:T(8,128)S(1)} %collective-permute-done.22.other_ref, ...), custom_call_target="tpu_custom_call" | custom-call | tf_op jit(solution)/shard_map/small_matrices/pallas_call | solution.py:253
  (64 shorter events, 23.0 us)
Async XLA Ops:
  1.6 8.1 %collective-permute-start.2 = (bf16[64,768]{1,0:T(8,128)(2,1)S(1)}, bf16[64,768]{1,0:T(8,128)(2,1)S(1)}, u32[]{:S(2)}, u32[]{:S(2)}) collective-permute-start(bf16[64,768]{1,0:T(8,128)(2,1)S(1)} %fusion.1), channel_id=1, source_target_pairs={{0,64},{16,80},{32,96},{48,112},{64,0},{80,16},{96,32},{112,48},{1... | collective-permute-start | bytes 294920 | tf_op jit(solution)/shard_map/ppermute | solution.py:322
  6.1 4.7 %collective-permute-start.1 = (bf16[64,768]{1,0:T(8,128)(2,1)S(1)}, bf16[64,768]{1,0:T(8,128)(2,1)S(1)}, u32[]{:S(2)}, u32[]{:S(2)}) collective-permute-start(bf16[64,768]{1,0:T(8,128)(2,1)S(1)} %fusion.1), channel_id=1, source_target_pairs={{0,32},{16,48},{32,64},{48,80},{64,96},{80,112},{96,0},{112,16},{1... | collective-permute-start | bytes 294920 | tf_op jit(solution)/shard_map/ppermute | solution.py:322
  6.8 4.5 %collective-permute-start = (bf16[64,768]{1,0:T(8,128)(2,1)S(1)}, bf16[64,768]{1,0:T(8,128)(2,1)S(1)}, u32[]{:S(2)}, u32[]{:S(2)}) collective-permute-start(bf16[64,768]{1,0:T(8,128)(2,1)S(1)} %fusion.1), channel_id=1, source_target_pairs={{0,96},{16,112},{32,0},{48,16},{64,32},{80,48},{96,64},{112,80},{1... | collective-permute-start | bytes 294920 | tf_op jit(solution)/shard_map/ppermute | solution.py:322
  11.4 3.1 %collective-permute-start.3 = (bf16[4,64,768]{2,1,0:T(8,128)(2,1)S(1)}, bf16[4,64,768]{2,1,0:T(8,128)(2,1)S(1)}, u32[]{:S(2)}, u32[]{:S(2)}) collective-permute-start(bf16[4,64,768]{2,1,0:T(8,128)(2,1)S(1)} %pad_maximum_fusion.near_ref), channel_id=1, source_target_pairs={{0,16},{16,0},{32,48},{48,32},{64,80},{80,64},{96,112},{112,96},{1... | collective-permute-start | bytes 1179656 | tf_op jit(solution)/shard_map/ppermute | solution.py:324
  47.9 5.2 %collective-permute-start.6 = (bf16[64,768]{1,0:T(8,128)(2,1)S(1)}, bf16[64,768]{1,0:T(8,128)(2,1)S(1)}, u32[]{:S(2)}, u32[]{:S(2)}) collective-permute-start(bf16[64,768]{1,0:T(8,128)(2,1)S(1)} %get-tuple-element.4), channel_id=1, source_target_pairs={{0,64},{16,80},{32,96},{48,112},{64,0},{80,16},{96,32},{112,48},{1... | collective-permute-start | bytes 294920 | tf_op jit(solution)/shard_map/ppermute | solution.py:322
  48.0 5.8 %collective-permute-start.5 = (bf16[64,768]{1,0:T(8,128)(2,1)S(1)}, bf16[64,768]{1,0:T(8,128)(2,1)S(1)}, u32[]{:S(2)}, u32[]{:S(2)}) collective-permute-start(bf16[64,768]{1,0:T(8,128)(2,1)S(1)} %get-tuple-element.4), channel_id=1, source_target_pairs={{0,32},{16,48},{32,64},{48,80},{64,96},{80,112},{96,0},{112,16},{1... | collective-permute-start | bytes 294920 | tf_op jit(solution)/shard_map/ppermute | solution.py:322
  50.8 4.0 %collective-permute-start.4 = (bf16[64,768]{1,0:T(8,128)(2,1)S(1)}, bf16[64,768]{1,0:T(8,128)(2,1)S(1)}, u32[]{:S(2)}, u32[]{:S(2)}) collective-permute-start(bf16[64,768]{1,0:T(8,128)(2,1)S(1)} %get-tuple-element.4), channel_id=1, source_target_pairs={{0,96},{16,112},{32,0},{48,16},{64,32},{80,48},{96,64},{112,80},{1... | collective-permute-start | bytes 294920 | tf_op jit(solution)/shard_map/ppermute | solution.py:322
  54.8 4.5 %collective-permute-start.7 = (bf16[4,64,768]{2,1,0:T(8,128)(2,1)S(1)}, bf16[4,64,768]{2,1,0:T(8,128)(2,1)S(1)}, u32[]{:S(2)}, u32[]{:S(2)}) collective-permute-start(bf16[4,64,768]{2,1,0:T(8,128)(2,1)S(1)} %pad_maximum_fusion.1.near_ref), channel_id=1, source_target_pairs={{0,16},{16,0},{32,48},{48,32},{64,80},{80,64},{96,112},{112,96},{1... | collective-permute-start | bytes 1179656 | tf_op jit(solution)/shard_map/ppermute | solution.py:324
  86.4 4.5 %collective-permute-start.10 = (bf16[32,768]{1,0:T(8,128)(2,1)S(1)}, bf16[32,768]{1,0:T(8,128)(2,1)S(1)}, u32[]{:S(2)}, u32[]{:S(2)}) collective-permute-start(bf16[32,768]{1,0:T(8,128)(2,1)S(1)} %get-tuple-element.7), channel_id=1, source_target_pairs={{0,64},{16,80},{32,96},{48,112},{64,0},{80,16},{96,32},{112,48},{1... | collective-permute-start | bytes 147464 | tf_op jit(solution)/shard_map/ppermute | solution.py:322
  87.2 4.2 %collective-permute-start.9 = (bf16[32,768]{1,0:T(8,128)(2,1)S(1)}, bf16[32,768]{1,0:T(8,128)(2,1)S(1)}, u32[]{:S(2)}, u32[]{:S(2)}) collective-permute-start(bf16[32,768]{1,0:T(8,128)(2,1)S(1)} %get-tuple-element.7), channel_id=1, source_target_pairs={{0,32},{16,48},{32,64},{48,80},{64,96},{80,112},{96,0},{112,16},{1... | collective-permute-start | bytes 147464 | tf_op jit(solution)/shard_map/ppermute | solution.py:322
  89.0 2.9 %collective-permute-start.8 = (bf16[32,768]{1,0:T(8,128)(2,1)S(1)}, bf16[32,768]{1,0:T(8,128)(2,1)S(1)}, u32[]{:S(2)}, u32[]{:S(2)}) collective-permute-start(bf16[32,768]{1,0:T(8,128)(2,1)S(1)} %get-tuple-element.7), channel_id=1, source_target_pairs={{0,96},{16,112},{32,0},{48,16},{64,32},{80,48},{96,64},{112,80},{1... | collective-permute-start | bytes 147464 | tf_op jit(solution)/shard_map/ppermute | solution.py:322
  92.0 5.2 %collective-permute-start.11 = (bf16[4,32,768]{2,1,0:T(8,128)(2,1)S(1)}, bf16[4,32,768]{2,1,0:T(8,128)(2,1)S(1)}, u32[]{:S(2)}, u32[]{:S(2)}) collective-permute-start(bf16[4,32,768]{2,1,0:T(8,128)(2,1)S(1)} %pad_maximum_fusion.2.near_ref), channel_id=1, source_target_pairs={{0,16},{16,0},{32,48},{48,32},{64,80},{80,64},{96,112},{112,96},{1... | collective-permute-start | bytes 589832 | tf_op jit(solution)/shard_map/ppermute | solution.py:324
  99.6 16.6 %all-to-all-start.2 = ((bf16[16,32,768]{2,1,0:T(8,128)(2,1)}), bf16[16,32,768]{2,1,0:T(8,128)(2,1)S(1)}, u32[]{:S(2)}, u32[]{:S(2)}) async-start(bf16[16,32,768]{2,1,0:T(8,128)(2,1)} %graph_partial.5), calls=%async_computation.2 | async-start | bytes 1572864 | tf_op jit(solution)/shard_map/all_to_all | solution.py:355
  116.9 3.7 %collective-permute-start.12 = (f32[104,128]{1,0:T(8,128)S(1)}, f32[104,128]{1,0:T(8,128)S(1)}, u32[]{:S(2)}, u32[]{:S(2)}) collective-permute-start(f32[104,128]{1,0:T(8,128)S(1)} %constant_dynamic-slice_fusion), channel_id=1, source_target_pairs={{0,16},{16,0},{32,48},{48,32},{64,80},{80,64},{96,112},{112,96},{1... | collective-permute-start | bytes 159752 | tf_op jit(solution)/shard_map/ppermute | solution.py:332
  120.7 4.8 %collective-permute-start.14 = (f32[104,128]{1,0:T(8,128)S(1)}, f32[104,128]{1,0:T(8,128)S(1)}, u32[]{:S(2)}, u32[]{:S(2)}) collective-permute-start(f32[104,128]{1,0:T(8,128)S(1)} %dynamic-slice_add_fusion), channel_id=1, source_target_pairs={{0,8},{1,9},{2,10},{3,11},{4,12},{5,13},{6,14},{7,15},{8,0},{9,1},... | collective-permute-start | bytes 159752 | tf_op jit(solution)/shard_map/ppermute | solution.py:334
  121.6 5.0 %collective-permute-start.15 = (f32[104,128]{1,0:T(8,128)S(1)}, f32[104,128]{1,0:T(8,128)S(1)}, u32[]{:S(2)}, u32[]{:S(2)}) collective-permute-start(f32[104,128]{1,0:T(8,128)S(1)} %dynamic-slice_add_fusion), channel_id=1, source_target_pairs={{0,4},{1,5},{2,6},{3,7},{4,8},{5,9},{6,10},{7,11},{8,12},{9,13},{1... | collective-permute-start | bytes 159752 | tf_op jit(solution)/shard_map/ppermute | solution.py:334
  122.1 4.5 %collective-permute-start.13 = (f32[104,128]{1,0:T(8,128)S(1)}, f32[104,128]{1,0:T(8,128)S(1)}, u32[]{:S(2)}, u32[]{:S(2)}) collective-permute-start(f32[104,128]{1,0:T(8,128)S(1)} %dynamic-slice_add_fusion), channel_id=1, source_target_pairs={{0,12},{1,13},{2,14},{3,15},{4,0},{5,1},{6,2},{7,3},{8,4},{9,5},{1... | collective-permute-start | bytes 159752 | tf_op jit(solution)/shard_map/ppermute | solution.py:334
  126.7 5.1 %collective-permute-start.17 = (f32[104,128]{1,0:T(8,128)S(1)}, f32[104,128]{1,0:T(8,128)S(1)}, u32[]{:S(2)}, u32[]{:S(2)}) collective-permute-start(f32[104,128]{1,0:T(8,128)S(1)} %add_add_fusion.2), channel_id=1, source_target_pairs={{0,64},{16,80},{32,96},{48,112},{64,0},{80,16},{96,32},{112,48},{1... | collective-permute-start | bytes 159752 | tf_op jit(solution)/shard_map/ppermute | solution.py:334
  129.1 4.4 %collective-permute-start.18 = (f32[104,128]{1,0:T(8,128)S(1)}, f32[104,128]{1,0:T(8,128)S(1)}, u32[]{:S(2)}, u32[]{:S(2)}) collective-permute-start(f32[104,128]{1,0:T(8,128)S(1)} %add_add_fusion.2), channel_id=1, source_target_pairs={{0,32},{16,48},{32,64},{48,80},{64,96},{80,112},{96,0},{112,16},{1... | collective-permute-start | bytes 159752 | tf_op jit(solution)/shard_map/ppermute | solution.py:334
  130.1 3.4 %collective-permute-start.16 = (f32[104,128]{1,0:T(8,128)S(1)}, f32[104,128]{1,0:T(8,128)S(1)}, u32[]{:S(2)}, u32[]{:S(2)}) collective-permute-start(f32[104,128]{1,0:T(8,128)S(1)} %add_add_fusion.2), channel_id=1, source_target_pairs={{0,96},{16,112},{32,0},{48,16},{64,32},{80,48},{96,64},{112,80},{1... | collective-permute-start | bytes 159752 | tf_op jit(solution)/shard_map/ppermute | solution.py:334
  133.5 4.6 %collective-permute-start.20 = (f32[104,128]{1,0:T(8,128)S(1)}, f32[104,128]{1,0:T(8,128)S(1)}, u32[]{:S(2)}, u32[]{:S(2)}) collective-permute-start(f32[104,128]{1,0:T(8,128)S(1)} %add_add_fusion.1), channel_id=1, source_target_pairs={{0,2},{1,3},{2,0},{3,1},{4,6},{5,7},{6,4},{7,5},{8,10},{9,11},{10,... | collective-permute-start | bytes 159752 | tf_op jit(solution)/shard_map/ppermute | solution.py:334
  134.4 4.2 %collective-permute-start.21 = (f32[104,128]{1,0:T(8,128)S(1)}, f32[104,128]{1,0:T(8,128)S(1)}, u32[]{:S(2)}, u32[]{:S(2)}) collective-permute-start(f32[104,128]{1,0:T(8,128)S(1)} %add_add_fusion.1), channel_id=1, source_target_pairs={{0,1},{1,2},{2,3},{3,0},{4,5},{5,6},{6,7},{7,4},{8,9},{9,10},{10,1... | collective-permute-start | bytes 159752 | tf_op jit(solution)/shard_map/ppermute | solution.py:334
  134.4 4.2 %collective-permute-start.19 = (f32[104,128]{1,0:T(8,128)S(1)}, f32[104,128]{1,0:T(8,128)S(1)}, u32[]{:S(2)}, u32[]{:S(2)}) collective-permute-start(f32[104,128]{1,0:T(8,128)S(1)} %add_add_fusion.1), channel_id=1, source_target_pairs={{0,3},{1,0},{2,1},{3,2},{4,7},{5,4},{6,5},{7,6},{8,11},{9,8},{10,9... | collective-permute-start | bytes 159752 | tf_op jit(solution)/shard_map/ppermute | solution.py:334
  138.7 4.8 %collective-permute-start.22 = (f32[104,128]{1,0:T(8,128)S(1)}, f32[104,128]{1,0:T(8,128)S(1)}, u32[]{:S(2)}, u32[]{:S(2)}) collective-permute-start(f32[104,128]{1,0:T(8,128)S(1)} %add_add_fusion.mine_ref), channel_id=1, source_target_pairs={{0,16},{16,0},{32,48},{48,32},{64,80},{80,64},{96,112},{112,96},{1... | collective-permute-start | bytes 159752 | tf_op jit(solution)/shard_map/ppermute | solution.py:336
  (5 other events, 98.1 us)

commit v6 on v5

--- a/solution.py
+++ b/solution.py
@@ -25,7 +25,8 @@
     return lax.dot_general(a, b, (((1,), (1,)), ((), ())), precision=HIGH, preferred_element_type=F32)
 
 
-def graph_kernel(table_ref, near_ref, far_ref, blocks_ref, out_ref, panel, acc, *own):
+def graph_kernel(n_out, table_ref, near_ref, far_ref, blocks_ref, *rest):
+    outs, (panel, acc, *own) = rest[:n_out], rest[n_out:]
     n_slots = blocks_ref.shape[0]
     live = table_ref[2 * n_slots]
     sub = panel.shape[0] // 8
@@ -58,21 +59,35 @@
             for s, prod in zip(slots, prods):
                 row = table_ref[s]
                 acc[row] = acc[row] + prod
-    for j in range(out_ref.shape[0]):
-        for q in range(sub):
-            out_ref[j, :, q * 256:(q + 1) * 256] = acc[j * sub + q].astype(BF)
-
-
-def graph_partial(table, near, far, blocks, owners, fetched):
+    if n_out == 1:
+        out_ref = outs[0]
+        for j in range(out_ref.shape[0]):
+            for q in range(sub):
+                out_ref[j, :, q * 256:(q + 1) * 256] = acc[j * sub + q].astype(BF)
+        return
+    mx, my = table_ref[2 * n_slots + 1], table_ref[2 * n_slots + 2]
+    half = acc.shape[1] // 2
+    for k in range(4):
+        for m in range(4):
+            for_x = jnp.bitwise_and(mx + k, 3) * 4 + jnp.bitwise_and(my + m, 3)
+            for_p = jnp.bitwise_and(mx + m, 3) * 4 + jnp.bitwise_and(my + k, 3)
+            for q in range(sub):
+                columns = pl.ds(q * 256, 256)
+                outs[k][m, :, columns] = acc[for_x * sub + q, :half].astype(BF)
+                outs[4 + k][m, :, columns] = acc[for_p * sub + q, half:].astype(BF)
+
+
+def graph_partial(table, near, far, blocks, owners, fetched, split=False):
     n_slots, side, _ = blocks.shape
     r, width = near.shape[1:]
     sub = width // side
     own = [pltpu.VMEM((n_slots, side, side), BF), pltpu.SemaphoreType.DMA((n_slots // CHUNK,))]
     return pl.pallas_call(
-        graph_kernel,
-        out_shape=jax.ShapeDtypeStruct((owners, r, width), BF),
+        functools.partial(graph_kernel, 8 if split else 1),
+        out_shape=([jax.ShapeDtypeStruct((4, r // 2, width), BF)] * 8 if split
+                   else jax.ShapeDtypeStruct((owners, r, width), BF)),
         in_specs=[SMEM] + [VMEM] * 2 + [pl.BlockSpec(memory_space=pltpu.HBM) if fetched else VMEM],
-        out_specs=VMEM,
+        out_specs=[VMEM] * 8 if split else VMEM,
         scratch_shapes=[
             pltpu.VMEM((8 * sub, r, side), BF),
             pltpu.VMEM((owners * sub + 1, r, side), F32),
@@ -320,8 +335,24 @@
 
 def gather_brow(v):
     got = {k: lax.ppermute(v, "brow", z_turn(k)) for k in (3, 2, 1)}
-    near = jnp.stack([v, got[3], got[1], got[2]])
+    near = jnp.stack([v, got[2], got[1], got[3]])
     return near, lax.ppermute(near, "brow", CORE)
+
+
+def turned_sum(pieces, turns):
+    got = [[lax.ppermute(p[k], "bcol", turn(k)) for p, turn in zip(pieces, turns)] for k in (2, 1, 3)]
+    return [p[0].astype(F32) + ((g[0].astype(F32) + g[1].astype(F32)) + g[2].astype(F32))
+            for p, g in zip(pieces, zip(*got))]
+
+
+def two_phases(x_parts, p_parts):
+    x, p = turned_sum([x_parts, p_parts], [x_turn, y_turn])
+    x, p = x.astype(F32), p.astype(F32)
+    x_own, p_own = x[0], p[0]
+    x, p = x.astype(BF), p.astype(BF)
+    x = [x_own] + [x[k] for k in (1, 2, 3)]
+    p = [p_own] + [p[k] for k in (1, 2, 3)]
+    return turned_sum([x, p], [y_turn, x_turn])
 
 
 def sum_all(g):
@@ -331,7 +362,7 @@
     other = lax.dynamic_slice_in_dim(g, (1 - me) * half, half, 0)
     v = mine + lax.ppermute(other, "brow", CORE)
     for axis, turn in (("bcol", x_turn), ("brow", z_turn), ("bcol", y_turn)):
-        a, b, c = [lax.ppermute(v, axis, turn(k)) for k in (3, 2, 1)]
+        a, b, c = [lax.ppermute(v, axis, turn(k)) for k in (2, 1, 3)]
         v = (v + a) + (b + c)
     return v, lax.ppermute(v, "brow", CORE)
 
@@ -345,9 +376,10 @@
     rows, source, live = pattern_rows[0, 0], pattern_cols[0, 0] // sub, live_count[0, 0]
     rows = jnp.where(jnp.arange(rows.shape[0]) < live, rows, owners * sub)
     turn = (brow // 2 - source // 2) % 4
-    place = jnp.where(turn > 0, turn % 3 + 1, 0)
+    place = jnp.where(turn == 1, 2, jnp.where(turn == 2, 1, turn))
     spots = (place + 4 * ((brow - source) % 2)) * sub + pattern_cols[0, 0] % sub
-    table = jnp.concatenate([rows, spots, live.reshape(1)])
+    bcol = lax.axis_index("bcol")
+    table = jnp.concatenate([rows, spots, jnp.stack([live, bcol // 4, bcol % 4])])
 
     def apply_graph(v, fetched=False):
         near, far = gather_brow((degree_scale * v).astype(BF))
@@ -355,10 +387,17 @@
         got = lax.all_to_all(part, "bcol", 0, 0)
         return degree_scale * jnp.sum(got.astype(F32), axis=0)
 
-    k1 = apply_graph(jnp.concatenate([eigen_block, direction], 0), True)
-    k2 = apply_graph(k1)
-    k3 = apply_graph(k2[:wanted])
-    parts = [eigen_block, direction, k1[:wanted], k1[wanted:], k2[:wanted], k2[wanted:], k3]
+    def apply_both(v, fetched=False):
+        near, far = gather_brow((degree_scale * v).astype(BF))
+        parts = graph_partial(table, near, far, block_set, owners, fetched, True)
+        found = two_phases(parts[:4], parts[4:])
+        return [degree_scale * f for f in found]
+
+    x0, p0 = eigen_block, direction
+    x1, p1 = apply_both(jnp.concatenate([x0, p0], 0), True)
+    x2, p2 = apply_both(jnp.concatenate([x1, p1], 0))
+    x3 = apply_graph(x2)
+    parts = [x0, p0, x1, p1, x2, p2, x3]
     mine, other = sum_all(packed_gram(parts))
     return tuple(small(cutoff, (brow % 2).reshape(1), mine, other, parts))
 

time: 162 us -> 159 us (0.981)
  blocking collectives: 54.5 us -> 0 us
  starting transfers between devices: 45.3 us -> 89 us
  waiting for transfers between devices: 28.6 us -> 35.6 us
    all_to_all x2 -> x0, blocking collectives: 54.5 us -> none  [apply_graph(): got = lax.all_to_all(part, 'bcol', 0, 0)]
    ppermute x9 -> x33, starting transfers between devices: 12.3 us -> 51 us  [the longest x24 39.8 us: turned_sum(): lax.ppermute(p[k], 'bcol', turn(k))]
    ppermute x9 -> x33, waiting for transfers between devices: 5.66 us -> 13.5 us  [the longest x24 6.92 us: turned_sum(): lax.ppermute(p[k], 'bcol', turn(k))]
    convert_element_type x0 -> x8, other arithmetic: none -> 2.36 us  [the longest x4 1.96 us: apply_both(): near, far = gather_brow((degree_scale * v).astype(BF))]
    all_to_all x1, starting transfers between devices: 3.8 us -> 5.74 us  [apply_graph(): got = lax.all_to_all(part, 'bcol', 0, 0)]
    convert_element_type x4 -> x1, other arithmetic: 1.96 us -> 0.06 us  [apply_graph(): near, far = gather_brow((degree_scale * v).astype(BF))]
    ppermute x3, starting transfers between devices: 8.88 us -> 10.7 us  [gather_brow(): return (near, lax.ppermute(near, 'brow', CORE))]
  transfers between devices with their start and end apart: 24 -> 48, of which waited for: 18 -> 28; matrix products, arithmetic and copies ran while one was open for 1% -> 1% of each run, Pallas kernels for 1% -> 1%
where the time goes in v6:
time: 159 us
  starting transfers between devices  89 us (56%)
  waiting for transfers between devices  35.6 us (22%)
  Pallas kernels  28.5 us (18%)
  other arithmetic  3.5 us (2%)
  between operations  2.19 us (1%)
    ppermute x24, starting transfers between devices, turned_sum(): lax.ppermute(p[k], 'bcol', turn(k))  39.8 us
    pallas_call x1, Pallas kernels, small(): pl.pallas_call(functools.partial(small_kernel, w), out_shape=[jax.ShapeDt...  18.2 us
    ppermute x9, starting transfers between devices, gather_brow(): got = {k: lax.ppermute(v, 'brow', z_turn(k)) for k in (3, 2, 1)}  14.4 us
    all_to_all x1, waiting for transfers between devices, apply_graph(): got = lax.all_to_all(part, 'bcol', 0, 0)  11.8 us
    ppermute x9, starting transfers between devices, sum_all(): a, b, c = [lax.ppermute(v, axis, turn(k)) for k in (2, 1, 3)]  11.3 us
    ppermute x3, starting transfers between devices, gather_brow(): return (near, lax.ppermute(near, 'brow', CORE))  10.7 us
    pallas_call x3, Pallas kernels, graph_partial(): pl.pallas_call(functools.partial(graph_kernel, 8 if split else 1), out_sh...  8.79 us
    ppermute x24, waiting for transfers between devices, turned_sum(): lax.ppermute(p[k], 'bcol', turn(k))  6.92 us
  transfers between devices with their start and end apart: 48, of which 28 were waited for; matrix products, arithmetic and copies ran while one was open for 1% of the time, Pallas kernels for 1%

profile of v6, /device:TPU:1, one launch (start us, length us, event | category | flops | bytes accessed | tf_op | source)
XLA Modules:
  0.0 159.0 jit_solution(18057953480803946208)
XLA Ops:
  1.6 4.5 %collective-permute-start = (bf16[64,768]{1,0:T(8,128)(2,1)S(1)}, bf16[64,768]{1,0:T(8,128)(2,1)S(1)}, u32[]{:S(2)}, u32[]{:S(2)}) collective-permute-start(bf16[64,768]{1,0:T(8,128)(2,1)S(1)} %fusion.1), channel_id=1, source_target_pairs={{0,64},{16,80},{32,96},{48,112},{64,0},{80,16},{96,32},{112,48},{1... | collective-permute-start | bytes 294920 | tf_op jit(solution)/shard_map/ppermute | solution.py:337
  6.8 1.9 %collective-permute-start.2 = (bf16[64,768]{1,0:T(8,128)(2,1)S(1)}, bf16[64,768]{1,0:T(8,128)(2,1)S(1)}, u32[]{:S(2)}, u32[]{:S(2)}) collective-permute-start(bf16[64,768]{1,0:T(8,128)(2,1)S(1)} %fusion.1), channel_id=1, source_target_pairs={{0,96},{16,112},{32,0},{48,16},{64,32},{80,48},{96,64},{112,80},{1... | collective-permute-start | bytes 294920 | tf_op jit(solution)/shard_map/ppermute | solution.py:337
  14.5 3.6 %graph_partial.3 = (bf16[4,32,768]{2,1,0:T(8,128)(2,1)S(1)}, bf16[4,32,768]{2,1,0:T(8,128)(2,1)S(1)}, bf16[4,32,768]{2,1,0:T(8,128)(2,1)S(1)}, bf16[4,32,768]{2,...) custom-call(s32[83]{0:T(128)S(1)} %concatenate.35.table_ref, ...), custom_call_target="tpu_custom_call" | custom-call | tf_op jit(solution)/shard_map/graph_partial/pallas_call | solution.py:85
  18.1 2.8 %collective-permute-start.4 = (bf16[4,32,768]{2,1,0:T(8,128)(2,1)S(1)}, bf16[4,32,768]{2,1,0:T(8,128)(2,1)S(1)}, u32[]{:S(2)}, u32[]{:S(2)}) collective-permute-start(bf16[4,32,768]{2,1,0:T(8,128)(2,1)S(1)} %get-tuple-element.21), channel_id=1, source_target_pairs={{0,8},{1,9},{2,10},{3,11},{4,12},{5,13},{6,14},{7,15},{8,0},{9,1},... | collective-permute-start | bytes 589832 | tf_op jit(solution)/shard_map/ppermute | solution.py:343
  21.2 2.4 %collective-permute-start.6 = (bf16[4,32,768]{2,1,0:T(8,128)(2,1)S(1)}, bf16[4,32,768]{2,1,0:T(8,128)(2,1)S(1)}, u32[]{:S(2)}, u32[]{:S(2)}) collective-permute-start(bf16[4,32,768]{2,1,0:T(8,128)(2,1)S(1)} %get-tuple-element.23), channel_id=1, source_target_pairs={{0,12},{1,13},{2,14},{3,15},{4,0},{5,1},{6,2},{7,3},{8,4},{9,5},{1... | collective-permute-start | bytes 589832 | tf_op jit(solution)/shard_map/ppermute | solution.py:343
  23.6 2.5 %collective-permute-start.10 = (bf16[4,32,768]{2,1,0:T(8,128)(2,1)S(1)}, bf16[4,32,768]{2,1,0:T(8,128)(2,1)S(1)}, u32[]{:S(2)}, u32[]{:S(2)}) collective-permute-start(bf16[4,32,768]{2,1,0:T(8,128)(2,1)S(1)} %get-tuple-element.25), channel_id=1, source_target_pairs={{0,2},{1,3},{2,0},{3,1},{4,6},{5,7},{6,4},{7,5},{8,10},{9,11},{10,... | collective-permute-start | bytes 589832 | tf_op jit(solution)/shard_map/ppermute | solution.py:343
  26.5 3.5 %collective-permute-start.12 = (bf16[4,32,768]{2,1,0:T(8,128)(2,1)S(1)}, bf16[4,32,768]{2,1,0:T(8,128)(2,1)S(1)}, u32[]{:S(2)}, u32[]{:S(2)}) collective-permute-start(bf16[4,32,768]{2,1,0:T(8,128)(2,1)S(1)} %get-tuple-element.27), channel_id=1, source_target_pairs={{0,3},{1,0},{2,1},{3,2},{4,7},{5,4},{6,5},{7,6},{8,11},{9,8},{10,9... | collective-permute-start | bytes 589832 | tf_op jit(solution)/shard_map/ppermute | solution.py:343
  30.9 2.9 %collective-permute-start.7 = (bf16[32,768]{1,0:T(8,128)(2,1)S(1)}, bf16[32,768]{1,0:T(8,128)(2,1)S(1)}, u32[]{:S(2)}, u32[]{:S(2)}) collective-permute-start(bf16[32,768]{1,0:T(8,128)(2,1)S(1)} %get-tuple-element.55), channel_id=1, source_target_pairs={{0,2},{1,3},{2,0},{3,1},{4,6},{5,7},{6,4},{7,5},{8,10},{9,11},{10,... | collective-permute-start | bytes 147464 | tf_op jit(solution)/shard_map/ppermute | solution.py:343
  44.5 2.1 %collective-permute-start.17 = (bf16[64,768]{1,0:T(8,128)(2,1)S(1)}, bf16[64,768]{1,0:T(8,128)(2,1)S(1)}, u32[]{:S(2)}, u32[]{:S(2)}) collective-permute-start(bf16[64,768]{1,0:T(8,128)(2,1)S(1)} %fusion.3), channel_id=1, source_target_pairs={{0,32},{16,48},{32,64},{48,80},{64,96},{80,112},{96,0},{112,16},{1... | collective-permute-start | bytes 294920 | tf_op jit(solution)/shard_map/ppermute | solution.py:337
  50.4 4.5 %collective-permute-start.19 = (bf16[4,64,768]{2,1,0:T(8,128)(2,1)S(1)}, bf16[4,64,768]{2,1,0:T(8,128)(2,1)S(1)}, u32[]{:S(2)}, u32[]{:S(2)}) collective-permute-start(bf16[4,64,768]{2,1,0:T(8,128)(2,1)S(1)} %pad_maximum_fusion.1.near_ref), channel_id=1, source_target_pairs={{0,16},{16,0},{32,48},{48,32},{64,80},{80,64},{96,112},{112,96},{1... | collective-permute-start | bytes 1179656 | tf_op jit(solution)/shard_map/ppermute | solution.py:339
  56.3 2.3 %graph_partial.4 = (bf16[4,32,768]{2,1,0:T(8,128)(2,1)S(1)}, bf16[4,32,768]{2,1,0:T(8,128)(2,1)S(1)}, bf16[4,32,768]{2,1,0:T(8,128)(2,1)S(1)}, bf16[4,32,768]{2,...) custom-call(s32[83]{0:T(128)S(1)} %concatenate.35.table_ref, ...), custom_call_target="tpu_custom_call" | custom-call | tf_op jit(solution)/shard_map/graph_partial/pallas_call | solution.py:85
  61.4 2.0 %collective-permute-start.20 = (bf16[4,32,768]{2,1,0:T(8,128)(2,1)S(1)}, bf16[4,32,768]{2,1,0:T(8,128)(2,1)S(1)}, u32[]{:S(2)}, u32[]{:S(2)}) collective-permute-start(bf16[4,32,768]{2,1,0:T(8,128)(2,1)S(1)} %get-tuple-element.29), channel_id=1, source_target_pairs={{0,8},{1,9},{2,10},{3,11},{4,12},{5,13},{6,14},{7,15},{8,0},{9,1},... | collective-permute-start | bytes 589832 | tf_op jit(solution)/shard_map/ppermute | solution.py:343
  66.3 3.5 %collective-permute-start.22 = (bf16[4,32,768]{2,1,0:T(8,128)(2,1)S(1)}, bf16[4,32,768]{2,1,0:T(8,128)(2,1)S(1)}, u32[]{:S(2)}, u32[]{:S(2)}) collective-permute-start(bf16[4,32,768]{2,1,0:T(8,128)(2,1)S(1)} %get-tuple-element.31), channel_id=1, source_target_pairs={{0,12},{1,13},{2,14},{3,15},{4,0},{5,1},{6,2},{7,3},{8,4},{9,5},{1... | collective-permute-start | bytes 589832 | tf_op jit(solution)/shard_map/ppermute | solution.py:343
  70.9 2.1 %collective-permute-start.33 = (bf16[32,768]{1,0:T(8,128)(2,1)S(1)}, bf16[32,768]{1,0:T(8,128)(2,1)S(1)}, u32[]{:S(2)}, u32[]{:S(2)}) collective-permute-start(bf16[32,768]{1,0:T(8,128)(2,1)S(1)} %get-tuple-element.46), channel_id=1, source_target_pairs={{0,8},{1,9},{2,10},{3,11},{4,12},{5,13},{6,14},{7,15},{8,0},{9,1},... | collective-permute-start | bytes 147464 | tf_op jit(solution)/shard_map/ppermute | solution.py:343
  77.0 2.0 %collective-permute-start.25 = (bf16[32,768]{1,0:T(8,128)(2,1)S(1)}, bf16[32,768]{1,0:T(8,128)(2,1)S(1)}, u32[]{:S(2)}, u32[]{:S(2)}) collective-permute-start(bf16[32,768]{1,0:T(8,128)(2,1)S(1)} %get-tuple-element.50), channel_id=1, source_target_pairs={{0,3},{1,0},{2,1},{3,2},{4,7},{5,4},{6,5},{7,6},{8,11},{9,8},{10,9... | collective-permute-start | bytes 147464 | tf_op jit(solution)/shard_map/ppermute | solution.py:343
  86.2 4.5 %collective-permute-start.29 = (bf16[4,32,768]{2,1,0:T(8,128)(2,1)S(1)}, bf16[4,32,768]{2,1,0:T(8,128)(2,1)S(1)}, u32[]{:S(2)}, u32[]{:S(2)}) collective-permute-start(bf16[4,32,768]{2,1,0:T(8,128)(2,1)S(1)} %pad_maximum_fusion.2.near_ref), channel_id=1, source_target_pairs={{0,16},{16,0},{32,48},{48,32},{64,80},{80,64},{96,112},{112,96},{1... | collective-permute-start | bytes 589832 | tf_op jit(solution)/shard_map/ppermute | solution.py:339
  91.7 2.9 %graph_partial.5 = bf16[16,32,768]{2,1,0:T(8,128)(2,1)} custom-call(s32[83]{0:T(128)S(1)} %concatenate.35.table_ref, bf16[4,32,768]{2,1,0:T(8,128)(2,1)S(1)} %pad_maximum_fusion.2.near_ref, bf16[4,32,768]{2,1,0:T(8,128)(2,1)S(1)} %collective-permute-done.29.far_ref, bf16[40,256,256]{2,1,0:T(8,128)(2,1)S(1)} %bitcast.92), custom_call_target="tpu_custom_call" | custom-call | tf_op jit(solution)/shard_map/graph_partial/pallas_call | solution.py:85
  94.6 5.7 %all-to-all-start = ((bf16[16,32,768]{2,1,0:T(8,128)(2,1)}), bf16[16,32,768]{2,1,0:T(8,128)(2,1)S(1)}, u32[]{:S(2)}, u32[]{:S(2)}) async-start(bf16[16,32,768]{2,1,0:T(8,128)(2,1)} %graph_partial.5), calls=%async_computation | async-start | bytes 1572864 | tf_op jit(solution)/shard_map/all_to_all | solution.py:387
  101.3 11.8 %all-to-all-done = bf16[16,32,768]{2,1,0:T(8,128)(2,1)S(1)} async-done(((bf16[16,32,768]{2,1,0:T(8,128)(2,1)}), bf16[16,32,768]{2,1,0:T(8,128)(2,1)S(1)}, u32[]{:S(2)}, u32[]{:S(2)}) %all-to-all-start) | async-done | bytes 786464 | tf_op jit(solution)/shard_map/all_to_all | solution.py:387
  113.9 2.8 %collective-permute-start.36 = (f32[104,128]{1,0:T(8,128)S(1)}, f32[104,128]{1,0:T(8,128)S(1)}, u32[]{:S(2)}, u32[]{:S(2)}) collective-permute-start(f32[104,128]{1,0:T(8,128)S(1)} %constant_dynamic-slice_fusion), channel_id=1, source_target_pairs={{0,16},{16,0},{32,48},{48,32},{64,80},{80,64},{96,112},{112,96},{1... | collective-permute-start | bytes 159752 | tf_op jit(solution)/shard_map/ppermute | solution.py:363
  118.9 2.2 %collective-permute-start.39 = (f32[104,128]{1,0:T(8,128)S(1)}, f32[104,128]{1,0:T(8,128)S(1)}, u32[]{:S(2)}, u32[]{:S(2)}) collective-permute-start(f32[104,128]{1,0:T(8,128)S(1)} %dynamic-slice_add_fusion), channel_id=1, source_target_pairs={{0,12},{1,13},{2,14},{3,15},{4,0},{5,1},{6,2},{7,3},{8,4},{9,5},{1... | collective-permute-start | bytes 159752 | tf_op jit(solution)/shard_map/ppermute | solution.py:365
  131.2 2.6 %collective-permute-start.45 = (f32[104,128]{1,0:T(8,128)S(1)}, f32[104,128]{1,0:T(8,128)S(1)}, u32[]{:S(2)}, u32[]{:S(2)}) collective-permute-start(f32[104,128]{1,0:T(8,128)S(1)} %add_add_fusion.5), channel_id=1, source_target_pairs={{0,3},{1,0},{2,1},{3,2},{4,7},{5,4},{6,5},{7,6},{8,11},{9,8},{10,9... | collective-permute-start | bytes 159752 | tf_op jit(solution)/shard_map/ppermute | solution.py:365
  135.5 4.4 %collective-permute-start.46 = (f32[104,128]{1,0:T(8,128)S(1)}, f32[104,128]{1,0:T(8,128)S(1)}, u32[]{:S(2)}, u32[]{:S(2)}) collective-permute-start(f32[104,128]{1,0:T(8,128)S(1)} %add_add_fusion.4.mine_ref), channel_id=1, source_target_pairs={{0,16},{16,0},{32,48},{48,32},{64,80},{80,64},{96,112},{112,96},{1... | collective-permute-start | bytes 159752 | tf_op jit(solution)/shard_map/ppermute | solution.py:367
  140.8 18.2 %small_matrices.1 = (f32[32,768]{1,0:T(8,128)}, f32[32,768]{1,0:T(8,128)}, f32[32,768]{1,0:T(8,128)}, f32[32,768]{1,0:T(8,128)}) custom-call(f32[1]{0:T(128)S(6)} %copy.13.cut_ref, s32[1]{0:T(128)} %bitcast.core_ref, f32[104,128]{1,0:T(8,128)S(1)} %add_add_fusion.4.mine_ref, f32[104,128]{1,0:T(8,128)S(1)} %collective-permute-done.46.other_ref, ...), custom_call_target="tpu_custom_call" | custom-call | tf_op jit(solution)/shard_map/small_matrices/pallas_call | solution.py:268
  (115 shorter events, 59.0 us)
Async XLA Ops:
  1.6 8.2 %collective-permute-start = (bf16[64,768]{1,0:T(8,128)(2,1)S(1)}, bf16[64,768]{1,0:T(8,128)(2,1)S(1)}, u32[]{:S(2)}, u32[]{:S(2)}) collective-permute-start(bf16[64,768]{1,0:T(8,128)(2,1)S(1)} %fusion.1), channel_id=1, source_target_pairs={{0,64},{16,80},{32,96},{48,112},{64,0},{80,16},{96,32},{112,48},{1... | collective-permute-start | bytes 294920 | tf_op jit(solution)/shard_map/ppermute | solution.py:337
  18.1 8.4 %collective-permute-start.4 = (bf16[4,32,768]{2,1,0:T(8,128)(2,1)S(1)}, bf16[4,32,768]{2,1,0:T(8,128)(2,1)S(1)}, u32[]{:S(2)}, u32[]{:S(2)}) collective-permute-start(bf16[4,32,768]{2,1,0:T(8,128)(2,1)S(1)} %get-tuple-element.21), channel_id=1, source_target_pairs={{0,8},{1,9},{2,10},{3,11},{4,12},{5,13},{6,14},{7,15},{8,0},{9,1},... | collective-permute-start | bytes 589832 | tf_op jit(solution)/shard_map/ppermute | solution.py:343
  20.9 9.8 %collective-permute-start.5 = (bf16[4,32,768]{2,1,0:T(8,128)(2,1)S(1)}, bf16[4,32,768]{2,1,0:T(8,128)(2,1)S(1)}, u32[]{:S(2)}, u32[]{:S(2)}) collective-permute-start(bf16[4,32,768]{2,1,0:T(8,128)(2,1)S(1)} %get-tuple-element.22), channel_id=1, source_target_pairs={{0,4},{1,5},{2,6},{3,7},{4,8},{5,9},{6,10},{7,11},{8,12},{9,13},{1... | collective-permute-start | bytes 589832 | tf_op jit(solution)/shard_map/ppermute | solution.py:343
  21.2 9.5 %collective-permute-start.6 = (bf16[4,32,768]{2,1,0:T(8,128)(2,1)S(1)}, bf16[4,32,768]{2,1,0:T(8,128)(2,1)S(1)}, u32[]{:S(2)}, u32[]{:S(2)}) collective-permute-start(bf16[4,32,768]{2,1,0:T(8,128)(2,1)S(1)} %get-tuple-element.23), channel_id=1, source_target_pairs={{0,12},{1,13},{2,14},{3,15},{4,0},{5,1},{6,2},{7,3},{8,4},{9,5},{1... | collective-permute-start | bytes 589832 | tf_op jit(solution)/shard_map/ppermute | solution.py:343
  23.6 11.3 %collective-permute-start.10 = (bf16[4,32,768]{2,1,0:T(8,128)(2,1)S(1)}, bf16[4,32,768]{2,1,0:T(8,128)(2,1)S(1)}, u32[]{:S(2)}, u32[]{:S(2)}) collective-permute-start(bf16[4,32,768]{2,1,0:T(8,128)(2,1)S(1)} %get-tuple-element.25), channel_id=1, source_target_pairs={{0,2},{1,3},{2,0},{3,1},{4,6},{5,7},{6,4},{7,5},{8,10},{9,11},{10,... | collective-permute-start | bytes 589832 | tf_op jit(solution)/shard_map/ppermute | solution.py:343
  26.1 10.5 %collective-permute-start.11 = (bf16[4,32,768]{2,1,0:T(8,128)(2,1)S(1)}, bf16[4,32,768]{2,1,0:T(8,128)(2,1)S(1)}, u32[]{:S(2)}, u32[]{:S(2)}) collective-permute-start(bf16[4,32,768]{2,1,0:T(8,128)(2,1)S(1)} %get-tuple-element.26), channel_id=1, source_target_pairs={{0,1},{1,2},{2,3},{3,0},{4,5},{5,6},{6,7},{7,4},{8,9},{9,10},{10,1... | collective-permute-start | bytes 589832 | tf_op jit(solution)/shard_map/ppermute | solution.py:343
  26.5 10.1 %collective-permute-start.12 = (bf16[4,32,768]{2,1,0:T(8,128)(2,1)S(1)}, bf16[4,32,768]{2,1,0:T(8,128)(2,1)S(1)}, u32[]{:S(2)}, u32[]{:S(2)}) collective-permute-start(bf16[4,32,768]{2,1,0:T(8,128)(2,1)S(1)} %get-tuple-element.27), channel_id=1, source_target_pairs={{0,3},{1,0},{2,1},{3,2},{4,7},{5,4},{6,5},{7,6},{8,11},{9,8},{10,9... | collective-permute-start | bytes 589832 | tf_op jit(solution)/shard_map/ppermute | solution.py:343
  30.9 8.3 %collective-permute-start.7 = (bf16[32,768]{1,0:T(8,128)(2,1)S(1)}, bf16[32,768]{1,0:T(8,128)(2,1)S(1)}, u32[]{:S(2)}, u32[]{:S(2)}) collective-permute-start(bf16[32,768]{1,0:T(8,128)(2,1)S(1)} %get-tuple-element.55), channel_id=1, source_target_pairs={{0,2},{1,3},{2,0},{3,1},{4,6},{5,7},{6,4},{7,5},{8,10},{9,11},{10,... | collective-permute-start | bytes 147464 | tf_op jit(solution)/shard_map/ppermute | solution.py:343
  33.8 7.3 %collective-permute-start.8 = (bf16[32,768]{1,0:T(8,128)(2,1)S(1)}, bf16[32,768]{1,0:T(8,128)(2,1)S(1)}, u32[]{:S(2)}, u32[]{:S(2)}) collective-permute-start(bf16[32,768]{1,0:T(8,128)(2,1)S(1)} %get-tuple-element.57), channel_id=1, source_target_pairs={{0,1},{1,2},{2,3},{3,0},{4,5},{5,6},{6,7},{7,4},{8,9},{9,10},{10,1... | collective-permute-start | bytes 147464 | tf_op jit(solution)/shard_map/ppermute | solution.py:343
  34.9 6.1 %collective-permute-start.9 = (bf16[32,768]{1,0:T(8,128)(2,1)S(1)}, bf16[32,768]{1,0:T(8,128)(2,1)S(1)}, u32[]{:S(2)}, u32[]{:S(2)}) collective-permute-start(bf16[32,768]{1,0:T(8,128)(2,1)S(1)} %get-tuple-element.56), channel_id=1, source_target_pairs={{0,3},{1,0},{2,1},{3,2},{4,7},{5,4},{6,5},{7,6},{8,11},{9,8},{10,9... | collective-permute-start | bytes 147464 | tf_op jit(solution)/shard_map/ppermute | solution.py:343
  43.1 5.1 %collective-permute-start.16 = (bf16[64,768]{1,0:T(8,128)(2,1)S(1)}, bf16[64,768]{1,0:T(8,128)(2,1)S(1)}, u32[]{:S(2)}, u32[]{:S(2)}) collective-permute-start(bf16[64,768]{1,0:T(8,128)(2,1)S(1)} %fusion.3), channel_id=1, source_target_pairs={{0,64},{16,80},{32,96},{48,112},{64,0},{80,16},{96,32},{112,48},{1... | collective-permute-start | bytes 294920 | tf_op jit(solution)/shard_map/ppermute | solution.py:337
  50.4 5.9 %collective-permute-start.19 = (bf16[4,64,768]{2,1,0:T(8,128)(2,1)S(1)}, bf16[4,64,768]{2,1,0:T(8,128)(2,1)S(1)}, u32[]{:S(2)}, u32[]{:S(2)}) collective-permute-start(bf16[4,64,768]{2,1,0:T(8,128)(2,1)S(1)} %pad_maximum_fusion.1.near_ref), channel_id=1, source_target_pairs={{0,16},{16,0},{32,48},{48,32},{64,80},{80,64},{96,112},{112,96},{1... | collective-permute-start | bytes 1179656 | tf_op jit(solution)/shard_map/ppermute | solution.py:339
  58.6 7.7 %collective-permute-start.30 = (bf16[4,32,768]{2,1,0:T(8,128)(2,1)S(1)}, bf16[4,32,768]{2,1,0:T(8,128)(2,1)S(1)}, u32[]{:S(2)}, u32[]{:S(2)}) collective-permute-start(bf16[4,32,768]{2,1,0:T(8,128)(2,1)S(1)} %get-tuple-element.33), channel_id=1, source_target_pairs={{0,2},{1,3},{2,0},{3,1},{4,6},{5,7},{6,4},{7,5},{8,10},{9,11},{10,... | collective-permute-start | bytes 589832 | tf_op jit(solution)/shard_map/ppermute | solution.py:343
  58.7 12.1 %collective-permute-start.31 = (bf16[4,32,768]{2,1,0:T(8,128)(2,1)S(1)}, bf16[4,32,768]{2,1,0:T(8,128)(2,1)S(1)}, u32[]{:S(2)}, u32[]{:S(2)}) collective-permute-start(bf16[4,32,768]{2,1,0:T(8,128)(2,1)S(1)} %get-tuple-element.34), channel_id=1, source_target_pairs={{0,1},{1,2},{2,3},{3,0},{4,5},{5,6},{6,7},{7,4},{8,9},{9,10},{10,1... | collective-permute-start | bytes 589832 | tf_op jit(solution)/shard_map/ppermute | solution.py:343
  60.2 10.6 %collective-permute-start.32 = (bf16[4,32,768]{2,1,0:T(8,128)(2,1)S(1)}, bf16[4,32,768]{2,1,0:T(8,128)(2,1)S(1)}, u32[]{:S(2)}, u32[]{:S(2)}) collective-permute-start(bf16[4,32,768]{2,1,0:T(8,128)(2,1)S(1)} %get-tuple-element.35), channel_id=1, source_target_pairs={{0,3},{1,0},{2,1},{3,2},{4,7},{5,4},{6,5},{7,6},{8,11},{9,8},{10,9... | collective-permute-start | bytes 589832 | tf_op jit(solution)/shard_map/ppermute | solution.py:343
  61.4 13.1 %collective-permute-start.20 = (bf16[4,32,768]{2,1,0:T(8,128)(2,1)S(1)}, bf16[4,32,768]{2,1,0:T(8,128)(2,1)S(1)}, u32[]{:S(2)}, u32[]{:S(2)}) collective-permute-start(bf16[4,32,768]{2,1,0:T(8,128)(2,1)S(1)} %get-tuple-element.29), channel_id=1, source_target_pairs={{0,8},{1,9},{2,10},{3,11},{4,12},{5,13},{6,14},{7,15},{8,0},{9,1},... | collective-permute-start | bytes 589832 | tf_op jit(solution)/shard_map/ppermute | solution.py:343
  63.4 12.2 %collective-permute-start.21 = (bf16[4,32,768]{2,1,0:T(8,128)(2,1)S(1)}, bf16[4,32,768]{2,1,0:T(8,128)(2,1)S(1)}, u32[]{:S(2)}, u32[]{:S(2)}) collective-permute-start(bf16[4,32,768]{2,1,0:T(8,128)(2,1)S(1)} %get-tuple-element.30), channel_id=1, source_target_pairs={{0,4},{1,5},{2,6},{3,7},{4,8},{5,9},{6,10},{7,11},{8,12},{9,13},{1... | collective-permute-start | bytes 589832 | tf_op jit(solution)/shard_map/ppermute | solution.py:343
  66.3 9.3 %collective-permute-start.22 = (bf16[4,32,768]{2,1,0:T(8,128)(2,1)S(1)}, bf16[4,32,768]{2,1,0:T(8,128)(2,1)S(1)}, u32[]{:S(2)}, u32[]{:S(2)}) collective-permute-start(bf16[4,32,768]{2,1,0:T(8,128)(2,1)S(1)} %get-tuple-element.31), channel_id=1, source_target_pairs={{0,12},{1,13},{2,14},{3,15},{4,0},{5,1},{6,2},{7,3},{8,4},{9,5},{1... | collective-permute-start | bytes 589832 | tf_op jit(solution)/shard_map/ppermute | solution.py:343
  70.9 6.1 %collective-permute-start.33 = (bf16[32,768]{1,0:T(8,128)(2,1)S(1)}, bf16[32,768]{1,0:T(8,128)(2,1)S(1)}, u32[]{:S(2)}, u32[]{:S(2)}) collective-permute-start(bf16[32,768]{1,0:T(8,128)(2,1)S(1)} %get-tuple-element.46), channel_id=1, source_target_pairs={{0,8},{1,9},{2,10},{3,11},{4,12},{5,13},{6,14},{7,15},{8,0},{9,1},... | collective-permute-start | bytes 147464 | tf_op jit(solution)/shard_map/ppermute | solution.py:343
  73.0 6.1 %collective-permute-start.34 = (bf16[32,768]{1,0:T(8,128)(2,1)S(1)}, bf16[32,768]{1,0:T(8,128)(2,1)S(1)}, u32[]{:S(2)}, u32[]{:S(2)}) collective-permute-start(bf16[32,768]{1,0:T(8,128)(2,1)S(1)} %get-tuple-element.48), channel_id=1, source_target_pairs={{0,4},{1,5},{2,6},{3,7},{4,8},{5,9},{6,10},{7,11},{8,12},{9,13},{1... | collective-permute-start | bytes 147464 | tf_op jit(solution)/shard_map/ppermute | solution.py:343
  86.2 5.6 %collective-permute-start.29 = (bf16[4,32,768]{2,1,0:T(8,128)(2,1)S(1)}, bf16[4,32,768]{2,1,0:T(8,128)(2,1)S(1)}, u32[]{:S(2)}, u32[]{:S(2)}) collective-permute-start(bf16[4,32,768]{2,1,0:T(8,128)(2,1)S(1)} %pad_maximum_fusion.2.near_ref), channel_id=1, source_target_pairs={{0,16},{16,0},{32,48},{48,32},{64,80},{80,64},{96,112},{112,96},{1... | collective-permute-start | bytes 589832 | tf_op jit(solution)/shard_map/ppermute | solution.py:339
  94.6 18.5 %all-to-all-start = ((bf16[16,32,768]{2,1,0:T(8,128)(2,1)}), bf16[16,32,768]{2,1,0:T(8,128)(2,1)S(1)}, u32[]{:S(2)}, u32[]{:S(2)}) async-start(bf16[16,32,768]{2,1,0:T(8,128)(2,1)} %graph_partial.5), calls=%async_computation | async-start | bytes 1572864 | tf_op jit(solution)/shard_map/all_to_all | solution.py:387
  118.4 5.0 %collective-permute-start.38 = (f32[104,128]{1,0:T(8,128)S(1)}, f32[104,128]{1,0:T(8,128)S(1)}, u32[]{:S(2)}, u32[]{:S(2)}) collective-permute-start(f32[104,128]{1,0:T(8,128)S(1)} %dynamic-slice_add_fusion), channel_id=1, source_target_pairs={{0,4},{1,5},{2,6},{3,7},{4,8},{5,9},{6,10},{7,11},{8,12},{9,13},{1... | collective-permute-start | bytes 159752 | tf_op jit(solution)/shard_map/ppermute | solution.py:365
  135.5 5.3 %collective-permute-start.46 = (f32[104,128]{1,0:T(8,128)S(1)}, f32[104,128]{1,0:T(8,128)S(1)}, u32[]{:S(2)}, u32[]{:S(2)}) collective-permute-start(f32[104,128]{1,0:T(8,128)S(1)} %add_add_fusion.4.mine_ref), channel_id=1, source_target_pairs={{0,16},{16,0},{32,48},{48,32},{64,80},{80,64},{96,112},{112,96},{1... | collective-permute-start | bytes 159752 | tf_op jit(solution)/shard_map/ppermute | solution.py:367
  (29 other events, 268.5 us)

commit v7 on v6

--- a/solution.py
+++ b/solution.py
@@ -352,7 +352,24 @@
     x, p = x.astype(BF), p.astype(BF)
     x = [x_own] + [x[k] for k in (1, 2, 3)]
     p = [p_own] + [p[k] for k in (1, 2, 3)]
-    return turned_sum([x, p], [y_turn, x_turn])
+    return turned_sum([x], [y_turn])[0], p
+
+
+def kept_kernel(v_ref, after_ref, out_ref):
+    out_ref[...] = v_ref[...]
+
+
+def late_phase(p, after):
+    sent = jnp.stack(p[1:])
+    sent = pl.pallas_call(
+        kept_kernel,
+        out_shape=jax.ShapeDtypeStruct(sent.shape, BF),
+        in_specs=[VMEM, pl.BlockSpec(memory_space=pl.ANY)],
+        out_specs=VMEM,
+        compiler_params=pltpu.CompilerParams(vmem_limit_bytes=8 * 2**20),
+        name="kept_pieces",
+    )(sent, after)
+    return turned_sum([[p[0], sent[0], sent[1], sent[2]]], [x_turn])[0]
 
 
 def sum_all(g):
@@ -381,22 +398,20 @@
     bcol = lax.axis_index("bcol")
     table = jnp.concatenate([rows, spots, jnp.stack([live, bcol // 4, bcol % 4])])
 
-    def apply_graph(v, fetched=False):
-        near, far = gather_brow((degree_scale * v).astype(BF))
-        part = graph_partial(table, near, far, block_set, owners, fetched)
-        got = lax.all_to_all(part, "bcol", 0, 0)
-        return degree_scale * jnp.sum(got.astype(F32), axis=0)
-
     def apply_both(v, fetched=False):
         near, far = gather_brow((degree_scale * v).astype(BF))
         parts = graph_partial(table, near, far, block_set, owners, fetched, True)
-        found = two_phases(parts[:4], parts[4:])
-        return [degree_scale * f for f in found]
+        found, p = two_phases(parts[:4], parts[4:])
+        return degree_scale * found, p
 
     x0, p0 = eigen_block, direction
     x1, p1 = apply_both(jnp.concatenate([x0, p0], 0), True)
+    p1 = degree_scale * turned_sum([p1], [x_turn])[0]
     x2, p2 = apply_both(jnp.concatenate([x1, p1], 0))
-    x3 = apply_graph(x2)
+    near, far = gather_brow((degree_scale * x2).astype(BF))
+    part = graph_partial(table, near, far, block_set, owners, False)
+    p2 = degree_scale * late_phase(p2, part)
+    x3 = degree_scale * jnp.sum(lax.all_to_all(part, "bcol", 0, 0).astype(F32), axis=0)
     parts = [x0, p0, x1, p1, x2, p2, x3]
     mine, other = sum_all(packed_gram(parts))
     return tuple(small(cutoff, (brow % 2).reshape(1), mine, other, parts))

time: 159 us -> 170 us (1.069)
  waiting for transfers between devices: 35.6 us -> 45.9 us
  starting transfers between devices: 89 us -> 91.4 us
    ppermute x24, waiting for transfers between devices: 6.92 us -> 29.7 us  [turned_sum(): lax.ppermute(p[k], 'bcol', turn(k))]
    all_to_all x1, waiting for transfers between devices: 11.8 us -> 0.01 us  [local(): lax.all_to_all(part, 'bcol', 0, 0).astype(F32)]
  transfers between devices with their start and end apart: 48 -> 48, of which waited for: 28 -> 30; matrix products, arithmetic and copies ran while one was open for 1% -> 1% of each run, Pallas kernels for 1% -> 0%
where the time goes in v7:
time: 170 us
  starting transfers between devices  91.4 us (54%)
  waiting for transfers between devices  45.9 us (27%)
  Pallas kernels  27.2 us (16%)
  other arithmetic  3.49 us (2%)
  between operations  2.19 us (1%)
    ppermute x24, starting transfers between devices, turned_sum(): lax.ppermute(p[k], 'bcol', turn(k))  40.8 us
    ppermute x24, waiting for transfers between devices, turned_sum(): lax.ppermute(p[k], 'bcol', turn(k))  29.7 us
    pallas_call x1, Pallas kernels, small(): pl.pallas_call(functools.partial(small_kernel, w), out_shape=[jax.ShapeDt...  18.2 us
    ppermute x9, starting transfers between devices, gather_brow(): got = {k: lax.ppermute(v, 'brow', z_turn(k)) for k in (3, 2, 1)}  15.4 us
    ppermute x9, starting transfers between devices, sum_all(): a, b, c = [lax.ppermute(v, axis, turn(k)) for k in (2, 1, 3)]  12 us
    ppermute x3, starting transfers between devices, gather_brow(): return (near, lax.ppermute(near, 'brow', CORE))  11.2 us
    pallas_call x3, Pallas kernels, graph_partial(): pl.pallas_call(functools.partial(graph_kernel, 8 if split else 1), out_sh...  7.48 us
    ppermute x9, waiting for transfers between devices, sum_all(): a, b, c = [lax.ppermute(v, axis, turn(k)) for k in (2, 1, 3)]  7.35 us
  transfers between devices with their start and end apart: 48, of which 30 were waited for; matrix products, arithmetic and copies ran while one was open for 1% of the time, Pallas kernels for 0%

profile of v7, /device:TPU:1, one launch (start us, length us, event | category | flops | bytes accessed | tf_op | source)
XLA Modules:
  0.0 170.4 jit_solution(6713528163293867950)
XLA Ops:
  1.6 4.5 %collective-permute-start = (bf16[64,768]{1,0:T(8,128)(2,1)S(1)}, bf16[64,768]{1,0:T(8,128)(2,1)S(1)}, u32[]{:S(2)}, u32[]{:S(2)}) collective-permute-start(bf16[64,768]{1,0:T(8,128)(2,1)S(1)} %fusion.1), channel_id=1, source_target_pairs={{0,64},{16,80},{32,96},{48,112},{64,0},{80,16},{96,32},{112,48},{1... | collective-permute-start | bytes 294920 | tf_op jit(solution)/shard_map/ppermute | solution.py:337
  14.5 3.1 %graph_partial.3 = (bf16[4,32,768]{2,1,0:T(8,128)(2,1)S(1)}, bf16[4,32,768]{2,1,0:T(8,128)(2,1)S(1)}, bf16[4,32,768]{2,1,0:T(8,128)(2,1)S(1)}, bf16[4,32,768]{2,...) custom-call(s32[83]{0:T(128)S(1)} %concatenate.35.table_ref, ...), custom_call_target="tpu_custom_call" | custom-call | tf_op jit(solution)/shard_map/graph_partial/pallas_call | solution.py:85
  17.6 2.8 %collective-permute-start.4 = (bf16[4,32,768]{2,1,0:T(8,128)(2,1)S(1)}, bf16[4,32,768]{2,1,0:T(8,128)(2,1)S(1)}, u32[]{:S(2)}, u32[]{:S(2)}) collective-permute-start(bf16[4,32,768]{2,1,0:T(8,128)(2,1)S(1)} %get-tuple-element.21), channel_id=1, source_target_pairs={{0,8},{1,9},{2,10},{3,11},{4,12},{5,13},{6,14},{7,15},{8,0},{9,1},... | collective-permute-start | bytes 589832 | tf_op jit(solution)/shard_map/ppermute | solution.py:343
  20.8 2.4 %collective-permute-start.6 = (bf16[4,32,768]{2,1,0:T(8,128)(2,1)S(1)}, bf16[4,32,768]{2,1,0:T(8,128)(2,1)S(1)}, u32[]{:S(2)}, u32[]{:S(2)}) collective-permute-start(bf16[4,32,768]{2,1,0:T(8,128)(2,1)S(1)} %get-tuple-element.23), channel_id=1, source_target_pairs={{0,12},{1,13},{2,14},{3,15},{4,0},{5,1},{6,2},{7,3},{8,4},{9,5},{1... | collective-permute-start | bytes 589832 | tf_op jit(solution)/shard_map/ppermute | solution.py:343
  23.1 2.9 %collective-permute-start.10 = (bf16[4,32,768]{2,1,0:T(8,128)(2,1)S(1)}, bf16[4,32,768]{2,1,0:T(8,128)(2,1)S(1)}, u32[]{:S(2)}, u32[]{:S(2)}) collective-permute-start(bf16[4,32,768]{2,1,0:T(8,128)(2,1)S(1)} %get-tuple-element.25), channel_id=1, source_target_pairs={{0,2},{1,3},{2,0},{3,1},{4,6},{5,7},{6,4},{7,5},{8,10},{9,11},{10,... | collective-permute-start | bytes 589832 | tf_op jit(solution)/shard_map/ppermute | solution.py:343
  26.5 2.3 %collective-permute-start.12 = (bf16[4,32,768]{2,1,0:T(8,128)(2,1)S(1)}, bf16[4,32,768]{2,1,0:T(8,128)(2,1)S(1)}, u32[]{:S(2)}, u32[]{:S(2)}) collective-permute-start(bf16[4,32,768]{2,1,0:T(8,128)(2,1)S(1)} %get-tuple-element.27), channel_id=1, source_target_pairs={{0,3},{1,0},{2,1},{3,2},{4,7},{5,4},{6,5},{7,6},{8,11},{9,8},{10,9... | collective-permute-start | bytes 589832 | tf_op jit(solution)/shard_map/ppermute | solution.py:343
  30.4 3.7 %collective-permute-start.7 = (bf16[32,768]{1,0:T(8,128)(2,1)S(1)}, bf16[32,768]{1,0:T(8,128)(2,1)S(1)}, u32[]{:S(2)}, u32[]{:S(2)}) collective-permute-start(bf16[32,768]{1,0:T(8,128)(2,1)S(1)} %get-tuple-element.50), channel_id=1, source_target_pairs={{0,2},{1,3},{2,0},{3,1},{4,6},{5,7},{6,4},{7,5},{8,10},{9,11},{10,... | collective-permute-start | bytes 147464 | tf_op jit(solution)/shard_map/ppermute | solution.py:343
  34.2 2.5 %collective-permute-start.9 = (bf16[32,768]{1,0:T(8,128)(2,1)S(1)}, bf16[32,768]{1,0:T(8,128)(2,1)S(1)}, u32[]{:S(2)}, u32[]{:S(2)}) collective-permute-start(bf16[32,768]{1,0:T(8,128)(2,1)S(1)} %get-tuple-element.51), channel_id=1, source_target_pairs={{0,3},{1,0},{2,1},{3,2},{4,7},{5,4},{6,5},{7,6},{8,11},{9,8},{10,9... | collective-permute-start | bytes 147464 | tf_op jit(solution)/shard_map/ppermute | solution.py:343
  49.6 4.9 %collective-permute-start.19 = (bf16[4,64,768]{2,1,0:T(8,128)(2,1)S(1)}, bf16[4,64,768]{2,1,0:T(8,128)(2,1)S(1)}, u32[]{:S(2)}, u32[]{:S(2)}) collective-permute-start(bf16[4,64,768]{2,1,0:T(8,128)(2,1)S(1)} %pad_maximum_fusion.1.near_ref), channel_id=1, source_target_pairs={{0,16},{16,0},{32,48},{48,32},{64,80},{80,64},{96,112},{112,96},{1... | collective-permute-start | bytes 1179656 | tf_op jit(solution)/shard_map/ppermute | solution.py:339
  62.1 3.4 %collective-permute-done.20 = bf16[4,32,768]{2,1,0:T(8,128)(2,1)S(1)} collective-permute-done((bf16[4,32,768]{2,1,0:T(8,128)(2,1)S(1)}, bf16[4,32,768]{2,1,0:T(8,128)(2,1)S(1)}, u32[]{:S(2)}, u32[]{:S(2)}) %collective-permute-start.20) | collective-permute-done | bytes 196640 | tf_op jit(solution)/shard_map/ppermute | solution.py:343
  65.5 4.9 %collective-permute-done.21 = bf16[4,32,768]{2,1,0:T(8,128)(2,1)S(1)} collective-permute-done((bf16[4,32,768]{2,1,0:T(8,128)(2,1)S(1)}, bf16[4,32,768]{2,1,0:T(8,128)(2,1)S(1)}, u32[]{:S(2)}, u32[]{:S(2)}) %collective-permute-start.21) | collective-permute-done | bytes 196640 | tf_op jit(solution)/shard_map/ppermute | solution.py:343
  81.6 4.6 %collective-permute-start.29 = (bf16[4,32,768]{2,1,0:T(8,128)(2,1)S(1)}, bf16[4,32,768]{2,1,0:T(8,128)(2,1)S(1)}, u32[]{:S(2)}, u32[]{:S(2)}) collective-permute-start(bf16[4,32,768]{2,1,0:T(8,128)(2,1)S(1)} %pad_maximum_fusion.2.near_ref), channel_id=1, source_target_pairs={{0,16},{16,0},{32,48},{48,32},{64,80},{80,64},{96,112},{112,96},{1... | collective-permute-start | bytes 589832 | tf_op jit(solution)/shard_map/ppermute | solution.py:339
  87.3 2.5 %graph_partial.5.after_ref = bf16[16,32,768]{2,1,0:T(8,128)(2,1)} custom-call(s32[83]{0:T(128)S(1)} %concatenate.35.table_ref, bf16[4,32,768]{2,1,0:T(8,128)(2,1)S(1)} %pad_maximum_fusion.2.near_ref, bf16[4,32,768]{2,1,0:T(8,128)(2,1)S(1)} %collective-permute-done.29.far_ref, bf16[40,256,256]{2,1,0:T(8,128)(2,1)S(1)} %bitcast.92), custom_call_target="tpu_custom_call" | custom-call | tf_op jit(solution)/shard_map/graph_partial/pallas_call | solution.py:85
  89.8 4.8 %all-to-all-start = ((bf16[16,32,768]{2,1,0:T(8,128)(2,1)}), bf16[16,32,768]{2,1,0:T(8,128)(2,1)S(1)}, u32[]{:S(2)}, u32[]{:S(2)}) async-start(bf16[16,32,768]{2,1,0:T(8,128)(2,1)} %graph_partial.5.after_ref), calls=%async_computation | async-start | bytes 1572864 | tf_op jit(solution)/shard_map/all_to_all | solution.py:414
  94.6 2.9 %collective-permute-start.30 = (bf16[4,32,768]{2,1,0:T(8,128)(2,1)S(1)}, bf16[4,32,768]{2,1,0:T(8,128)(2,1)S(1)}, u32[]{:S(2)}, u32[]{:S(2)}) collective-permute-start(bf16[4,32,768]{2,1,0:T(8,128)(2,1)S(1)} %get-tuple-element.33), channel_id=1, source_target_pairs={{0,2},{1,3},{2,0},{3,1},{4,6},{5,7},{6,4},{7,5},{8,10},{9,11},{10,... | collective-permute-start | bytes 589832 | tf_op jit(solution)/shard_map/ppermute | solution.py:343
  97.8 2.4 %collective-permute-start.32 = (bf16[4,32,768]{2,1,0:T(8,128)(2,1)S(1)}, bf16[4,32,768]{2,1,0:T(8,128)(2,1)S(1)}, u32[]{:S(2)}, u32[]{:S(2)}) collective-permute-start(bf16[4,32,768]{2,1,0:T(8,128)(2,1)S(1)} %get-tuple-element.35), channel_id=1, source_target_pairs={{0,3},{1,0},{2,1},{3,2},{4,7},{5,4},{6,5},{7,6},{8,11},{9,8},{10,9... | collective-permute-start | bytes 589832 | tf_op jit(solution)/shard_map/ppermute | solution.py:343
  100.2 10.3 %collective-permute-done.30 = bf16[4,32,768]{2,1,0:T(8,128)(2,1)S(1)} collective-permute-done((bf16[4,32,768]{2,1,0:T(8,128)(2,1)S(1)}, bf16[4,32,768]{2,1,0:T(8,128)(2,1)S(1)}, u32[]{:S(2)}, u32[]{:S(2)}) %collective-permute-start.30) | collective-permute-done | bytes 196640 | tf_op jit(solution)/shard_map/ppermute | solution.py:343
  110.4 4.9 %collective-permute-done.31 = bf16[4,32,768]{2,1,0:T(8,128)(2,1)S(1)} collective-permute-done((bf16[4,32,768]{2,1,0:T(8,128)(2,1)S(1)}, bf16[4,32,768]{2,1,0:T(8,128)(2,1)S(1)}, u32[]{:S(2)}, u32[]{:S(2)}) %collective-permute-start.31) | collective-permute-done | bytes 196640 | tf_op jit(solution)/shard_map/ppermute | solution.py:343
  115.5 2.5 %collective-permute-start.33 = (bf16[32,768]{1,0:T(8,128)(2,1)S(1)}, bf16[32,768]{1,0:T(8,128)(2,1)S(1)}, u32[]{:S(2)}, u32[]{:S(2)}) collective-permute-start(bf16[32,768]{1,0:T(8,128)(2,1)S(1)} %get-tuple-element.53), channel_id=1, source_target_pairs={{0,8},{1,9},{2,10},{3,11},{4,12},{5,13},{6,14},{7,15},{8,0},{9,1},... | collective-permute-start | bytes 147464 | tf_op jit(solution)/shard_map/ppermute | solution.py:343
  118.3 2.4 %collective-permute-start.35 = (bf16[32,768]{1,0:T(8,128)(2,1)S(1)}, bf16[32,768]{1,0:T(8,128)(2,1)S(1)}, u32[]{:S(2)}, u32[]{:S(2)}) collective-permute-start(bf16[32,768]{1,0:T(8,128)(2,1)S(1)} %get-tuple-element.54), channel_id=1, source_target_pairs={{0,12},{1,13},{2,14},{3,15},{4,0},{5,1},{6,2},{7,3},{8,4},{9,5},{1... | collective-permute-start | bytes 147464 | tf_op jit(solution)/shard_map/ppermute | solution.py:343
  123.8 2.3 %collective-permute-start.36 = (f32[104,128]{1,0:T(8,128)S(1)}, f32[104,128]{1,0:T(8,128)S(1)}, u32[]{:S(2)}, u32[]{:S(2)}) collective-permute-start(f32[104,128]{1,0:T(8,128)S(1)} %constant_dynamic-slice_fusion), channel_id=1, source_target_pairs={{0,16},{16,0},{32,48},{48,32},{64,80},{80,64},{96,112},{112,96},{1... | collective-permute-start | bytes 159752 | tf_op jit(solution)/shard_map/ppermute | solution.py:380
  135.2 2.4 %collective-permute-start.41 = (f32[104,128]{1,0:T(8,128)S(1)}, f32[104,128]{1,0:T(8,128)S(1)}, u32[]{:S(2)}, u32[]{:S(2)}) collective-permute-start(f32[104,128]{1,0:T(8,128)S(1)} %add_add_fusion.6), channel_id=1, source_target_pairs={{0,32},{16,48},{32,64},{48,80},{64,96},{80,112},{96,0},{112,16},{1... | collective-permute-start | bytes 159752 | tf_op jit(solution)/shard_map/ppermute | solution.py:382
  146.4 4.9 %collective-permute-start.46 = (f32[104,128]{1,0:T(8,128)S(1)}, f32[104,128]{1,0:T(8,128)S(1)}, u32[]{:S(2)}, u32[]{:S(2)}) collective-permute-start(f32[104,128]{1,0:T(8,128)S(1)} %add_add_fusion.4.mine_ref), channel_id=1, source_target_pairs={{0,16},{16,0},{32,48},{48,32},{64,80},{80,64},{96,112},{112,96},{1... | collective-permute-start | bytes 159752 | tf_op jit(solution)/shard_map/ppermute | solution.py:384
  152.2 18.2 %small_matrices.1 = (f32[32,768]{1,0:T(8,128)}, f32[32,768]{1,0:T(8,128)}, f32[32,768]{1,0:T(8,128)}, f32[32,768]{1,0:T(8,128)}) custom-call(f32[1]{0:T(128)S(6)} %copy.13.cut_ref, s32[1]{0:T(128)} %bitcast.core_ref, f32[104,128]{1,0:T(8,128)S(1)} %add_add_fusion.4.mine_ref, f32[104,128]{1,0:T(8,128)S(1)} %collective-permute-done.46.other_ref, ...), custom_call_target="tpu_custom_call" | custom-call | tf_op jit(solution)/shard_map/small_matrices/pallas_call | solution.py:268
  (117 shorter events, 65.6 us)
Async XLA Ops:
  1.6 8.2 %collective-permute-start = (bf16[64,768]{1,0:T(8,128)(2,1)S(1)}, bf16[64,768]{1,0:T(8,128)(2,1)S(1)}, u32[]{:S(2)}, u32[]{:S(2)}) collective-permute-start(bf16[64,768]{1,0:T(8,128)(2,1)S(1)} %fusion.1), channel_id=1, source_target_pairs={{0,64},{16,80},{32,96},{48,112},{64,0},{80,16},{96,32},{112,48},{1... | collective-permute-start | bytes 294920 | tf_op jit(solution)/shard_map/ppermute | solution.py:337
  6.1 4.7 %collective-permute-start.1 = (bf16[64,768]{1,0:T(8,128)(2,1)S(1)}, bf16[64,768]{1,0:T(8,128)(2,1)S(1)}, u32[]{:S(2)}, u32[]{:S(2)}) collective-permute-start(bf16[64,768]{1,0:T(8,128)(2,1)S(1)} %fusion.1), channel_id=1, source_target_pairs={{0,32},{16,48},{32,64},{48,80},{64,96},{80,112},{96,0},{112,16},{1... | collective-permute-start | bytes 294920 | tf_op jit(solution)/shard_map/ppermute | solution.py:337
  17.6 8.8 %collective-permute-start.4 = (bf16[4,32,768]{2,1,0:T(8,128)(2,1)S(1)}, bf16[4,32,768]{2,1,0:T(8,128)(2,1)S(1)}, u32[]{:S(2)}, u32[]{:S(2)}) collective-permute-start(bf16[4,32,768]{2,1,0:T(8,128)(2,1)S(1)} %get-tuple-element.21), channel_id=1, source_target_pairs={{0,8},{1,9},{2,10},{3,11},{4,12},{5,13},{6,14},{7,15},{8,0},{9,1},... | collective-permute-start | bytes 589832 | tf_op jit(solution)/shard_map/ppermute | solution.py:343
  20.5 9.8 %collective-permute-start.5 = (bf16[4,32,768]{2,1,0:T(8,128)(2,1)S(1)}, bf16[4,32,768]{2,1,0:T(8,128)(2,1)S(1)}, u32[]{:S(2)}, u32[]{:S(2)}) collective-permute-start(bf16[4,32,768]{2,1,0:T(8,128)(2,1)S(1)} %get-tuple-element.22), channel_id=1, source_target_pairs={{0,4},{1,5},{2,6},{3,7},{4,8},{5,9},{6,10},{7,11},{8,12},{9,13},{1... | collective-permute-start | bytes 589832 | tf_op jit(solution)/shard_map/ppermute | solution.py:343
  20.8 9.5 %collective-permute-start.6 = (bf16[4,32,768]{2,1,0:T(8,128)(2,1)S(1)}, bf16[4,32,768]{2,1,0:T(8,128)(2,1)S(1)}, u32[]{:S(2)}, u32[]{:S(2)}) collective-permute-start(bf16[4,32,768]{2,1,0:T(8,128)(2,1)S(1)} %get-tuple-element.23), channel_id=1, source_target_pairs={{0,12},{1,13},{2,14},{3,15},{4,0},{5,1},{6,2},{7,3},{8,4},{9,5},{1... | collective-permute-start | bytes 589832 | tf_op jit(solution)/shard_map/ppermute | solution.py:343
  23.1 11.1 %collective-permute-start.10 = (bf16[4,32,768]{2,1,0:T(8,128)(2,1)S(1)}, bf16[4,32,768]{2,1,0:T(8,128)(2,1)S(1)}, u32[]{:S(2)}, u32[]{:S(2)}) collective-permute-start(bf16[4,32,768]{2,1,0:T(8,128)(2,1)S(1)} %get-tuple-element.25), channel_id=1, source_target_pairs={{0,2},{1,3},{2,0},{3,1},{4,6},{5,7},{6,4},{7,5},{8,10},{9,11},{10,... | collective-permute-start | bytes 589832 | tf_op jit(solution)/shard_map/ppermute | solution.py:343
  26.1 10.7 %collective-permute-start.11 = (bf16[4,32,768]{2,1,0:T(8,128)(2,1)S(1)}, bf16[4,32,768]{2,1,0:T(8,128)(2,1)S(1)}, u32[]{:S(2)}, u32[]{:S(2)}) collective-permute-start(bf16[4,32,768]{2,1,0:T(8,128)(2,1)S(1)} %get-tuple-element.26), channel_id=1, source_target_pairs={{0,1},{1,2},{2,3},{3,0},{4,5},{5,6},{6,7},{7,4},{8,9},{9,10},{10,1... | collective-permute-start | bytes 589832 | tf_op jit(solution)/shard_map/ppermute | solution.py:343
  26.5 10.3 %collective-permute-start.12 = (bf16[4,32,768]{2,1,0:T(8,128)(2,1)S(1)}, bf16[4,32,768]{2,1,0:T(8,128)(2,1)S(1)}, u32[]{:S(2)}, u32[]{:S(2)}) collective-permute-start(bf16[4,32,768]{2,1,0:T(8,128)(2,1)S(1)} %get-tuple-element.27), channel_id=1, source_target_pairs={{0,3},{1,0},{2,1},{3,2},{4,7},{5,4},{6,5},{7,6},{8,11},{9,8},{10,9... | collective-permute-start | bytes 589832 | tf_op jit(solution)/shard_map/ppermute | solution.py:343
  30.4 8.6 %collective-permute-start.7 = (bf16[32,768]{1,0:T(8,128)(2,1)S(1)}, bf16[32,768]{1,0:T(8,128)(2,1)S(1)}, u32[]{:S(2)}, u32[]{:S(2)}) collective-permute-start(bf16[32,768]{1,0:T(8,128)(2,1)S(1)} %get-tuple-element.50), channel_id=1, source_target_pairs={{0,2},{1,3},{2,0},{3,1},{4,6},{5,7},{6,4},{7,5},{8,10},{9,11},{10,... | collective-permute-start | bytes 147464 | tf_op jit(solution)/shard_map/ppermute | solution.py:343
  34.1 7.1 %collective-permute-start.8 = (bf16[32,768]{1,0:T(8,128)(2,1)S(1)}, bf16[32,768]{1,0:T(8,128)(2,1)S(1)}, u32[]{:S(2)}, u32[]{:S(2)}) collective-permute-start(bf16[32,768]{1,0:T(8,128)(2,1)S(1)} %get-tuple-element.52), channel_id=1, source_target_pairs={{0,1},{1,2},{2,3},{3,0},{4,5},{5,6},{6,7},{7,4},{8,9},{9,10},{10,1... | collective-permute-start | bytes 147464 | tf_op jit(solution)/shard_map/ppermute | solution.py:343
  34.2 7.0 %collective-permute-start.9 = (bf16[32,768]{1,0:T(8,128)(2,1)S(1)}, bf16[32,768]{1,0:T(8,128)(2,1)S(1)}, u32[]{:S(2)}, u32[]{:S(2)}) collective-permute-start(bf16[32,768]{1,0:T(8,128)(2,1)S(1)} %get-tuple-element.51), channel_id=1, source_target_pairs={{0,3},{1,0},{2,1},{3,2},{4,7},{5,4},{6,5},{7,6},{8,11},{9,8},{10,9... | collective-permute-start | bytes 147464 | tf_op jit(solution)/shard_map/ppermute | solution.py:343
  42.8 5.1 %collective-permute-start.16 = (bf16[64,768]{1,0:T(8,128)(2,1)S(1)}, bf16[64,768]{1,0:T(8,128)(2,1)S(1)}, u32[]{:S(2)}, u32[]{:S(2)}) collective-permute-start(bf16[64,768]{1,0:T(8,128)(2,1)S(1)} %fusion.3), channel_id=1, source_target_pairs={{0,64},{16,80},{32,96},{48,112},{64,0},{80,16},{96,32},{112,48},{1... | collective-permute-start | bytes 294920 | tf_op jit(solution)/shard_map/ppermute | solution.py:337
  49.6 6.3 %collective-permute-start.19 = (bf16[4,64,768]{2,1,0:T(8,128)(2,1)S(1)}, bf16[4,64,768]{2,1,0:T(8,128)(2,1)S(1)}, u32[]{:S(2)}, u32[]{:S(2)}) collective-permute-start(bf16[4,64,768]{2,1,0:T(8,128)(2,1)S(1)} %pad_maximum_fusion.1.near_ref), channel_id=1, source_target_pairs={{0,16},{16,0},{32,48},{48,32},{64,80},{80,64},{96,112},{112,96},{1... | collective-permute-start | bytes 1179656 | tf_op jit(solution)/shard_map/ppermute | solution.py:339
  57.8 7.7 %collective-permute-start.20 = (bf16[4,32,768]{2,1,0:T(8,128)(2,1)S(1)}, bf16[4,32,768]{2,1,0:T(8,128)(2,1)S(1)}, u32[]{:S(2)}, u32[]{:S(2)}) collective-permute-start(bf16[4,32,768]{2,1,0:T(8,128)(2,1)S(1)} %get-tuple-element.29), channel_id=1, source_target_pairs={{0,8},{1,9},{2,10},{3,11},{4,12},{5,13},{6,14},{7,15},{8,0},{9,1},... | collective-permute-start | bytes 589832 | tf_op jit(solution)/shard_map/ppermute | solution.py:343
  59.4 11.0 %collective-permute-start.21 = (bf16[4,32,768]{2,1,0:T(8,128)(2,1)S(1)}, bf16[4,32,768]{2,1,0:T(8,128)(2,1)S(1)}, u32[]{:S(2)}, u32[]{:S(2)}) collective-permute-start(bf16[4,32,768]{2,1,0:T(8,128)(2,1)S(1)} %get-tuple-element.30), channel_id=1, source_target_pairs={{0,4},{1,5},{2,6},{3,7},{4,8},{5,9},{6,10},{7,11},{8,12},{9,13},{1... | collective-permute-start | bytes 589832 | tf_op jit(solution)/shard_map/ppermute | solution.py:343
  61.4 9.0 %collective-permute-start.22 = (bf16[4,32,768]{2,1,0:T(8,128)(2,1)S(1)}, bf16[4,32,768]{2,1,0:T(8,128)(2,1)S(1)}, u32[]{:S(2)}, u32[]{:S(2)}) collective-permute-start(bf16[4,32,768]{2,1,0:T(8,128)(2,1)S(1)} %get-tuple-element.31), channel_id=1, source_target_pairs={{0,12},{1,13},{2,14},{3,15},{4,0},{5,1},{6,2},{7,3},{8,4},{9,5},{1... | collective-permute-start | bytes 589832 | tf_op jit(solution)/shard_map/ppermute | solution.py:343
  70.5 4.7 %collective-permute-start.23 = (bf16[32,768]{1,0:T(8,128)(2,1)S(1)}, bf16[32,768]{1,0:T(8,128)(2,1)S(1)}, u32[]{:S(2)}, u32[]{:S(2)}) collective-permute-start(bf16[32,768]{1,0:T(8,128)(2,1)S(1)} %get-tuple-element.44), channel_id=1, source_target_pairs={{0,2},{1,3},{2,0},{3,1},{4,6},{5,7},{6,4},{7,5},{8,10},{9,11},{10,... | collective-permute-start | bytes 147464 | tf_op jit(solution)/shard_map/ppermute | solution.py:343
  81.6 5.7 %collective-permute-start.29 = (bf16[4,32,768]{2,1,0:T(8,128)(2,1)S(1)}, bf16[4,32,768]{2,1,0:T(8,128)(2,1)S(1)}, u32[]{:S(2)}, u32[]{:S(2)}) collective-permute-start(bf16[4,32,768]{2,1,0:T(8,128)(2,1)S(1)} %pad_maximum_fusion.2.near_ref), channel_id=1, source_target_pairs={{0,16},{16,0},{32,48},{48,32},{64,80},{80,64},{96,112},{112,96},{1... | collective-permute-start | bytes 589832 | tf_op jit(solution)/shard_map/ppermute | solution.py:339
  89.8 30.9 %all-to-all-start = ((bf16[16,32,768]{2,1,0:T(8,128)(2,1)}), bf16[16,32,768]{2,1,0:T(8,128)(2,1)S(1)}, u32[]{:S(2)}, u32[]{:S(2)}) async-start(bf16[16,32,768]{2,1,0:T(8,128)(2,1)} %graph_partial.5.after_ref), calls=%async_computation | async-start | bytes 1572864 | tf_op jit(solution)/shard_map/all_to_all | solution.py:414
  94.6 15.8 %collective-permute-start.30 = (bf16[4,32,768]{2,1,0:T(8,128)(2,1)S(1)}, bf16[4,32,768]{2,1,0:T(8,128)(2,1)S(1)}, u32[]{:S(2)}, u32[]{:S(2)}) collective-permute-start(bf16[4,32,768]{2,1,0:T(8,128)(2,1)S(1)} %get-tuple-element.33), channel_id=1, source_target_pairs={{0,2},{1,3},{2,0},{3,1},{4,6},{5,7},{6,4},{7,5},{8,10},{9,11},{10,... | collective-permute-start | bytes 589832 | tf_op jit(solution)/shard_map/ppermute | solution.py:343
  97.5 17.8 %collective-permute-start.31 = (bf16[4,32,768]{2,1,0:T(8,128)(2,1)S(1)}, bf16[4,32,768]{2,1,0:T(8,128)(2,1)S(1)}, u32[]{:S(2)}, u32[]{:S(2)}) collective-permute-start(bf16[4,32,768]{2,1,0:T(8,128)(2,1)S(1)} %get-tuple-element.34), channel_id=1, source_target_pairs={{0,1},{1,2},{2,3},{3,0},{4,5},{5,6},{6,7},{7,4},{8,9},{9,10},{10,1... | collective-permute-start | bytes 589832 | tf_op jit(solution)/shard_map/ppermute | solution.py:343
  97.8 17.5 %collective-permute-start.32 = (bf16[4,32,768]{2,1,0:T(8,128)(2,1)S(1)}, bf16[4,32,768]{2,1,0:T(8,128)(2,1)S(1)}, u32[]{:S(2)}, u32[]{:S(2)}) collective-permute-start(bf16[4,32,768]{2,1,0:T(8,128)(2,1)S(1)} %get-tuple-element.35), channel_id=1, source_target_pairs={{0,3},{1,0},{2,1},{3,2},{4,7},{5,4},{6,5},{7,6},{8,11},{9,8},{10,9... | collective-permute-start | bytes 589832 | tf_op jit(solution)/shard_map/ppermute | solution.py:343
  115.5 5.3 %collective-permute-start.33 = (bf16[32,768]{1,0:T(8,128)(2,1)S(1)}, bf16[32,768]{1,0:T(8,128)(2,1)S(1)}, u32[]{:S(2)}, u32[]{:S(2)}) collective-permute-start(bf16[32,768]{1,0:T(8,128)(2,1)S(1)} %get-tuple-element.53), channel_id=1, source_target_pairs={{0,8},{1,9},{2,10},{3,11},{4,12},{5,13},{6,14},{7,15},{8,0},{9,1},... | collective-permute-start | bytes 147464 | tf_op jit(solution)/shard_map/ppermute | solution.py:343
  146.4 5.8 %collective-permute-start.46 = (f32[104,128]{1,0:T(8,128)S(1)}, f32[104,128]{1,0:T(8,128)S(1)}, u32[]{:S(2)}, u32[]{:S(2)}) collective-permute-start(f32[104,128]{1,0:T(8,128)S(1)} %add_add_fusion.4.mine_ref), channel_id=1, source_target_pairs={{0,16},{16,0},{32,48},{48,32},{64,80},{80,64},{96,112},{112,96},{1... | collective-permute-start | bytes 159752 | tf_op jit(solution)/shard_map/ppermute | solution.py:384
  (29 other events, 293.8 us)
